TPU v7x, 32 devices: a whole 2x2x4 slice. The times are simulated.
32 devices in a mesh: grp: 4 (over y, core), row: 8 (over z, x).
Axes of the slice: x: 2, y: 2, z: 4, core: 2. Of those that a mesh axis runs over, the one named last changes fastest.
Arguments:
- stiffness: bfloat16 [7, 2, 192, 192], replicated, may hold values from -0.4375 to 0.4375
- lame: float32 [768, 7, 2], P(('grp', 'row')), may hold values from 0.3 to 3
- prolong: bfloat16 [768, 24, 192], P(('grp', 'row')), may hold values from -0.4375 to 0.4375
- columns: int32 [768, 7], P(('grp', 'row')), may hold values from -1 to 47, as said below
- ghost_count: int32 [32, 2], P(('grp', 'row')), may hold values from 1 to 12
- ghost_offset: int32 [32, 2], P(('grp', 'row')), may hold values from 0 to 23, as said below
- owner_map: int32 [768, 1], P(('grp', 'row')), may hold values from 0 to 3; in each aligned block of 24 rows (0 to 23, 24 to 47, ...) at most 12 rows name the same one
Outputs:
- coarse_rows: bfloat16 [1536, 24, 168], P(('grp', 'row'))
- coarse_ids: int32 [1536], P(('grp', 'row'))
Inputs may be any that keep to these rules, and one draw needn't show every extreme that they name: `columns`: slot 0 of every row names the row's own element; -1 marks an empty slot. ghost_offset + ghost_count <= 24 entry by entry. `owner_map`: at most 12 elements of one device name the same subgroup index.
All inputs are finite; a program needn't handle non-finite values.
Results may differ from a plain program's by a relative error of at most 0.001.
Values may be sent and summed in bfloat16 or wider, within the bound.
No kernel may reach another device: no remote copies, remote signals or barrier semaphores. Data moves between devices by JAX's collectives and lax.ppermute only.
A program may use at most 64 MiB of HBM per device.

v0:
```python
import jax
import jax.numpy as jnp
from jax import lax
from jax.sharding import PartitionSpec as P


def passed_along(value, axis, by):
    peers = lax.axis_size(axis)
    pairs = [(i, i + by) for i in range(peers) if 0 <= i + by < peers]
    return lax.ppermute(value, axis, pairs)


def slot_rank(target):
    matching = target[..., :, None] == target[..., None, :]
    places = jnp.arange(target.shape[-1])
    earlier = places[None, :] < places[:, None]
    return jnp.sum(jnp.logical_and(matching, earlier), axis=-1)


def pack_run(flattened, first_index, run_length, ghosts):
    slot_index = jnp.arange(ghosts)[:, None]
    element_index = jnp.arange(flattened.shape[0])[None, :]
    selector = ((element_index == first_index + slot_index) & (slot_index < run_length)).astype(
        jnp.bfloat16
    )
    return jnp.dot(selector, flattened, preferred_element_type=jnp.float32).astype(jnp.bfloat16)


def on_device(stiffness, lame, prolong, columns, ghost_count, ghost_offset, owner_map):
    element_count = prolong.shape[0]
    block_slots = stiffness.shape[0]
    fine_width = stiffness.shape[2]
    coarse = prolong.shape[1]
    ghosts = element_count // 2
    flattened = prolong.reshape(element_count, coarse * fine_width)
    to_below = pack_run(flattened, ghost_offset[0, 0], ghost_count[0, 0], ghosts)
    to_above = pack_run(flattened, ghost_offset[0, 1], ghost_count[0, 1], ghosts)
    from_below = passed_along(to_above, "row", 1)
    from_above = passed_along(to_below, "row", -1)
    empty_row = jnp.zeros((1, coarse * fine_width), jnp.bfloat16)
    prolong_table = jnp.concatenate([flattened, from_below, from_above, empty_row], axis=0)
    table_rows = prolong_table.shape[0]
    lookup = jnp.where(columns < 0, table_rows - 1, columns).reshape(-1)
    gathered = jnp.take(prolong_table, lookup, axis=0)
    gathered = gathered.reshape(element_count, block_slots, coarse, fine_width)
    part_first = jnp.einsum(
        "eskj,sij->eski", gathered, stiffness[:, 0], preferred_element_type=jnp.float32
    )
    part_second = jnp.einsum(
        "eskj,sij->eski", gathered, stiffness[:, 1], preferred_element_type=jnp.float32
    )
    applied = lame[:, :, 0, None, None] * part_first + lame[:, :, 1, None, None] * part_second
    coarse_block = jnp.einsum(
        "eai,eski->eask", prolong.astype(jnp.float32), applied, precision=lax.Precision.HIGHEST
    )
    row_width = coarse * block_slots * coarse
    coarse_flat = coarse_block.reshape(element_count, row_width).astype(jnp.bfloat16)
    group_count = lax.axis_size("grp")
    row_count = lax.axis_size("row")
    group_index = lax.axis_index("grp")
    row_index = lax.axis_index("row")
    capacity = 2 * ((element_count + group_count - 1) // group_count)
    target = owner_map[:, 0]
    capacity_index = jnp.arange(capacity)
    all_rows, all_targets = (
        lax.all_gather(coarse_flat, "grp", axis=0, tiled=True),
        lax.all_gather(target, "grp", axis=0, tiled=True),
    )
    all_rows = all_rows.reshape(group_count, element_count, row_width)
    all_targets = all_targets.reshape(group_count, element_count)
    position = slot_rank(all_targets)
    owned = all_targets == group_index
    selected = owned[:, None, :] & (position[:, None, :] == capacity_index[None, :, None])
    received = jnp.einsum(
        "sce,sex->scx", selected.astype(jnp.bfloat16), all_rows, preferred_element_type=jnp.float32
    ).astype(jnp.bfloat16)
    element_ids = (
        jnp.arange(group_count)[:, None] * row_count + row_index
    ) * element_count + jnp.arange(element_count)[None, :]
    id_sums = jnp.sum(jnp.where(selected, element_ids[:, None, :], 0), axis=-1)
    received_ids = jnp.where(jnp.any(selected, axis=-1), id_sums, -1)
    coarse_rows = received.reshape(group_count * capacity, coarse, block_slots * coarse)
    coarse_ids = received_ids.reshape(group_count * capacity)
    return (coarse_rows, coarse_ids)


def solution(mesh):
    in_specs = (
        P(),
        P(("grp", "row"), None, None),
        P(("grp", "row"), None, None),
        P(("grp", "row"), None),
        P(("grp", "row"), None),
        P(("grp", "row"), None),
        P(("grp", "row"), None),
    )
    out_specs = (P(("grp", "row"), None, None), P(("grp", "row")))
    return jax.shard_map(
        on_device, mesh=mesh, in_specs=in_specs, out_specs=out_specs, check_vma=False
    )
```

profile of v0, /device:TPU:9, one launch (start us, length us, event | category | flops | bytes accessed | tf_op | source)
XLA Modules:
  0.0 48.9 jit_solution(6919523257422462196)
XLA Ops:
  0.6 1.2 %reshape.135 = bf16[24,4608]{1,0:T(8,128)(2,1)S(1)} reshape(bf16[24,24,192]{2,1,0:T(8,128)(2,1)} %param.9) | data formatting | bytes 442368 | tf_op jit(solution)/shard_map/reshape | solution.py:35
  1.9 1.3 %fusion.37 = (s32[1,1]{1,0:T(1,128)}, s32[1,1]{1,0:T(1,128)}) fusion(s32[1,2]{1,0:T(1,128)} %param.12), kind=kLoop, calls=%fused_computation.57 | loop fusion | bytes 16 | tf_op jit(solution)/shard_map/slice | solution.py:37
  3.2 0.6 %iota_add_fusion.2 = s32[12]{0:T(128)S(1)} fusion(s32[]{:T(128)} %bitcast.3), kind=kLoop, calls=%fused_computation.52 | loop fusion | flops 12 | bytes 52 | tf_op jit(solution)/shard_map/add | solution.py:23
  3.8 1.3 %fusion.36 = (s32[1,1]{1,0:T(1,128)}, s32[1,1]{1,0:T(1,128)}) fusion(s32[1,2]{1,0:T(1,128)} %param.11), kind=kLoop, calls=%fused_computation.56 | loop fusion | bytes 16 | tf_op jit(solution)/shard_map/slice | solution.py:37
  5.2 0.6 %iota_compare_fusion.5 = pred[12]{0:T(512)(128)(4,1)S(1)} fusion(s32[]{:T(128)} %bitcast.4), kind=kLoop, calls=%fused_computation.51 | loop fusion | flops 12 | bytes 16 | tf_op jit(solution)/shard_map/lt | solution.py:23
  5.8 0.2 convolution_convert_fusion.1
  6.0 3.1 %collective-permute-start = (bf16[12,4608]{1,0:T(8,128)(2,1)S(1)}, bf16[12,4608]{1,0:T(8,128)(2,1)S(1)}, u32[]{:S(2)}, u32[]{:S(2)}) collective-permute-start(bf16[12,4608]{1,0:T(8,128)(2,1)S(1)} %convolution_convert_fusion.1), channel_id=1, source_target_pairs={{0,1},{1,2},{2,3},{3,4},{4,5},{5,6},{6,7},{8,9},{9,10},{10,11},{11... | collective-permute-start | bytes 331784 | tf_op jit(solution)/shard_map/ppermute | solution.py:10
  9.2 0.7 %iota_add_fusion.1 = s32[12]{0:T(128)S(1)} fusion(s32[]{:T(128)} %bitcast.5), kind=kLoop, calls=%fused_computation.50 | loop fusion | flops 12 | bytes 52 | tf_op jit(solution)/shard_map/add | solution.py:23
  9.8 0.7 %iota_compare_fusion.4 = pred[12]{0:T(512)(128)(4,1)S(1)} fusion(s32[]{:T(128)} %bitcast.6), kind=kLoop, calls=%fused_computation.49 | loop fusion | flops 12 | bytes 16 | tf_op jit(solution)/shard_map/lt | solution.py:23
  10.5 0.2 convolution_convert_fusion
  10.8 3.1 %collective-permute-start.1 = (bf16[12,4608]{1,0:T(8,128)(2,1)S(1)}, bf16[12,4608]{1,0:T(8,128)(2,1)S(1)}, u32[]{:S(2)}, u32[]{:S(2)}) collective-permute-start(bf16[12,4608]{1,0:T(8,128)(2,1)S(1)} %convolution_convert_fusion), channel_id=1, source_target_pairs={{1,0},{2,1},{3,2},{4,3},{5,4},{6,5},{7,6},{9,8},{10,9},{11,10},{12... | collective-permute-start | bytes 331784 | tf_op jit(solution)/shard_map/ppermute | solution.py:10
  13.8 0.7 %compare_select_fusion.1 = s32[24,7]{0,1:T(8,128)S(1)} fusion(s32[24,7]{0,1:T(8,128)} %param.10), kind=kLoop, calls=%fused_computation.32 | loop fusion | flops 336 | bytes 1344 | tf_op jit(solution)/shard_map/jit(_where)/select_n | solution.py:43
  14.5 0.7 %compare_and_fusion = pred[24,7]{0,1:T(8,128)(4,1)S(1)} fusion(s32[24,7]{0,1:T(8,128)} %param.10), kind=kLoop, calls=%fused_computation.43 | loop fusion | flops 1344 | bytes 840 | tf_op jit(solution)/shard_map/jit(_take)/and | solution.py:44
  15.2 0.1 copy.22
  15.3 0.1 reshape.136
  15.4 0.1 copy.21
  15.5 0.8 %fusion.35 = (f32[24,7,1]{0,2,1:T(1,128)S(1)}, f32[24,7,1]{0,2,1:T(1,128)S(1)}) fusion(f32[24,7,2]{0,2,1:T(2,128)} %param.8), kind=kLoop, calls=%fused_computation.55 | loop fusion | bytes 2688 | tf_op jit(solution)/shard_map/slice | solution.py:52
  16.3 0.1 copy.33
  16.4 0.1 copy.34
  16.5 1.2 %dynamic-slice = u32[1]{0:T(128)} dynamic-slice(u32[32]{0:T(128)} %constant.45, u32[]{:T(128)S(6)} %add.89), dynamic_slice_sizes={1} | dynamic-slice | bytes 12
  18.4 0.8 %bitcast_dynamic-update-slice_fusion = s32[96]{0:T(128)S(1)} fusion(s32[96]{0:T(128)S(1)} %broadcast.99, u32[]{:T(128)} %bitcast.1, s32[24,1]{0,1:T(1,128)} %param.13), kind=kLoop, calls=%fused_computation.47 | loop fusion | bytes 484
  19.1 4.8 %all-reduce = s32[96]{0:T(128)S(1)} all-reduce(s32[96]{0:T(128)S(1)} %bitcast_dynamic-update-slice_fusion), channel_id=2, replica_groups=mesh['grp'=4,'row'=8] {'grp'}, use_global_device_ids=true, to_apply=%add | all-reduce | flops 96 | bytes 768
  23.9 0.1 reshape.134
  24.0 0.2 convert_reduce_fusion
  24.3 0.1 iota_add_fusion
  24.3 0.1 fusion.21
  24.5 0.2 select_reduce_fusion
  24.7 0.6 %select_n.44 = s32[48]{0:T(128)} reshape(s32[4,12]{1,0:T(4,128)S(1)} %broadcast_select_fusion.3) | data formatting | bytes 384 | tf_op jit(solution)/shard_map/jit(_where)/select_n | solution.py:81
  25.3 0.1 pad.3.clone
  25.3 0.0 collective-permute-done
  25.3 0.0 collective-permute-done.1
  25.4 0.2 maximum_maximum_fusion
  25.5 2.6 %gather_fusion = bf16[168,4608]{1,0:T(8,128)(2,1)} fusion(bf16[49,4608]{1,0:T(8,128)(2,1)S(1)} %maximum_maximum_fusion, s32[1024]{0:T(1024)S(1)} %pad_clamp_fusion), kind=kCustom, calls=%fused_computation | custom fusion | bytes 3097248 | tf_op jit(solution)/shard_map/jit(_take)/gather | solution.py:44
  28.2 0.0 copy-start
  28.2 3.3 %gather.7 = bf16[24,7,24,192]{3,2,1,0:T(8,128)(2,1)S(1)} reshape(bf16[168,4608]{1,0:T(8,128)(2,1)} %gather_fusion) | data formatting | bytes 3096576 | tf_op jit(solution)/shard_map/jit(_take)/gather | solution.py:44
  31.5 0.0 copy-done
  31.5 0.8 %fusion.5 = f32[7,24,24,192]{3,2,0,1:T(8,128)S(1)} fusion(bf16[24,7,24,192]{3,2,1,0:T(8,128)(2,1)S(1)} %gather.7, pred[24,7]{1,0:T(8,128)(4,1)S(1)} %copy.21, bf16[7,2,192,192]{3,2,1,0:T(8,128)(2,1)S(1)} %copy-done), kind=kOutput, calls=%fused_computation.11 | convolution fusion | flops 298045440 | bytes 5852160 | tf_op jit(solution)/shard_map/eskj,sij->eski/dot_general | solution.py:49
  32.3 0.0 copy-start.1
  32.3 0.8 %fusion.6 = f32[7,24,24,192]{3,2,0,1:T(8,128)S(1)} fusion(bf16[24,7,24,192]{3,2,1,0:T(8,128)(2,1)S(1)} %gather.7, pred[24,7]{1,0:T(8,128)(4,1)S(1)} %copy.21, bf16[7,2,192,192]{3,2,1,0:T(8,128)(2,1)S(1)} %copy-done), kind=kOutput, calls=%fused_computation.12 | convolution fusion | flops 298045440 | bytes 5852160 | tf_op jit(solution)/shard_map/eskj,sij->eski/dot_general | solution.py:46
  33.0 0.2 copy-done.1
  33.2 2.5 %fusion.10 = bf16[24,24,7,24]{1,3,2,0:T(8,128)(2,1)S(1)} fusion(f32[7,24,24,192]{3,2,0,1:T(8,128)S(1)} %fusion.5, f32[7,24,24,192]{3,2,0,1:T(8,128)S(1)} %fusion.6, f32[24,7]{1,0:T(8,128)S(1)} %bitcast.56, f32[24,7]{1,0:T(8,128)S(1)} %bitcast.55, bf16[24,24,192]{2,1,0:T(8,128)(2,1)S(1)} %copy-done.1), kind=kOutput, calls=%fused_computation.14 | convolution fusion | flops 225372672 | bytes 6609216 | tf_op jit(solution)/shard_map/eai,eski->eask/dot_general | solution.py:53
  35.7 0.9 %copy.27 = bf16[24,24,7,24]{3,2,1,0:T(8,128)(2,1)S(1)} copy(bf16[24,24,7,24]{1,3,2,0:T(8,128)(2,1)S(1)} %fusion.10) | data formatting | bytes 387072 | tf_op jit(solution)/shard_map/convert_element_type | solution.py:57
  36.6 1.1 %convert_element_type.30 = bf16[24,4032]{1,0:T(8,128)(2,1)S(1)} reshape(bf16[24,24,7,24]{3,2,1,0:T(8,128)(2,1)S(1)} %copy.27) | data formatting | bytes 387072 | tf_op jit(solution)/shard_map/convert_element_type | solution.py:57
  37.7 9.2 %all_gather.7 = bf16[96,4032]{1,0:T(8,128)(2,1)S(1)} all-gather(bf16[24,4032]{1,0:T(8,128)(2,1)S(1)} %convert_element_type.30), channel_id=1, replica_groups=mesh['grp'=4,'row'=8] {'grp'}, dimensions={0}, use_global_device_ids=true | all-gather | bytes 967680 | tf_op jit(solution)/shard_map/all_gather | solution.py:66
  46.9 0.3 convolution_convert_fusion.2
  47.2 1.7 %reshape.138 = bf16[48,24,168]{2,1,0:T(8,128)(2,1)} reshape(bf16[4,12,4032]{2,1,0:T(8,128)(2,1)S(1)} %convolution_convert_fusion.2) | data formatting | bytes 774144 | tf_op jit(solution)/shard_map/reshape | solution.py:82
  (7 shorter events, 0.0 us)
Async XLA Ops:
  6.0 19.3 %collective-permute-start = (bf16[12,4608]{1,0:T(8,128)(2,1)S(1)}, bf16[12,4608]{1,0:T(8,128)(2,1)S(1)}, u32[]{:S(2)}, u32[]{:S(2)}) collective-permute-start(bf16[12,4608]{1,0:T(8,128)(2,1)S(1)} %convolution_convert_fusion.1), channel_id=1, source_target_pairs={{0,1},{1,2},{2,3},{3,4},{4,5},{5,6},{6,7},{8,9},{9,10},{10,11},{11... | collective-permute-start | bytes 331784 | tf_op jit(solution)/shard_map/ppermute | solution.py:10
  10.8 14.6 %collective-permute-start.1 = (bf16[12,4608]{1,0:T(8,128)(2,1)S(1)}, bf16[12,4608]{1,0:T(8,128)(2,1)S(1)}, u32[]{:S(2)}, u32[]{:S(2)}) collective-permute-start(bf16[12,4608]{1,0:T(8,128)(2,1)S(1)} %convolution_convert_fusion), channel_id=1, source_target_pairs={{1,0},{2,1},{3,2},{4,3},{5,4},{6,5},{7,6},{9,8},{10,9},{11,10},{12... | collective-permute-start | bytes 331784 | tf_op jit(solution)/shard_map/ppermute | solution.py:10
  28.2 3.3 %copy-start = (bf16[7,2,192,192]{3,2,1,0:T(8,128)(2,1)S(1)}, bf16[7,2,192,192]{3,2,1,0:T(8,128)(2,1)}, u32[]{:S(2)}) copy-start(bf16[7,2,192,192]{3,2,1,0:T(8,128)(2,1)} %param.7) | copy-start | bytes 3096580
  32.3 1.0 %copy-start.1 = (bf16[24,24,192]{2,1,0:T(8,128)(2,1)S(1)}, bf16[24,24,192]{2,1,0:T(8,128)(2,1)}, u32[]{:S(2)}) copy-start(bf16[24,24,192]{2,1,0:T(8,128)(2,1)} %param.9) | copy-start | bytes 663556
where the time goes:
time: 49.5 us; the launch traced here: 48.9 us
  local copies, waits for them, and re-layouts  17.8 us (36%)
  blocking collectives  14 us (28%)
  starting transfers between devices  6.18 us (12%)
  other arithmetic  4.8 us (10%)
  matrix products  4.74 us (10%)
  between operations  1.46 us (3%)
    all_gather x1, blocking collectives, on_device(): lax.all_gather(coarse_flat, 'grp', axis=0, tiled=True)  9.16 us
    ppermute x2, starting transfers between devices, passed_along(): return lax.ppermute(value, axis, pairs)  6.18 us
    gather x2, local copies, waits for them, and re-layouts, on_device(): gathered = jnp.take(prolong_table, lookup, axis=0)  5.97 us
    unnamed x1, blocking collectives  4.81 us
    dot_general x1, matrix products, on_device(): jnp.einsum('eai,eski->eask', prolong.astype(jnp.float32), applied, precis...  2.47 us
    unnamed x7, local copies, waits for them, and re-layouts  2.19 us
    convert_element_type x2, local copies, waits for them, and re-layouts, on_device(): coarse_block.reshape(element_count, row_width).astype(jnp.bfloat16)  2.03 us
    reshape x1, local copies, waits for them, and re-layouts, on_device(): received.reshape(group_count * capacity, coarse, block_slots * coarse)  1.73 us
  transfers between devices with their start and end apart: 2, of which 0 were waited for; matrix products, arithmetic and copies ran while one was open for 15% of the time, Pallas kernels for 0%

commit v1 on v0

v1 whole, which is shorter than its diff:
```python
import functools

import jax
import jax.numpy as jnp
from jax import lax
from jax.experimental import pallas as pl
from jax.experimental.pallas import tpu as pltpu
from jax.sharding import PartitionSpec as P

LANES = 128
VMEM = pl.BlockSpec(memory_space=pltpu.VMEM)
SMEM = pl.BlockSpec(memory_space=pltpu.SMEM)


def in_vmem(value):
    return pltpu.with_memory_space_constraint(value, pltpu.VMEM)


def params():
    return pltpu.CompilerParams(vmem_limit_bytes=24 * 1024 * 1024)


def passed_along(value, axis, by):
    peers = lax.axis_size(axis)
    pairs = [(i, i + by) for i in range(peers) if 0 <= i + by < peers]
    return lax.ppermute(value, axis, pairs)


def pack_kernel(count_ref, offset_ref, prolong_ref, below_ref, above_ref):
    elements = prolong_ref.shape[0]
    for way, out_ref in enumerate((below_ref, above_ref)):
        first = offset_ref[0, way]
        length = count_ref[0, way]

        def block(slot):
            value = prolong_ref[jnp.minimum(first + slot, elements - 1)].astype(jnp.float32)
            return jnp.where(slot < length, value, 0.0)

        for pair in range(out_ref.shape[0]):
            even, odd = block(2 * pair), block(2 * pair + 1)
            tail = jnp.concatenate([even[:, LANES:], odd[:, LANES:]], axis=1)
            out_ref[pair] = jnp.concatenate(
                [even[:, :LANES], odd[:, :LANES], tail], axis=0
            ).astype(jnp.bfloat16)


def left_kernel(lame_ref, stiffness_ref, prolong_ref, left_ref):
    elements, slots, rows, _ = left_ref.shape
    coarse = rows // 2
    own = prolong_ref[...]
    for s in range(slots):
        first = jnp.dot(own, stiffness_ref[s, 0], preferred_element_type=jnp.float32)
        second = jnp.dot(own, stiffness_ref[s, 1], preferred_element_type=jnp.float32)
        for e in range(elements):
            part = slice(e * coarse, (e + 1) * coarse)
            total = lame_ref[s, 0, e] * first[part] + lame_ref[s, 1, e] * second[part]
            high = total.astype(jnp.bfloat16).astype(jnp.float32)
            left_ref[e, s] = jnp.concatenate([high, total - high], axis=0).astype(jnp.bfloat16)


def rows_kernel(columns_ref, owner_ref, prolong_ref, below_ref, above_ref, left_ref, out_ref, table, filled):
    elements, coarse, fine = prolong_ref.shape
    slots = left_ref.shape[1]
    ghosts = 2 * below_ref.shape[0]
    owners = filled.shape[0]
    capacity = out_ref.shape[0] // owners
    half = fine - LANES
    for e in range(elements):
        table[e] = prolong_ref[e].astype(jnp.float32)
    for start, ref in ((elements, below_ref), (elements + ghosts, above_ref)):
        for pair in range(ghosts // 2):
            block = ref[pair].astype(jnp.float32)
            tail = block[2 * coarse :]
            for odd in range(2):
                table[start + 2 * pair + odd] = jnp.concatenate(
                    [block[odd * coarse : (odd + 1) * coarse], tail[:, odd * half : (odd + 1) * half]], axis=1
                )
    table[elements + 2 * ghosts] = jnp.zeros((coarse, fine), jnp.float32)

    lane8 = lax.broadcasted_iota(jnp.int32, (8, LANES), 1)
    empty = jnp.concatenate(
        [jnp.zeros((coarse, LANES), jnp.float32), jnp.where(lane8 >= 120, -1.0, 0.0)], axis=0
    ).astype(jnp.bfloat16)
    for i in range(out_ref.shape[0]):
        out_ref[i] = empty
    for t in range(owners):
        filled[t] = 0

    width = slots * coarse
    lane = lax.broadcasted_iota(jnp.int32, (coarse, width), 1)
    for e in range(elements):
        blocks = []
        for s in range(slots):
            c = columns_ref[e, s]
            blocks.append(table[jnp.where(c < 0, elements + 2 * ghosts, c)])
        right = jnp.concatenate(blocks, axis=0).astype(jnp.bfloat16)
        left = left_ref[e].reshape(slots * 2 * coarse, fine)
        product = lax.dot_general(
            left, right, (((1,), (1,)), ((), ())), preferred_element_type=jnp.float32
        )
        result = None
        for s in range(slots):
            at = 2 * coarse * s
            part = product[at : at + coarse] + product[at + coarse : at + 2 * coarse]
            result = part if s == 0 else jnp.where(lane >= s * coarse, part, result)
        rest = result[:, LANES:]
        tail = jnp.concatenate(
            [rest[0:8], rest[8:16], rest[16:24], jnp.full((8, 8), e, jnp.float32)], axis=1
        )
        target = owner_ref[e]
        position = filled[target]
        filled[target] = position + 1
        out_ref[target * capacity + position] = jnp.concatenate(
            [result[:, :LANES], tail], axis=0
        ).astype(jnp.bfloat16)


def unpack_kernel(elements, capacity, received_ref, rows_ref, ids_ref):
    rest = rows_ref.shape[2] - LANES
    lane = lax.broadcasted_iota(jnp.int32, (8, LANES), 1)
    count = rows_ref.shape[0]
    wide = pl.cdiv(count, LANES)
    local = [jnp.full((8, LANES), -1.0, jnp.float32) for _ in range(wide)]
    for i in range(count):
        block = received_ref[i].astype(jnp.float32)
        tail = block[24:32]
        rows_ref[i] = jnp.concatenate(
            [
                block[0:24],
                jnp.concatenate([tail[:, rest * q : rest * (q + 1)] for q in range(3)], axis=0),
            ],
            axis=1,
        ).astype(jnp.bfloat16)
        local[i // LANES] = jnp.where(lane == i % LANES, tail[:, 127:128], local[i // LANES])
    local = jnp.concatenate(local, axis=1)[0:1, :count].astype(jnp.int32)
    group = lax.broadcasted_iota(jnp.int32, (1, count), 1) // capacity
    first = (group * lax.axis_size("row") + lax.axis_index("row")) * elements
    ids_ref[...] = jnp.where(local >= 0, first + local, -1)


def on_device(stiffness, lame, prolong, columns, ghost_count, ghost_offset, owner_map):
    elements, coarse, fine = prolong.shape
    slots = stiffness.shape[0]
    ghosts = elements // 2
    owners = lax.axis_size("grp")
    capacity = 2 * ((elements + owners - 1) // owners)
    run = pltpu.VMEM((ghosts // 2, 3 * coarse, LANES), jnp.bfloat16)
    to_below, to_above = pl.pallas_call(
        pack_kernel, out_shape=(run, run), in_specs=[SMEM, SMEM, VMEM], out_specs=(VMEM, VMEM),
        compiler_params=params(), name="pack",
    )(ghost_count, ghost_offset, prolong)
    from_below = passed_along(to_above, "row", 1)
    from_above = passed_along(to_below, "row", -1)
    left = pl.pallas_call(
        left_kernel,
        out_shape=pltpu.VMEM((elements, slots, 2 * coarse, fine), jnp.bfloat16),
        in_specs=[SMEM, VMEM, VMEM], out_specs=VMEM,
        compiler_params=params(), name="left",
    )(lame.transpose(1, 2, 0), stiffness, prolong.reshape(elements * coarse, fine))
    packed = pl.pallas_call(
        rows_kernel,
        out_shape=pltpu.VMEM((owners * capacity, 32, LANES), jnp.bfloat16),
        in_specs=[SMEM, SMEM, VMEM, VMEM, VMEM, VMEM], out_specs=VMEM,
        scratch_shapes=[
            pltpu.VMEM((elements + 2 * ghosts + 1, coarse, fine), jnp.float32),
            pltpu.SMEM((owners,), jnp.int32),
        ],
        compiler_params=params(), name="rows",
    )(columns, owner_map[:, 0], prolong, in_vmem(from_below), in_vmem(from_above), in_vmem(left))
    received = lax.all_to_all(packed, "grp", split_axis=0, concat_axis=0, tiled=True)
    coarse_rows, ids = pl.pallas_call(
        functools.partial(unpack_kernel, elements, capacity),
        out_shape=(
            jax.ShapeDtypeStruct((owners * capacity, coarse, slots * coarse), jnp.bfloat16),
            jax.ShapeDtypeStruct((1, owners * capacity), jnp.int32),
        ),
        in_specs=[VMEM], out_specs=(VMEM, VMEM),
        compiler_params=params(), name="unpack",
    )(in_vmem(received))
    return (coarse_rows, ids.reshape(-1))


def solution(mesh):
    split = ("grp", "row")
    return jax.shard_map(
        on_device, mesh=mesh,
        in_specs=(P(), P(split, None, None), P(split, None, None)) + (P(split, None),) * 4,
        out_specs=(P(split, None, None), P(split)), check_vma=False,
    )
```

time: 49.5 us -> 29.6 us (0.60)
  the two profiles are of different devices: /device:TPU:9 before, /device:TPU:24 now
where the time goes in v1:
time: 29.6 us; the launch traced here: 29.3 us
  blocking collectives  10 us (34%)
  starting transfers between devices  6.74 us (23%)
  local copies, waits for them, and re-layouts  6.03 us (20%)
  Pallas kernels  5.76 us (19%)
  between operations  0.7 us (2%)
    all_to_all x1, blocking collectives, on_device(): lax.all_to_all(packed, 'grp', split_axis=0, concat_axis=0, tiled=True)  10 us
    ppermute x2, starting transfers between devices, passed_along(): return lax.ppermute(value, axis, pairs)  6.74 us
    unnamed x15, local copies, waits for them, and re-layouts  6.03 us
    pallas_call x1, Pallas kernels, on_device(): pl.pallas_call(rows_kernel, out_shape=pltpu.VMEM((owners * capacity, 32,...  2.25 us
    pallas_call x1, Pallas kernels, on_device(): pl.pallas_call(left_kernel, out_shape=pltpu.VMEM((elements, slots, 2 * co...  1.89 us
    pallas_call x1, Pallas kernels, on_device(): pl.pallas_call(functools.partial(unpack_kernel, elements, capacity), out_...  0.97 us
    pallas_call x1, Pallas kernels, on_device(): pl.pallas_call(pack_kernel, out_shape=(run, run), in_specs=[SMEM, SMEM, V...  0.65 us
  transfers between devices with their start and end apart: 2, of which 0 were waited for; matrix products, arithmetic and copies ran while one was open for 3% of the time, Pallas kernels for 6%

profile of v1, /device:TPU:24, one launch (start us, length us, event | category | flops | bytes accessed | tf_op | source)
XLA Modules:
  0.0 29.3 jit_solution(18056663023483149617)
XLA Ops:
  0.6 0.0 copy-start
  0.6 1.0 %copy-done = bf16[24,24,192]{2,1,0:T(8,128)(2,1)S(1)} copy-done((bf16[24,24,192]{2,1,0:T(8,128)(2,1)S(1)}, bf16[24,24,192]{2,1,0:T(8,128)(2,1)}, u32[]{:S(2)}) %copy-start) | copy-done | bytes 221208
  1.6 0.0 copy-start.4
  1.6 0.7 %copy-done.4 = s32[1,2]{1,0:T(1,128)S(1)} copy-done((s32[1,2]{1,0:T(1,128)S(1)}, s32[1,2]{1,0:T(1,128)}, u32[]{:S(2)}) %copy-start.4) | copy-done | bytes 32
  2.3 0.0 copy-start.5
  2.3 0.7 %copy-done.5 = s32[1,2]{1,0:T(1,128)S(1)} copy-done((s32[1,2]{1,0:T(1,128)S(1)}, s32[1,2]{1,0:T(1,128)}, u32[]{:S(2)}) %copy-start.5) | copy-done | bytes 32
  2.9 0.0 copy-start.6
  2.9 0.6 %pack.1 = (bf16[6,72,128]{2,1,0:T(8,128)(2,1)S(1)}, bf16[6,72,128]{2,1,0:T(8,128)(2,1)S(1)}) custom-call(s32[1,2]{1,0:T(1,128)S(1)} %copy-done.4, s32[1,2]{1,0:T(1,128)S(1)} %copy-done.5, bf16[24,24,192]{2,1,0:T(8,128)(2,1)S(1)} %copy-done), custom_call_target="tpu_custom_call" | custom-call | tf_op jit(solution)/shard_map/pack/pallas_call | solution.py:148
  3.6 3.4 %collective-permute-start = (bf16[6,72,128]{2,1,0:T(8,128)(2,1)S(1)}, bf16[6,72,128]{2,1,0:T(8,128)(2,1)S(1)}, u32[]{:S(2)}, u32[]{:S(2)}) collective-permute-start(bf16[6,72,128]{2,1,0:T(8,128)(2,1)S(1)} %get-tuple-element.6), channel_id=1, source_target_pairs={{0,1},{1,2},{2,3},{3,4},{4,5},{5,6},{6,7},{8,9},{9,10},{10,11},{11... | collective-permute-start | bytes 331784 | tf_op jit(solution)/shard_map/ppermute | solution.py:26
  7.0 3.3 %collective-permute-start.1 = (bf16[6,72,128]{2,1,0:T(8,128)(2,1)S(1)}, bf16[6,72,128]{2,1,0:T(8,128)(2,1)S(1)}, u32[]{:S(2)}, u32[]{:S(2)}) collective-permute-start(bf16[6,72,128]{2,1,0:T(8,128)(2,1)S(1)} %get-tuple-element.7), channel_id=1, source_target_pairs={{1,0},{2,1},{3,2},{4,3},{5,4},{6,5},{7,6},{9,8},{10,9},{11,10},{12... | collective-permute-start | bytes 331784 | tf_op jit(solution)/shard_map/ppermute | solution.py:26
  10.3 0.8 %copy.9.columns_ref = s32[24,7]{1,0:T(8,128)S(1)} copy(s32[24,7]{0,1:T(8,128)} %param.10) | data formatting | bytes 1344 | tf_op args[3]
  11.1 0.0 copy-start.1
  11.1 1.0 %copy-done.1 = bf16[24,24,192]{2,1,0:T(8,128)(2,1)S(1)} copy-done((bf16[24,24,192]{2,1,0:T(8,128)(2,1)S(1)}, bf16[24,24,192]{2,1,0:T(8,128)(2,1)}, u32[]{:S(2)}) %copy-start.1) | copy-done | bytes 221208
  12.1 0.0 copy-start.2
  12.1 1.3 %copy-done.2 = bf16[7,2,192,192]{3,2,1,0:T(8,128)(2,1)S(1)} copy-done((bf16[7,2,192,192]{3,2,1,0:T(8,128)(2,1)S(1)}, bf16[7,2,192,192]{3,2,1,0:T(8,128)(2,1)}, u32[]{:S(2)}) %copy-start.2) | copy-done | bytes 1032216
  13.4 0.0 copy-start.3
  13.4 0.7 %copy-done.3 = f32[24,7,2]{0,2,1:T(2,128)S(1)} copy-done((f32[24,7,2]{0,2,1:T(2,128)S(1)}, f32[24,7,2]{0,2,1:T(2,128)}, u32[]{:S(2)}) %copy-start.3) | copy-done | bytes 1368
  14.1 1.9 %left.1.left_ref = bf16[24,7,48,192]{3,2,1,0:T(8,128)(2,1)S(1)} custom-call(f32[7,2,24]{2,1,0:T(2,128)S(1)} %bitcast.5, bf16[7,2,192,192]{3,2,1,0:T(8,128)(2,1)S(1)} %copy-done.2, bf16[576,192]{1,0:T(8,128)(2,1)S(1)} %bitcast.4), custom_call_target="tpu_custom_call" | custom-call | tf_op jit(solution)/shard_map/left/pallas_call | solution.py:154
  16.0 0.0 collective-permute-done.below_ref
  16.0 0.0 collective-permute-done.1.above_ref
  16.0 0.0 copy-done.6
  16.0 2.3 %rows.1 = bf16[48,32,128]{2,1,0:T(8,128)(2,1)S(1)} custom-call(s32[24,7]{1,0:T(8,128)S(1)} %copy.9.columns_ref, s32[24]{0:T(128)S(1)} %bitcast.6, bf16[24,24,192]{2,1,0:T(8,128)(2,1)S(1)} %copy-done.1, bf16[6,72,128]{2,1,0:T(8,128)(2,1)S(1)} %collective-permute-done.below_ref, bf16[6,72,128]{2,1,0:T(8,128)(2,1)S(1)} %collective-permute-done.1.above_ref, ...), custom_call_target="tpu_custom_call" | custom-call | tf_op jit(solution)/shard_map/rows/pallas_call | solution.py:160
  18.3 10.0 %all_to_all.5.received_ref = bf16[48,32,128]{2,1,0:T(8,128)(2,1)S(1)} all-to-all(bf16[48,32,128]{2,1,0:T(8,128)(2,1)S(1)} %rows.1), channel_id=1, replica_groups=mesh['grp'=4,'row'=8] {'grp'}, dimensions={0} | all-to-all | bytes 786432 | tf_op jit(solution)/shard_map/all_to_all | solution.py:170
  28.3 1.0 %unpack.1 = (bf16[48,24,168]{2,1,0:T(8,128)(2,1)}, s32[1,48]{1,0:T(1,128)}) custom-call(bf16[48,32,128]{2,1,0:T(8,128)(2,1)S(1)} %all_to_all.5.received_ref), custom_call_target="tpu_custom_call" | custom-call | tf_op jit(solution)/shard_map/unpack/pallas_call | solution.py:171
Async XLA Ops:
  0.6 1.0 %copy-start = (bf16[24,24,192]{2,1,0:T(8,128)(2,1)S(1)}, bf16[24,24,192]{2,1,0:T(8,128)(2,1)}, u32[]{:S(2)}) copy-start(bf16[24,24,192]{2,1,0:T(8,128)(2,1)} %prolong_ref.3) | copy-start | bytes 663556
  1.6 0.7 %copy-start.4 = (s32[1,2]{1,0:T(1,128)S(1)}, s32[1,2]{1,0:T(1,128)}, u32[]{:S(2)}) copy-start(s32[1,2]{1,0:T(1,128)} %count_ref.1) | copy-start | bytes 28
  2.3 0.7 %copy-start.5 = (s32[1,2]{1,0:T(1,128)S(1)}, s32[1,2]{1,0:T(1,128)}, u32[]{:S(2)}) copy-start(s32[1,2]{1,0:T(1,128)} %offset_ref.1) | copy-start | bytes 28
  2.9 13.1 %copy-start.6 = (s32[24,1]{0,1:T(1,128)S(1)}, s32[24,1]{0,1:T(1,128)}, u32[]{:S(2)}) copy-start(s32[24,1]{0,1:T(1,128)} %param.13) | copy-start | bytes 292
  3.6 12.4 %collective-permute-start = (bf16[6,72,128]{2,1,0:T(8,128)(2,1)S(1)}, bf16[6,72,128]{2,1,0:T(8,128)(2,1)S(1)}, u32[]{:S(2)}, u32[]{:S(2)}) collective-permute-start(bf16[6,72,128]{2,1,0:T(8,128)(2,1)S(1)} %get-tuple-element.6), channel_id=1, source_target_pairs={{0,1},{1,2},{2,3},{3,4},{4,5},{5,6},{6,7},{8,9},{9,10},{10,11},{11... | collective-permute-start | bytes 331784 | tf_op jit(solution)/shard_map/ppermute | solution.py:26
  7.0 9.0 %collective-permute-start.1 = (bf16[6,72,128]{2,1,0:T(8,128)(2,1)S(1)}, bf16[6,72,128]{2,1,0:T(8,128)(2,1)S(1)}, u32[]{:S(2)}, u32[]{:S(2)}) collective-permute-start(bf16[6,72,128]{2,1,0:T(8,128)(2,1)S(1)} %get-tuple-element.7), channel_id=1, source_target_pairs={{1,0},{2,1},{3,2},{4,3},{5,4},{6,5},{7,6},{9,8},{10,9},{11,10},{12... | collective-permute-start | bytes 331784 | tf_op jit(solution)/shard_map/ppermute | solution.py:26
  11.1 1.0 %copy-start.1 = (bf16[24,24,192]{2,1,0:T(8,128)(2,1)S(1)}, bf16[24,24,192]{2,1,0:T(8,128)(2,1)}, u32[]{:S(2)}) copy-start(bf16[24,24,192]{2,1,0:T(8,128)(2,1)} %prolong_ref.3) | copy-start | bytes 663556
  12.1 1.3 %copy-start.2 = (bf16[7,2,192,192]{3,2,1,0:T(8,128)(2,1)S(1)}, bf16[7,2,192,192]{3,2,1,0:T(8,128)(2,1)}, u32[]{:S(2)}) copy-start(bf16[7,2,192,192]{3,2,1,0:T(8,128)(2,1)} %stiffness_ref.1) | copy-start | bytes 3096580
  13.4 0.7 %copy-start.3 = (f32[24,7,2]{0,2,1:T(2,128)S(1)}, f32[24,7,2]{0,2,1:T(2,128)}, u32[]{:S(2)}) copy-start(f32[24,7,2]{0,2,1:T(2,128)} %param.8) | copy-start | bytes 4036

commit v2 on v1

v2 whole, which is shorter than its diff:
```python
import functools

import jax
import jax.numpy as jnp
from jax import lax
from jax.experimental import pallas as pl
from jax.experimental.pallas import tpu as pltpu
from jax.sharding import PartitionSpec as P

LANES = 128
VMEM = pl.BlockSpec(memory_space=pltpu.VMEM)
HBM = pl.BlockSpec(memory_space=pltpu.HBM)
SMEM = pl.BlockSpec(memory_space=pltpu.SMEM)


def in_vmem(value):
    return pltpu.with_memory_space_constraint(value, pltpu.VMEM)


def in_smem(value):
    return pltpu.with_memory_space_constraint(value, pltpu.SMEM)


def in_hbm(value):
    return pltpu.with_memory_space_constraint(value, pltpu.HBM)


def params():
    return pltpu.CompilerParams(vmem_limit_bytes=24 * 1024 * 1024)


def passed_along(value, axis, by):
    peers = lax.axis_size(axis)
    pairs = [(i, i + by) for i in range(peers) if 0 <= i + by < peers]
    return lax.ppermute(value, axis, pairs)


def fetch(pairs, sems):
    copies = [pltpu.make_async_copy(src, dst, sems.at[i]) for i, (src, dst) in enumerate(pairs)]
    for copy in copies:
        copy.start()
    return copies


def pack_kernel(count_hbm, offset_hbm, prolong_hbm, below_ref, above_ref, count_ref, offset_ref, prolong_ref, sems):
    copies = fetch(
        [(count_hbm, count_ref), (offset_hbm, offset_ref), (prolong_hbm, prolong_ref)], sems
    )
    for copy in copies:
        copy.wait()
    elements = prolong_ref.shape[0]
    for way, out_ref in enumerate((below_ref, above_ref)):
        first = offset_ref[0, way]
        length = count_ref[0, way]

        def block(slot):
            value = prolong_ref[jnp.minimum(first + slot, elements - 1)].astype(jnp.float32)
            return jnp.where(slot < length, value, 0.0)

        for pair in range(out_ref.shape[0]):
            even, odd = block(2 * pair), block(2 * pair + 1)
            tail = jnp.concatenate([even[:, LANES:], odd[:, LANES:]], axis=1)
            out_ref[pair] = jnp.concatenate(
                [even[:, :LANES], odd[:, :LANES], tail], axis=0
            ).astype(jnp.bfloat16)


def left_kernel(
    lame_hbm, columns_hbm, owner_hbm, stiffness_hbm, prolong_hbm,
    left_ref, prolong_ref, columns_ref, place_ref, start_ref,
    lame_ref, owner_ref, stiffness_ref, filled, sems,
):
    elements, slots, rows, _ = left_ref.shape
    coarse = rows // 2
    owners = filled.shape[0]
    copies = fetch(
        [(prolong_hbm, prolong_ref), (lame_hbm, lame_ref), (owner_hbm, owner_ref), (columns_hbm, columns_ref)]
        + [(stiffness_hbm.at[s], stiffness_ref.at[s]) for s in range(slots)],
        sems,
    )
    for copy in copies[:3]:
        copy.wait()
    for t in range(owners):
        filled[t] = 0
    for e in range(elements):
        filled[owner_ref[0, e]] = filled[owner_ref[0, e]] + 1
    total = jnp.int32(0)
    for t in range(owners):
        start_ref[t] = total
        total = total + filled[t]
        filled[t] = start_ref[t]
    start_ref[owners] = total
    for e in range(elements):
        place_ref[e] = filled[owner_ref[0, e]]
        filled[owner_ref[0, e]] = place_ref[e] + 1

    own = prolong_ref[...]
    for s in range(slots):
        copies[4 + s].wait()
        first = jnp.dot(own, stiffness_ref[s, 0], preferred_element_type=jnp.float32)
        second = jnp.dot(own, stiffness_ref[s, 1], preferred_element_type=jnp.float32)
        for e in range(elements):
            part = slice(e * coarse, (e + 1) * coarse)
            total = lame_ref[s, 0, e] * first[part] + lame_ref[s, 1, e] * second[part]
            high = total.astype(jnp.bfloat16).astype(jnp.float32)
            left_ref[e, s] = jnp.concatenate([high, total - high], axis=0).astype(jnp.bfloat16)
    copies[3].wait()


def rows_kernel(columns_ref, place_ref, start_ref, prolong_ref, below_ref, above_ref, left_ref, out_ref, table):
    elements, slots, rows, fine = left_ref.shape
    coarse = rows // 2
    ghosts = 2 * below_ref.shape[0]
    half = fine - LANES
    owners = start_ref.shape[0] - 1
    for e in range(elements):
        table[e] = prolong_ref[e * coarse : (e + 1) * coarse].astype(jnp.float32)
    for start, ref in ((elements, below_ref), (elements + ghosts, above_ref)):
        for pair in range(ghosts // 2):
            block = ref[pair].astype(jnp.float32)
            tail = block[2 * coarse :]
            for odd in range(2):
                table[start + 2 * pair + odd] = jnp.concatenate(
                    [block[odd * coarse : (odd + 1) * coarse], tail[:, odd * half : (odd + 1) * half]], axis=1
                )
    table[elements + 2 * ghosts] = jnp.zeros((coarse, fine), jnp.float32)

    row8 = lax.broadcasted_iota(jnp.int32, (8, 8), 0)
    lane8 = lax.broadcasted_iota(jnp.int32, (8, 8), 1)
    starts = jnp.zeros((8, 8), jnp.float32)
    for t in range(owners):
        here = jnp.logical_and(row8 == t % 8, lane8 == t // 8)
        starts = jnp.where(here, start_ref[t].astype(jnp.float32), starts)

    width = slots * coarse
    lane = lax.broadcasted_iota(jnp.int32, (coarse, width), 1)
    for e in range(elements):
        blocks = []
        for s in range(slots):
            c = columns_ref[s, e]
            blocks.append(table[jnp.where(c < 0, elements + 2 * ghosts, c)])
        right = jnp.concatenate(blocks, axis=0).astype(jnp.bfloat16)
        left = left_ref[e].reshape(slots * 2 * coarse, fine)
        product = lax.dot_general(
            left, right, (((1,), (1,)), ((), ())), preferred_element_type=jnp.float32
        )
        result = None
        for s in range(slots):
            at = 2 * coarse * s
            part = product[at : at + coarse] + product[at + coarse : at + 2 * coarse]
            result = part if s == 0 else jnp.where(lane >= s * coarse, part, result)
        rest = result[:, LANES:]
        spare = jnp.where(lane8 >= 2, jnp.float32(e), starts)
        tail = jnp.concatenate([rest[0:8], rest[8:16], rest[16:24], spare], axis=1)
        out_ref[place_ref[e]] = jnp.concatenate([result[:, :LANES], tail], axis=0).astype(jnp.bfloat16)


def unpack_kernel(elements, capacity, received_ref, rows_ref, ids_ref):
    rest = rows_ref.shape[2] - LANES
    count = rows_ref.shape[0]
    owners = count // capacity
    me = lax.axis_index("grp")
    row = lax.broadcasted_iota(jnp.int32, (8, LANES), 0)
    lane = lax.broadcasted_iota(jnp.int32, (8, LANES), 1)
    wide = pl.cdiv(count, LANES)
    local = [jnp.full((8, LANES), -1.0, jnp.float32) for _ in range(wide)]

    def start_of(tail, t):
        here = jnp.logical_and(row == t % 8, lane == 120 + t // 8)
        return jnp.sum(jnp.where(here, tail, 0.0)).astype(jnp.int32)

    bounds = []
    for source in range(owners):
        tail = received_ref[source * elements].astype(jnp.float32)[24:32]
        begin = start_of(tail, me)
        end = jnp.where(me == owners - 1, elements, start_of(tail, jnp.minimum(me + 1, owners - 1)))
        bounds.append((begin, end - begin))
    for i in range(count):
        source, slot = i // capacity, i % capacity
        begin, length = bounds[source]
        block = received_ref[source * elements + jnp.minimum(begin + slot, elements - 1)].astype(jnp.float32)
        block = jnp.where(slot < length, block, 0.0)
        tail = block[24:32]
        rows_ref[i] = jnp.concatenate(
            [
                block[0:24],
                jnp.concatenate([tail[:, rest * q : rest * (q + 1)] for q in range(3)], axis=0),
            ],
            axis=1,
        ).astype(jnp.bfloat16)
        here = jnp.logical_and(lane == i % LANES, slot < length)
        local[i // LANES] = jnp.where(here, tail[:, 127:128], local[i // LANES])
    local = jnp.concatenate(local, axis=1)[0:1, :count].astype(jnp.int32)
    group = lax.broadcasted_iota(jnp.int32, (1, count), 1) // capacity
    first = (group * lax.axis_size("row") + lax.axis_index("row")) * elements
    ids_ref[...] = jnp.where(local >= 0, first + local, -1)


def on_device(stiffness, lame, prolong, columns, ghost_count, ghost_offset, owner_map):
    elements, coarse, fine = prolong.shape
    slots = stiffness.shape[0]
    ghosts = elements // 2
    owners = lax.axis_size("grp")
    capacity = 2 * ((elements + owners - 1) // owners)
    run = pltpu.VMEM((ghosts // 2, 3 * coarse, LANES), jnp.bfloat16)
    to_below, to_above = pl.pallas_call(
        pack_kernel, out_shape=(run, run), in_specs=[HBM] * 3, out_specs=(VMEM, VMEM),
        scratch_shapes=[
            pltpu.SMEM(ghost_count.shape, jnp.int32),
            pltpu.SMEM(ghost_offset.shape, jnp.int32),
            pltpu.VMEM(prolong.shape, jnp.bfloat16),
            pltpu.SemaphoreType.DMA((3,)),
        ],
        compiler_params=params(), name="pack",
    )(in_hbm(ghost_count), in_hbm(ghost_offset), in_hbm(prolong))
    from_below = passed_along(to_above, "row", 1)
    from_above = passed_along(to_below, "row", -1)
    left, own, by_slot, place, start = pl.pallas_call(
        left_kernel,
        out_shape=(
            pltpu.VMEM((elements, slots, 2 * coarse, fine), jnp.bfloat16),
            pltpu.VMEM((elements * coarse, fine), jnp.bfloat16),
            pltpu.SMEM((slots, elements), jnp.int32),
            pltpu.SMEM((elements,), jnp.int32),
            pltpu.SMEM((owners + 1,), jnp.int32),
        ),
        in_specs=[HBM] * 5, out_specs=(VMEM, VMEM, SMEM, SMEM, SMEM),
        scratch_shapes=[
            pltpu.SMEM((slots, 2, elements), jnp.float32),
            pltpu.SMEM((1, elements), jnp.int32),
            pltpu.VMEM(stiffness.shape, jnp.bfloat16),
            pltpu.SMEM((owners,), jnp.int32),
            pltpu.SemaphoreType.DMA((4 + slots,)),
        ],
        compiler_params=params(), name="left",
    )(
        in_hbm(lame.transpose(1, 2, 0)), in_hbm(columns.T), in_hbm(owner_map.T),
        in_hbm(stiffness), in_hbm(prolong.reshape(elements * coarse, fine)),
    )
    packed = pl.pallas_call(
        rows_kernel,
        out_shape=pltpu.VMEM((elements, 32, LANES), jnp.bfloat16),
        in_specs=[SMEM, SMEM, SMEM, VMEM, VMEM, VMEM, VMEM], out_specs=VMEM,
        scratch_shapes=[pltpu.VMEM((elements + 2 * ghosts + 1, coarse, fine), jnp.float32)],
        compiler_params=params(), name="rows",
    )(
        in_smem(by_slot), in_smem(place), in_smem(start), in_vmem(own),
        in_vmem(from_below), in_vmem(from_above), in_vmem(left),
    )
    received = lax.all_gather(packed, "grp", axis=0, tiled=True)
    coarse_rows, ids = pl.pallas_call(
        functools.partial(unpack_kernel, elements, capacity),
        out_shape=(
            jax.ShapeDtypeStruct((owners * capacity, coarse, slots * coarse), jnp.bfloat16),
            jax.ShapeDtypeStruct((1, owners * capacity), jnp.int32),
        ),
        in_specs=[VMEM], out_specs=(VMEM, VMEM),
        compiler_params=params(), name="unpack",
    )(in_vmem(received))
    return (coarse_rows, ids.reshape(-1))


def solution(mesh):
    split = ("grp", "row")
    return jax.shard_map(
        on_device, mesh=mesh,
        in_specs=(P(), P(split, None, None), P(split, None, None)) + (P(split, None),) * 4,
        out_specs=(P(split, None, None), P(split)), check_vma=False,
    )
```

time: 29.6 us -> 24.7 us (0.83)
  the two profiles are of different devices: /device:TPU:24 before, /device:TPU:11 now
where the time goes in v2:
time: 24.7 us; the launch traced here: 24.5 us
  blocking collectives  10.6 us (43%)
  Pallas kernels  7.32 us (30%)
  starting transfers between devices  5.28 us (21%)
  waiting for transfers between devices  0.68 us (3%)
  between operations  0.67 us (3%)
    all_gather x1, blocking collectives, on_device(): received = lax.all_gather(packed, 'grp', axis=0, tiled=True)  10.6 us
    ppermute x2, starting transfers between devices, passed_along(): return lax.ppermute(value, axis, pairs)  5.28 us
    pallas_call x1, Pallas kernels, on_device(): pl.pallas_call(left_kernel, out_shape=(pltpu.VMEM((elements, slots, 2 * c...  3.58 us
    pallas_call x1, Pallas kernels, on_device(): pl.pallas_call(rows_kernel, out_shape=pltpu.VMEM((elements, 32, LANES), j...  1.48 us
    pallas_call x1, Pallas kernels, on_device(): pl.pallas_call(functools.partial(unpack_kernel, elements, capacity), out_...  1.17 us
    pallas_call x1, Pallas kernels, on_device(): pl.pallas_call(pack_kernel, out_shape=(run, run), in_specs=[HBM] * 3, out...  1.09 us
    ppermute x2, waiting for transfers between devices, passed_along(): return lax.ppermute(value, axis, pairs)  0.68 us
  transfers between devices with their start and end apart: 2, of which 1 were waited for; matrix products, arithmetic and copies ran while one was open for 0% of the time, Pallas kernels for 15%

profile of v2, /device:TPU:11, one launch (start us, length us, event | category | flops | bytes accessed | tf_op | source)
XLA Modules:
  0.0 24.5 jit_solution(9098199062458924237)
XLA Ops:
  0.6 1.1 %pack.1 = (bf16[6,72,128]{2,1,0:T(8,128)(2,1)S(1)}, bf16[6,72,128]{2,1,0:T(8,128)(2,1)S(1)}) custom-call(s32[1,2]{1,0:T(1,128)} %count_hbm.1, s32[1,2]{1,0:T(1,128)} %offset_hbm.1, bf16[24,24,192]{2,1,0:T(8,128)(2,1)} %prolong_hbm.1), custom_call_target="tpu_custom_call" | custom-call | tf_op jit(solution)/shard_map/pack/pallas_call | solution.py:206
  1.7 3.2 %collective-permute-start = (bf16[6,72,128]{2,1,0:T(8,128)(2,1)S(1)}, bf16[6,72,128]{2,1,0:T(8,128)(2,1)S(1)}, u32[]{:S(2)}, u32[]{:S(2)}) collective-permute-start(bf16[6,72,128]{2,1,0:T(8,128)(2,1)S(1)} %get-tuple-element.15), channel_id=1, source_target_pairs={{0,1},{1,2},{2,3},{3,4},{4,5},{5,6},{6,7},{8,9},{9,10},{10,11},{11... | collective-permute-start | bytes 331784 | tf_op jit(solution)/shard_map/ppermute | solution.py:35
  4.9 2.1 %collective-permute-start.1 = (bf16[6,72,128]{2,1,0:T(8,128)(2,1)S(1)}, bf16[6,72,128]{2,1,0:T(8,128)(2,1)S(1)}, u32[]{:S(2)}, u32[]{:S(2)}) collective-permute-start(bf16[6,72,128]{2,1,0:T(8,128)(2,1)S(1)} %get-tuple-element.16), channel_id=1, source_target_pairs={{1,0},{2,1},{3,2},{4,3},{5,4},{6,5},{7,6},{9,8},{10,9},{11,10},{12... | collective-permute-start | bytes 331784 | tf_op jit(solution)/shard_map/ppermute | solution.py:35
  7.0 3.6 %left.1 = (bf16[24,7,48,192]{3,2,1,0:T(8,128)(2,1)S(1)}, bf16[576,192]{1,0:T(8,128)(2,1)S(1)}, s32[7,24]{1,0:T(8,128)S(4)}, s32[24]{0:T(128)S(4)}, s32[5]{0:T(128)S(4)}) custom-call(f32[7,2,24]{2,1,0:T(2,128)} %bitcast.6, s32[7,24]{1,0:T(8,128)} %bitcast.7, s32[1,24]{1,0:T(1,128)} %bitcast.8, bf16[7,2,192,192]{3,2,1,0:T(8,128)(2,1)} %stiffness_hbm.1, ...), custom_call_target="tpu_custom_call" | custom-call | tf_op jit(solution)/shard_map/left/pallas_call | solution.py:218
  10.6 0.0 collective-permute-done.below_ref
  10.6 0.7 %collective-permute-done.1.above_ref = bf16[6,72,128]{2,1,0:T(8,128)(2,1)S(1)} collective-permute-done((bf16[6,72,128]{2,1,0:T(8,128)(2,1)S(1)}, bf16[6,72,128]{2,1,0:T(8,128)(2,1)S(1)}, u32[]{:S(2)}, u32[]{:S(2)}) %collective-permute-start.1) | collective-permute-done | bytes 110624 | tf_op jit(solution)/shard_map/ppermute | solution.py:35
  11.3 1.5 %rows.1 = bf16[24,32,128]{2,1,0:T(8,128)(2,1)S(1)} custom-call(s32[7,24]{1,0:T(8,128)S(4)} %get-tuple-element.11.columns_ref, s32[24]{0:T(128)S(4)} %get-tuple-element.12.place_ref, s32[5]{0:T(128)S(4)} %get-tuple-element.13.start_ref, bf16[576,192]{1,0:T(8,128)(2,1)S(1)} %get-tuple-element.14.prolong_ref, ...), custom_call_target="tpu_custom_call" | custom-call | tf_op jit(solution)/shard_map/rows/pallas_call | solution.py:240
  12.8 10.6 %all_gather.3.received_ref = bf16[96,32,128]{2,1,0:T(8,128)(2,1)S(1)} all-gather(bf16[24,32,128]{2,1,0:T(8,128)(2,1)S(1)} %rows.1), channel_id=1, replica_groups=mesh['grp'=4,'row'=8] {'grp'}, dimensions={0}, use_global_device_ids=true | all-gather | bytes 983040 | tf_op jit(solution)/shard_map/all_gather | solution.py:250
  23.3 1.2 %unpack.1 = (bf16[48,24,168]{2,1,0:T(8,128)(2,1)}, s32[1,48]{1,0:T(1,128)}) custom-call(bf16[96,32,128]{2,1,0:T(8,128)(2,1)S(1)} %all_gather.3.received_ref), custom_call_target="tpu_custom_call" | custom-call | tf_op jit(solution)/shard_map/unpack/pallas_call | solution.py:251
Async XLA Ops:
  1.7 8.9 %collective-permute-start = (bf16[6,72,128]{2,1,0:T(8,128)(2,1)S(1)}, bf16[6,72,128]{2,1,0:T(8,128)(2,1)S(1)}, u32[]{:S(2)}, u32[]{:S(2)}) collective-permute-start(bf16[6,72,128]{2,1,0:T(8,128)(2,1)S(1)} %get-tuple-element.15), channel_id=1, source_target_pairs={{0,1},{1,2},{2,3},{3,4},{4,5},{5,6},{6,7},{8,9},{9,10},{10,11},{11... | collective-permute-start | bytes 331784 | tf_op jit(solution)/shard_map/ppermute | solution.py:35
  4.9 6.4 %collective-permute-start.1 = (bf16[6,72,128]{2,1,0:T(8,128)(2,1)S(1)}, bf16[6,72,128]{2,1,0:T(8,128)(2,1)S(1)}, u32[]{:S(2)}, u32[]{:S(2)}) collective-permute-start(bf16[6,72,128]{2,1,0:T(8,128)(2,1)S(1)} %get-tuple-element.16), channel_id=1, source_target_pairs={{1,0},{2,1},{3,2},{4,3},{5,4},{6,5},{7,6},{9,8},{10,9},{11,10},{12... | collective-permute-start | bytes 331784 | tf_op jit(solution)/shard_map/ppermute | solution.py:35

commit v3 on v2

--- a/solution.py
+++ b/solution.py
@@ -29,10 +29,10 @@
     return pltpu.CompilerParams(vmem_limit_bytes=24 * 1024 * 1024)
 
 
-def passed_along(value, axis, by):
+def swapped(value, axis, parity):
     peers = lax.axis_size(axis)
-    pairs = [(i, i + by) for i in range(peers) if 0 <= i + by < peers]
-    return lax.ppermute(value, axis, pairs)
+    pairs = [(i, i + 1) for i in range(parity, peers - 1, 2)]
+    return lax.ppermute(value, axis, pairs + [(j, i) for i, j in pairs])
 
 
 def fetch(pairs, sems):
@@ -42,14 +42,23 @@
     return copies
 
 
-def pack_kernel(count_hbm, offset_hbm, prolong_hbm, below_ref, above_ref, count_ref, offset_ref, prolong_ref, sems):
+def pack_kernel(
+    count_hbm, offset_hbm, prolong_hbm, lame_hbm, columns_hbm, owner_hbm, stiffness_hbm,
+    odd_ref, even_ref, prolong_ref, lame_ref, columns_ref, owner_ref, stiffness_ref,
+    count_ref, offset_ref, sems,
+):
     copies = fetch(
-        [(count_hbm, count_ref), (offset_hbm, offset_ref), (prolong_hbm, prolong_ref)], sems
-    )
-    for copy in copies:
+        [
+            (count_hbm, count_ref), (offset_hbm, offset_ref), (prolong_hbm, prolong_ref), (lame_hbm, lame_ref),
+            (columns_hbm, columns_ref), (owner_hbm, owner_ref), (stiffness_hbm, stiffness_ref),
+        ],
+        sems,
+    )
+    for copy in copies[:3]:
         copy.wait()
     elements = prolong_ref.shape[0]
-    for way, out_ref in enumerate((below_ref, above_ref)):
+    odd_row = lax.rem(lax.axis_index("row"), 2)
+    for way, out_ref in ((odd_row, odd_ref), (1 - odd_row, even_ref)):
         first = offset_ref[0, way]
         length = count_ref[0, way]
 
@@ -63,23 +72,14 @@
             out_ref[pair] = jnp.concatenate(
                 [even[:, :LANES], odd[:, :LANES], tail], axis=0
             ).astype(jnp.bfloat16)
-
-
-def left_kernel(
-    lame_hbm, columns_hbm, owner_hbm, stiffness_hbm, prolong_hbm,
-    left_ref, prolong_ref, columns_ref, place_ref, start_ref,
-    lame_ref, owner_ref, stiffness_ref, filled, sems,
-):
+    for copy in copies[3:]:
+        copy.wait()
+
+
+def left_kernel(lame_ref, owner_ref, stiffness_ref, prolong_ref, left_ref, place_ref, start_ref, filled):
     elements, slots, rows, _ = left_ref.shape
     coarse = rows // 2
     owners = filled.shape[0]
-    copies = fetch(
-        [(prolong_hbm, prolong_ref), (lame_hbm, lame_ref), (owner_hbm, owner_ref), (columns_hbm, columns_ref)]
-        + [(stiffness_hbm.at[s], stiffness_ref.at[s]) for s in range(slots)],
-        sems,
-    )
-    for copy in copies[:3]:
-        copy.wait()
     for t in range(owners):
         filled[t] = 0
     for e in range(elements):
@@ -96,7 +96,6 @@
 
     own = prolong_ref[...]
     for s in range(slots):
-        copies[4 + s].wait()
         first = jnp.dot(own, stiffness_ref[s, 0], preferred_element_type=jnp.float32)
         second = jnp.dot(own, stiffness_ref[s, 1], preferred_element_type=jnp.float32)
         for e in range(elements):
@@ -104,18 +103,18 @@
             total = lame_ref[s, 0, e] * first[part] + lame_ref[s, 1, e] * second[part]
             high = total.astype(jnp.bfloat16).astype(jnp.float32)
             left_ref[e, s] = jnp.concatenate([high, total - high], axis=0).astype(jnp.bfloat16)
-    copies[3].wait()
-
-
-def rows_kernel(columns_ref, place_ref, start_ref, prolong_ref, below_ref, above_ref, left_ref, out_ref, table):
+
+
+def rows_kernel(columns_ref, place_ref, start_ref, prolong_ref, odd_ref, even_ref, left_ref, out_ref, table):
     elements, slots, rows, fine = left_ref.shape
     coarse = rows // 2
-    ghosts = 2 * below_ref.shape[0]
+    ghosts = 2 * odd_ref.shape[0]
+    odd_row = lax.rem(lax.axis_index("row"), 2)
     half = fine - LANES
     owners = start_ref.shape[0] - 1
     for e in range(elements):
         table[e] = prolong_ref[e * coarse : (e + 1) * coarse].astype(jnp.float32)
-    for start, ref in ((elements, below_ref), (elements + ghosts, above_ref)):
+    for start, ref in ((elements + ghosts * odd_row, odd_ref), (elements + ghosts * (1 - odd_row), even_ref)):
         for pair in range(ghosts // 2):
             block = ref[pair].astype(jnp.float32)
             tail = block[2 * coarse :]
@@ -203,40 +202,41 @@
     owners = lax.axis_size("grp")
     capacity = 2 * ((elements + owners - 1) // owners)
     run = pltpu.VMEM((ghosts // 2, 3 * coarse, LANES), jnp.bfloat16)
-    to_below, to_above = pl.pallas_call(
-        pack_kernel, out_shape=(run, run), in_specs=[HBM] * 3, out_specs=(VMEM, VMEM),
+    by_odd, by_even, own, lame_slots, by_slot, owner, tables = pl.pallas_call(
+        pack_kernel,
+        out_shape=(
+            run, run,
+            pltpu.VMEM(prolong.shape, jnp.bfloat16),
+            pltpu.SMEM((slots, 2, elements), jnp.float32),
+            pltpu.SMEM((slots, elements), jnp.int32),
+            pltpu.SMEM((1, elements), jnp.int32),
+            pltpu.VMEM(stiffness.shape, jnp.bfloat16),
+        ),
+        in_specs=[HBM] * 7, out_specs=(VMEM, VMEM, VMEM, SMEM, SMEM, SMEM, VMEM),
         scratch_shapes=[
             pltpu.SMEM(ghost_count.shape, jnp.int32),
             pltpu.SMEM(ghost_offset.shape, jnp.int32),
-            pltpu.VMEM(prolong.shape, jnp.bfloat16),
-            pltpu.SemaphoreType.DMA((3,)),
+            pltpu.SemaphoreType.DMA((7,)),
         ],
         compiler_params=params(), name="pack",
-    )(in_hbm(ghost_count), in_hbm(ghost_offset), in_hbm(prolong))
-    from_below = passed_along(to_above, "row", 1)
-    from_above = passed_along(to_below, "row", -1)
-    left, own, by_slot, place, start = pl.pallas_call(
+    )(
+        in_hbm(ghost_count), in_hbm(ghost_offset), in_hbm(prolong), in_hbm(lame.transpose(1, 2, 0)),
+        in_hbm(columns.T), in_hbm(owner_map.T), in_hbm(stiffness),
+    )
+    from_odd = swapped(by_odd, "row", 1)
+    from_even = swapped(by_even, "row", 0)
+    own = in_vmem(own.reshape(elements * coarse, fine))
+    left, place, start = pl.pallas_call(
         left_kernel,
         out_shape=(
             pltpu.VMEM((elements, slots, 2 * coarse, fine), jnp.bfloat16),
-            pltpu.VMEM((elements * coarse, fine), jnp.bfloat16),
-            pltpu.SMEM((slots, elements), jnp.int32),
             pltpu.SMEM((elements,), jnp.int32),
             pltpu.SMEM((owners + 1,), jnp.int32),
         ),
-        in_specs=[HBM] * 5, out_specs=(VMEM, VMEM, SMEM, SMEM, SMEM),
-        scratch_shapes=[
-            pltpu.SMEM((slots, 2, elements), jnp.float32),
-            pltpu.SMEM((1, elements), jnp.int32),
-            pltpu.VMEM(stiffness.shape, jnp.bfloat16),
-            pltpu.SMEM((owners,), jnp.int32),
-            pltpu.SemaphoreType.DMA((4 + slots,)),
-        ],
+        in_specs=[SMEM, SMEM, VMEM, VMEM], out_specs=(VMEM, SMEM, SMEM),
+        scratch_shapes=[pltpu.SMEM((owners,), jnp.int32)],
         compiler_params=params(), name="left",
-    )(
-        in_hbm(lame.transpose(1, 2, 0)), in_hbm(columns.T), in_hbm(owner_map.T),
-        in_hbm(stiffness), in_hbm(prolong.reshape(elements * coarse, fine)),
-    )
+    )(in_smem(lame_slots), in_smem(owner), in_vmem(tables), own)
     packed = pl.pallas_call(
         rows_kernel,
         out_shape=pltpu.VMEM((elements, 32, LANES), jnp.bfloat16),
@@ -244,8 +244,8 @@
         scratch_shapes=[pltpu.VMEM((elements + 2 * ghosts + 1, coarse, fine), jnp.float32)],
         compiler_params=params(), name="rows",
     )(
-        in_smem(by_slot), in_smem(place), in_smem(start), in_vmem(own),
-        in_vmem(from_below), in_vmem(from_above), in_vmem(left),
+        in_smem(by_slot), in_smem(place), in_smem(start), own,
+        in_vmem(from_odd), in_vmem(from_even), in_vmem(left),
     )
     received = lax.all_gather(packed, "grp", axis=0, tiled=True)
     coarse_rows, ids = pl.pallas_call(

time: 24.7 us -> 24.1 us (0.976)
  the two profiles are of different devices: /device:TPU:11 before, /device:TPU:9 now
where the time goes in v3:
time: 24.1 us; the launch traced here: 23.9 us
  blocking collectives  8.94 us (37%)
  Pallas kernels  5.4 us (22%)
  starting transfers between devices  4.45 us (18%)
  waiting for transfers between devices  4.44 us (18%)
  between operations  0.66 us (3%)
    all_gather x1, blocking collectives, on_device(): received = lax.all_gather(packed, 'grp', axis=0, tiled=True)  8.94 us
    ppermute x2, starting transfers between devices, swapped(): return lax.ppermute(value, axis, pairs + [(j, i) for i, j in pairs])  4.45 us
    ppermute x2, waiting for transfers between devices, swapped(): return lax.ppermute(value, axis, pairs + [(j, i) for i, j in pairs])  4.44 us
    pallas_call x1, Pallas kernels, on_device(): pl.pallas_call(pack_kernel, out_shape=(run, run, pltpu.VMEM(prolong.shape...  1.51 us
    pallas_call x1, Pallas kernels, on_device(): pl.pallas_call(rows_kernel, out_shape=pltpu.VMEM((elements, 32, LANES), j...  1.49 us
    pallas_call x1, Pallas kernels, on_device(): pl.pallas_call(left_kernel, out_shape=(pltpu.VMEM((elements, slots, 2 * c...  1.24 us
    pallas_call x1, Pallas kernels, on_device(): pl.pallas_call(functools.partial(unpack_kernel, elements, capacity), out_...  1.17 us
  transfers between devices with their start and end apart: 2, of which 2 were waited for; matrix products, arithmetic and copies ran while one was open for 0% of the time, Pallas kernels for 5%

profile of v3, /device:TPU:9, one launch (start us, length us, event | category | flops | bytes accessed | tf_op | source)
XLA Modules:
  0.0 23.9 jit_solution(3629721762831680918)
XLA Ops:
  0.6 1.5 %pack.1 = (bf16[6,72,128]{2,1,0:T(8,128)(2,1)S(1)}, bf16[6,72,128]{2,1,0:T(8,128)(2,1)S(1)}, bf16[24,24,192]{2,1,0:T(8,128)(2,1)S(1)}, f32[7,2,24]{2,1,0:T(2,128...) custom-call(s32[1,2]{1,0:T(1,128)} %count_hbm.1, s32[1,2]{1,0:T(1,128)} %offset_hbm.1, ...), custom_call_target="tpu_custom_call" | custom-call | tf_op jit(solution)/shard_map/pack/pallas_call | solution.py:205
  2.1 3.0 %collective-permute-start = (bf16[6,72,128]{2,1,0:T(8,128)(2,1)S(1)}, bf16[6,72,128]{2,1,0:T(8,128)(2,1)S(1)}, u32[]{:S(2)}, u32[]{:S(2)}) collective-permute-start(bf16[6,72,128]{2,1,0:T(8,128)(2,1)S(1)} %get-tuple-element.21), channel_id=1, source_target_pairs={{1,2},{3,4},{5,6},{2,1},{4,3},{6,5},{9,10},{11,12},{13,14},{10,9},... | collective-permute-start | bytes 331784 | tf_op jit(solution)/shard_map/ppermute | solution.py:35
  5.2 1.4 %collective-permute-start.1 = (bf16[6,72,128]{2,1,0:T(8,128)(2,1)S(1)}, bf16[6,72,128]{2,1,0:T(8,128)(2,1)S(1)}, u32[]{:S(2)}, u32[]{:S(2)}) collective-permute-start(bf16[6,72,128]{2,1,0:T(8,128)(2,1)S(1)} %get-tuple-element.22), channel_id=1, source_target_pairs={{0,1},{2,3},{4,5},{6,7},{1,0},{3,2},{5,4},{7,6},{8,9},{10,11},{12,... | collective-permute-start | bytes 331784 | tf_op jit(solution)/shard_map/ppermute | solution.py:35
  6.6 1.2 %left.1 = (bf16[24,7,48,192]{3,2,1,0:T(8,128)(2,1)S(1)}, s32[24]{0:T(128)S(4)}, s32[5]{0:T(128)S(4)}) custom-call(f32[7,2,24]{2,1,0:T(2,128)S(4)} %get-tuple-element.15.lame_ref, s32[1,24]{1,0:T(1,128)S(4)} %get-tuple-element.16.owner_ref, bf16[7,2,192,192]{3,2,1,0:T(8,128)(2,1)S(1)} %get-tuple-element.17.stiffness_ref, bf16[576,192]{1,0:T(8,128)(2,1)S(1)} %bitcast.5), custom_call_target="tpu_custom_call" | custom-call | tf_op jit(solution)/shard_map/left/pallas_call | solution.py:229
  7.8 1.0 %collective-permute-done.odd_ref = bf16[6,72,128]{2,1,0:T(8,128)(2,1)S(1)} collective-permute-done((bf16[6,72,128]{2,1,0:T(8,128)(2,1)S(1)}, bf16[6,72,128]{2,1,0:T(8,128)(2,1)S(1)}, u32[]{:S(2)}, u32[]{:S(2)}) %collective-permute-start) | collective-permute-done | bytes 110624 | tf_op jit(solution)/shard_map/ppermute | solution.py:35
  8.9 3.4 %collective-permute-done.1.even_ref = bf16[6,72,128]{2,1,0:T(8,128)(2,1)S(1)} collective-permute-done((bf16[6,72,128]{2,1,0:T(8,128)(2,1)S(1)}, bf16[6,72,128]{2,1,0:T(8,128)(2,1)S(1)}, u32[]{:S(2)}, u32[]{:S(2)}) %collective-permute-start.1) | collective-permute-done | bytes 110624 | tf_op jit(solution)/shard_map/ppermute | solution.py:35
  12.3 1.5 %rows.1 = bf16[24,32,128]{2,1,0:T(8,128)(2,1)S(1)} custom-call(s32[7,24]{1,0:T(8,128)S(4)} %get-tuple-element.14.columns_ref, s32[24]{0:T(128)S(4)} %get-tuple-element.19.place_ref, s32[5]{0:T(128)S(4)} %get-tuple-element.20.start_ref, bf16[576,192]{1,0:T(8,128)(2,1)S(1)} %bitcast.6, bf16[6,72,128]{2,1,0:T(8,128)(2,1)S(1)} %collective-permute-done.odd_ref, ...), custom_call_target="tpu_custom_call" | custom-call | tf_op jit(solution)/shard_map/rows/pallas_call | solution.py:240
  13.8 8.9 %all_gather.3.received_ref = bf16[96,32,128]{2,1,0:T(8,128)(2,1)S(1)} all-gather(bf16[24,32,128]{2,1,0:T(8,128)(2,1)S(1)} %rows.1), channel_id=1, replica_groups=mesh['grp'=4,'row'=8] {'grp'}, dimensions={0}, use_global_device_ids=true | all-gather | bytes 983040 | tf_op jit(solution)/shard_map/all_gather | solution.py:250
  22.7 1.2 %unpack.1 = (bf16[48,24,168]{2,1,0:T(8,128)(2,1)}, s32[1,48]{1,0:T(1,128)}) custom-call(bf16[96,32,128]{2,1,0:T(8,128)(2,1)S(1)} %all_gather.3.received_ref), custom_call_target="tpu_custom_call" | custom-call | tf_op jit(solution)/shard_map/unpack/pallas_call | solution.py:251
Async XLA Ops:
  2.1 6.7 %collective-permute-start = (bf16[6,72,128]{2,1,0:T(8,128)(2,1)S(1)}, bf16[6,72,128]{2,1,0:T(8,128)(2,1)S(1)}, u32[]{:S(2)}, u32[]{:S(2)}) collective-permute-start(bf16[6,72,128]{2,1,0:T(8,128)(2,1)S(1)} %get-tuple-element.21), channel_id=1, source_target_pairs={{1,2},{3,4},{5,6},{2,1},{4,3},{6,5},{9,10},{11,12},{13,14},{10,9},... | collective-permute-start | bytes 331784 | tf_op jit(solution)/shard_map/ppermute | solution.py:35
  5.2 7.1 %collective-permute-start.1 = (bf16[6,72,128]{2,1,0:T(8,128)(2,1)S(1)}, bf16[6,72,128]{2,1,0:T(8,128)(2,1)S(1)}, u32[]{:S(2)}, u32[]{:S(2)}) collective-permute-start(bf16[6,72,128]{2,1,0:T(8,128)(2,1)S(1)} %get-tuple-element.22), channel_id=1, source_target_pairs={{0,1},{2,3},{4,5},{6,7},{1,0},{3,2},{5,4},{7,6},{8,9},{10,11},{12,... | collective-permute-start | bytes 331784 | tf_op jit(solution)/shard_map/ppermute | solution.py:35

commit v4 on v3

--- a/solution.py
+++ b/solution.py
@@ -43,18 +43,12 @@
 
 
 def pack_kernel(
-    count_hbm, offset_hbm, prolong_hbm, lame_hbm, columns_hbm, owner_hbm, stiffness_hbm,
-    odd_ref, even_ref, prolong_ref, lame_ref, columns_ref, owner_ref, stiffness_ref,
-    count_ref, offset_ref, sems,
+    count_hbm, offset_hbm, prolong_hbm, odd_ref, even_ref, prolong_ref, count_ref, offset_ref, sems,
 ):
     copies = fetch(
-        [
-            (count_hbm, count_ref), (offset_hbm, offset_ref), (prolong_hbm, prolong_ref), (lame_hbm, lame_ref),
-            (columns_hbm, columns_ref), (owner_hbm, owner_ref), (stiffness_hbm, stiffness_ref),
-        ],
-        sems,
-    )
-    for copy in copies[:3]:
+        [(prolong_hbm, prolong_ref), (count_hbm, count_ref), (offset_hbm, offset_ref)], sems
+    )
+    for copy in copies:
         copy.wait()
     elements = prolong_ref.shape[0]
     odd_row = lax.rem(lax.axis_index("row"), 2)
@@ -72,14 +66,22 @@
             out_ref[pair] = jnp.concatenate(
                 [even[:, :LANES], odd[:, :LANES], tail], axis=0
             ).astype(jnp.bfloat16)
-    for copy in copies[3:]:
-        copy.wait()
-
-
-def left_kernel(lame_ref, owner_ref, stiffness_ref, prolong_ref, left_ref, place_ref, start_ref, filled):
+
+
+def left_kernel(
+    lame_hbm, columns_hbm, owner_hbm, stiffness_hbm, prolong_ref,
+    left_ref, columns_ref, place_ref, start_ref,
+    lame_ref, owner_ref, stiffness_ref, filled, sems,
+):
     elements, slots, rows, _ = left_ref.shape
     coarse = rows // 2
     owners = filled.shape[0]
+    copies = fetch(
+        [(stiffness_hbm.at[s], stiffness_ref.at[s]) for s in range(slots)]
+        + [(lame_hbm, lame_ref), (owner_hbm, owner_ref), (columns_hbm, columns_ref)],
+        sems,
+    )
+    copies[slots + 1].wait()
     for t in range(owners):
         filled[t] = 0
     for e in range(elements):
@@ -94,8 +96,11 @@
         place_ref[e] = filled[owner_ref[0, e]]
         filled[owner_ref[0, e]] = place_ref[e] + 1
 
+    for copy in copies[slots:slots + 1] + copies[slots + 2:]:
+        copy.wait()
     own = prolong_ref[...]
     for s in range(slots):
+        copies[s].wait()
         first = jnp.dot(own, stiffness_ref[s, 0], preferred_element_type=jnp.float32)
         second = jnp.dot(own, stiffness_ref[s, 1], preferred_element_type=jnp.float32)
         for e in range(elements):
@@ -202,41 +207,38 @@
     owners = lax.axis_size("grp")
     capacity = 2 * ((elements + owners - 1) // owners)
     run = pltpu.VMEM((ghosts // 2, 3 * coarse, LANES), jnp.bfloat16)
-    by_odd, by_even, own, lame_slots, by_slot, owner, tables = pl.pallas_call(
+    by_odd, by_even, own = pl.pallas_call(
         pack_kernel,
-        out_shape=(
-            run, run,
-            pltpu.VMEM(prolong.shape, jnp.bfloat16),
-            pltpu.SMEM((slots, 2, elements), jnp.float32),
-            pltpu.SMEM((slots, elements), jnp.int32),
-            pltpu.SMEM((1, elements), jnp.int32),
-            pltpu.VMEM(stiffness.shape, jnp.bfloat16),
-        ),
-        in_specs=[HBM] * 7, out_specs=(VMEM, VMEM, VMEM, SMEM, SMEM, SMEM, VMEM),
+        out_shape=(run, run, pltpu.VMEM(prolong.shape, jnp.bfloat16)),
+        in_specs=[HBM] * 3, out_specs=(VMEM, VMEM, VMEM),
         scratch_shapes=[
             pltpu.SMEM(ghost_count.shape, jnp.int32),
             pltpu.SMEM(ghost_offset.shape, jnp.int32),
-            pltpu.SemaphoreType.DMA((7,)),
+            pltpu.SemaphoreType.DMA((3,)),
         ],
         compiler_params=params(), name="pack",
-    )(
-        in_hbm(ghost_count), in_hbm(ghost_offset), in_hbm(prolong), in_hbm(lame.transpose(1, 2, 0)),
-        in_hbm(columns.T), in_hbm(owner_map.T), in_hbm(stiffness),
-    )
+    )(in_hbm(ghost_count), in_hbm(ghost_offset), in_hbm(prolong))
+    from_even = swapped(by_even, "row", 0)
     from_odd = swapped(by_odd, "row", 1)
-    from_even = swapped(by_even, "row", 0)
     own = in_vmem(own.reshape(elements * coarse, fine))
-    left, place, start = pl.pallas_call(
+    left, by_slot, place, start = pl.pallas_call(
         left_kernel,
         out_shape=(
             pltpu.VMEM((elements, slots, 2 * coarse, fine), jnp.bfloat16),
+            pltpu.SMEM((slots, elements), jnp.int32),
             pltpu.SMEM((elements,), jnp.int32),
             pltpu.SMEM((owners + 1,), jnp.int32),
         ),
-        in_specs=[SMEM, SMEM, VMEM, VMEM], out_specs=(VMEM, SMEM, SMEM),
-        scratch_shapes=[pltpu.SMEM((owners,), jnp.int32)],
+        in_specs=[HBM] * 4 + [VMEM], out_specs=(VMEM, SMEM, SMEM, SMEM),
+        scratch_shapes=[
+            pltpu.SMEM((slots, 2, elements), jnp.float32),
+            pltpu.SMEM((1, elements), jnp.int32),
+            pltpu.VMEM(stiffness.shape, jnp.bfloat16),
+            pltpu.SMEM((owners,), jnp.int32),
+            pltpu.SemaphoreType.DMA((slots + 3,)),
+        ],
         compiler_params=params(), name="left",
-    )(in_smem(lame_slots), in_smem(owner), in_vmem(tables), own)
+    )(in_hbm(lame.transpose(1, 2, 0)), in_hbm(columns.T), in_hbm(owner_map.T), in_hbm(stiffness), own)
     packed = pl.pallas_call(
         rows_kernel,
         out_shape=pltpu.VMEM((elements, 32, LANES), jnp.bfloat16),

time: 24.1 us -> 23.7 us (0.983)
  waiting for transfers between devices: 4.44 us -> 2.15 us
  Pallas kernels: 5.4 us -> 7.3 us
    ppermute x2, waiting for transfers between devices: 4.44 us -> 2.15 us  [swapped(): return lax.ppermute(value, axis, pairs + [(j, i) for i, j in pairs])]
    pallas_call x1, Pallas kernels: 1.24 us -> 3.51 us  [on_device(): pl.pallas_call(left_kernel, out_shape=(pltpu.VMEM((elements, slots, 2 * c...]
    pallas_call x1, Pallas kernels: 1.51 us -> 1.12 us  [on_device(): pl.pallas_call(pack_kernel, out_shape=(run, run, pltpu.VMEM(prolong.shape...]
  transfers between devices with their start and end apart: 2 -> 2, of which waited for: 2 -> 1; matrix products, arithmetic and copies ran while one was open for 0% -> 0% of each run, Pallas kernels for 5% -> 15%
where the time goes in v4:
time: 23.7 us; the launch traced here: 23.5 us
  blocking collectives  8.94 us (38%)
  Pallas kernels  7.3 us (31%)
  starting transfers between devices  4.45 us (19%)
  waiting for transfers between devices  2.15 us (9%)
  between operations  0.66 us (3%)
    all_gather x1, blocking collectives, on_device(): received = lax.all_gather(packed, 'grp', axis=0, tiled=True)  8.94 us
    ppermute x2, starting transfers between devices, swapped(): return lax.ppermute(value, axis, pairs + [(j, i) for i, j in pairs])  4.45 us
    pallas_call x1, Pallas kernels, on_device(): pl.pallas_call(left_kernel, out_shape=(pltpu.VMEM((elements, slots, 2 * c...  3.51 us
    ppermute x2, waiting for transfers between devices, swapped(): return lax.ppermute(value, axis, pairs + [(j, i) for i, j in pairs])  2.15 us
    pallas_call x1, Pallas kernels, on_device(): pl.pallas_call(rows_kernel, out_shape=pltpu.VMEM((elements, 32, LANES), j...  1.5 us
    pallas_call x1, Pallas kernels, on_device(): pl.pallas_call(functools.partial(unpack_kernel, elements, capacity), out_...  1.17 us
    pallas_call x1, Pallas kernels, on_device(): pl.pallas_call(pack_kernel, out_shape=(run, run, pltpu.VMEM(prolong.shape...  1.12 us
  transfers between devices with their start and end apart: 2, of which 1 were waited for; matrix products, arithmetic and copies ran while one was open for 0% of the time, Pallas kernels for 15%

profile of v4, /device:TPU:9, one launch (start us, length us, event | category | flops | bytes accessed | tf_op | source)
XLA Modules:
  0.0 23.5 jit_solution(3624188592118290934)
XLA Ops:
  0.6 1.1 %pack.1 = (bf16[6,72,128]{2,1,0:T(8,128)(2,1)S(1)}, bf16[6,72,128]{2,1,0:T(8,128)(2,1)S(1)}, bf16[24,24,192]{2,1,0:T(8,128)(2,1)S(1)}) custom-call(s32[1,2]{1,0:T(1,128)} %count_hbm.1, s32[1,2]{1,0:T(1,128)} %offset_hbm.1, bf16[24,24,192]{2,1,0:T(8,128)(2,1)} %prolong_hbm.1), custom_call_target="tpu_custom_call" | custom-call | tf_op jit(solution)/shard_map/pack/pallas_call | solution.py:210
  1.8 3.0 %collective-permute-start = (bf16[6,72,128]{2,1,0:T(8,128)(2,1)S(1)}, bf16[6,72,128]{2,1,0:T(8,128)(2,1)S(1)}, u32[]{:S(2)}, u32[]{:S(2)}) collective-permute-start(bf16[6,72,128]{2,1,0:T(8,128)(2,1)S(1)} %get-tuple-element.15), channel_id=1, source_target_pairs={{1,2},{3,4},{5,6},{2,1},{4,3},{6,5},{9,10},{11,12},{13,14},{10,9},... | collective-permute-start | bytes 331784 | tf_op jit(solution)/shard_map/ppermute | solution.py:35
  4.8 1.4 %collective-permute-start.1 = (bf16[6,72,128]{2,1,0:T(8,128)(2,1)S(1)}, bf16[6,72,128]{2,1,0:T(8,128)(2,1)S(1)}, u32[]{:S(2)}, u32[]{:S(2)}) collective-permute-start(bf16[6,72,128]{2,1,0:T(8,128)(2,1)S(1)} %get-tuple-element.16), channel_id=1, source_target_pairs={{0,1},{2,3},{4,5},{6,7},{1,0},{3,2},{5,4},{7,6},{8,9},{10,11},{12,... | collective-permute-start | bytes 331784 | tf_op jit(solution)/shard_map/ppermute | solution.py:35
  6.2 3.5 %left.1 = (bf16[24,7,48,192]{3,2,1,0:T(8,128)(2,1)S(1)}, s32[7,24]{1,0:T(8,128)S(4)}, s32[24]{0:T(128)S(4)}, s32[5]{0:T(128)S(4)}) custom-call(f32[7,2,24]{2,1,0:T(2,128)} %bitcast.7, s32[7,24]{1,0:T(8,128)} %bitcast.8, s32[1,24]{1,0:T(1,128)} %bitcast.9, bf16[7,2,192,192]{3,2,1,0:T(8,128)(2,1)} %stiffness_hbm.1, bf16[576,192]{1,0:T(8,128)(2,1)S(1)} %bitcast.5), custom_call_target="tpu_custom_call" | custom-call | tf_op jit(solution)/shard_map/left/pallas_call | solution.py:224
  9.7 0.0 collective-permute-done.odd_ref
  9.8 2.1 %collective-permute-done.1.even_ref = bf16[6,72,128]{2,1,0:T(8,128)(2,1)S(1)} collective-permute-done((bf16[6,72,128]{2,1,0:T(8,128)(2,1)S(1)}, bf16[6,72,128]{2,1,0:T(8,128)(2,1)S(1)}, u32[]{:S(2)}, u32[]{:S(2)}) %collective-permute-start.1) | collective-permute-done | bytes 110624 | tf_op jit(solution)/shard_map/ppermute | solution.py:35
  11.9 1.5 %rows.1 = bf16[24,32,128]{2,1,0:T(8,128)(2,1)S(1)} custom-call(s32[7,24]{1,0:T(8,128)S(4)} %get-tuple-element.12.columns_ref, s32[24]{0:T(128)S(4)} %get-tuple-element.13.place_ref, s32[5]{0:T(128)S(4)} %get-tuple-element.14.start_ref, bf16[576,192]{1,0:T(8,128)(2,1)S(1)} %bitcast.6, bf16[6,72,128]{2,1,0:T(8,128)(2,1)S(1)} %collective-permute-done.odd_ref, ...), custom_call_target="tpu_custom_call" | custom-call | tf_op jit(solution)/shard_map/rows/pallas_call | solution.py:242
  13.4 8.9 %all_gather.3.received_ref = bf16[96,32,128]{2,1,0:T(8,128)(2,1)S(1)} all-gather(bf16[24,32,128]{2,1,0:T(8,128)(2,1)S(1)} %rows.1), channel_id=1, replica_groups=mesh['grp'=4,'row'=8] {'grp'}, dimensions={0}, use_global_device_ids=true | all-gather | bytes 983040 | tf_op jit(solution)/shard_map/all_gather | solution.py:252
  22.3 1.2 %unpack.1 = (bf16[48,24,168]{2,1,0:T(8,128)(2,1)}, s32[1,48]{1,0:T(1,128)}) custom-call(bf16[96,32,128]{2,1,0:T(8,128)(2,1)S(1)} %all_gather.3.received_ref), custom_call_target="tpu_custom_call" | custom-call | tf_op jit(solution)/shard_map/unpack/pallas_call | solution.py:253
Async XLA Ops:
  1.8 8.0 %collective-permute-start = (bf16[6,72,128]{2,1,0:T(8,128)(2,1)S(1)}, bf16[6,72,128]{2,1,0:T(8,128)(2,1)S(1)}, u32[]{:S(2)}, u32[]{:S(2)}) collective-permute-start(bf16[6,72,128]{2,1,0:T(8,128)(2,1)S(1)} %get-tuple-element.15), channel_id=1, source_target_pairs={{1,2},{3,4},{5,6},{2,1},{4,3},{6,5},{9,10},{11,12},{13,14},{10,9},... | collective-permute-start | bytes 331784 | tf_op jit(solution)/shard_map/ppermute | solution.py:35
  4.8 7.1 %collective-permute-start.1 = (bf16[6,72,128]{2,1,0:T(8,128)(2,1)S(1)}, bf16[6,72,128]{2,1,0:T(8,128)(2,1)S(1)}, u32[]{:S(2)}, u32[]{:S(2)}) collective-permute-start(bf16[6,72,128]{2,1,0:T(8,128)(2,1)S(1)} %get-tuple-element.16), channel_id=1, source_target_pairs={{0,1},{2,3},{4,5},{6,7},{1,0},{3,2},{5,4},{7,6},{8,9},{10,11},{12,... | collective-permute-start | bytes 331784 | tf_op jit(solution)/shard_map/ppermute | solution.py:35

commit v5 on v3

--- a/solution.py
+++ b/solution.py
@@ -43,18 +43,18 @@
 
 
 def pack_kernel(
-    count_hbm, offset_hbm, prolong_hbm, lame_hbm, columns_hbm, owner_hbm, stiffness_hbm,
-    odd_ref, even_ref, prolong_ref, lame_ref, columns_ref, owner_ref, stiffness_ref,
+    count_hbm, offset_hbm, prolong_hbm, lame_hbm, columns_hbm, owner_hbm,
+    odd_ref, even_ref, prolong_ref, lame_ref, columns_ref, owner_ref,
     count_ref, offset_ref, sems,
 ):
     copies = fetch(
         [
-            (count_hbm, count_ref), (offset_hbm, offset_ref), (prolong_hbm, prolong_ref), (lame_hbm, lame_ref),
-            (columns_hbm, columns_ref), (owner_hbm, owner_ref), (stiffness_hbm, stiffness_ref),
+            (prolong_hbm, prolong_ref), (count_hbm, count_ref), (offset_hbm, offset_ref),
+            (lame_hbm, lame_ref), (columns_hbm, columns_ref), (owner_hbm, owner_ref),
         ],
         sems,
     )
-    for copy in copies[:3]:
+    for copy in copies:
         copy.wait()
     elements = prolong_ref.shape[0]
     odd_row = lax.rem(lax.axis_index("row"), 2)
@@ -72,14 +72,15 @@
             out_ref[pair] = jnp.concatenate(
                 [even[:, :LANES], odd[:, :LANES], tail], axis=0
             ).astype(jnp.bfloat16)
-    for copy in copies[3:]:
-        copy.wait()
-
-
-def left_kernel(lame_ref, owner_ref, stiffness_ref, prolong_ref, left_ref, place_ref, start_ref, filled):
+
+
+def left_kernel(
+    lame_ref, owner_ref, stiffness_hbm, prolong_ref, left_ref, place_ref, start_ref, stiffness_ref, filled, sems,
+):
     elements, slots, rows, _ = left_ref.shape
     coarse = rows // 2
     owners = filled.shape[0]
+    copies = fetch([(stiffness_hbm.at[s], stiffness_ref.at[s]) for s in range(slots)], sems)
     for t in range(owners):
         filled[t] = 0
     for e in range(elements):
@@ -96,6 +97,7 @@
 
     own = prolong_ref[...]
     for s in range(slots):
+        copies[s].wait()
         first = jnp.dot(own, stiffness_ref[s, 0], preferred_element_type=jnp.float32)
         second = jnp.dot(own, stiffness_ref[s, 1], preferred_element_type=jnp.float32)
         for e in range(elements):
@@ -105,7 +107,7 @@
             left_ref[e, s] = jnp.concatenate([high, total - high], axis=0).astype(jnp.bfloat16)
 
 
-def rows_kernel(columns_ref, place_ref, start_ref, prolong_ref, odd_ref, even_ref, left_ref, out_ref, table):
+def rows_kernel(columns_ref, place_ref, start_ref, prolong_ref, even_ref, odd_ref, left_ref, out_ref, table):
     elements, slots, rows, fine = left_ref.shape
     coarse = rows // 2
     ghosts = 2 * odd_ref.shape[0]
@@ -114,7 +116,7 @@
     owners = start_ref.shape[0] - 1
     for e in range(elements):
         table[e] = prolong_ref[e * coarse : (e + 1) * coarse].astype(jnp.float32)
-    for start, ref in ((elements + ghosts * odd_row, odd_ref), (elements + ghosts * (1 - odd_row), even_ref)):
+    for start, ref in ((elements + ghosts * (1 - odd_row), even_ref), (elements + ghosts * odd_row, odd_ref)):
         for pair in range(ghosts // 2):
             block = ref[pair].astype(jnp.float32)
             tail = block[2 * coarse :]
@@ -154,7 +156,7 @@
         out_ref[place_ref[e]] = jnp.concatenate([result[:, :LANES], tail], axis=0).astype(jnp.bfloat16)
 
 
-def unpack_kernel(elements, capacity, received_ref, rows_ref, ids_ref):
+def unpack_kernel(elements, capacity, received_ref, rows_hbm, ids_ref, rows_ref, sems):
     rest = rows_ref.shape[2] - LANES
     count = rows_ref.shape[0]
     owners = count // capacity
@@ -174,6 +176,7 @@
         begin = start_of(tail, me)
         end = jnp.where(me == owners - 1, elements, start_of(tail, jnp.minimum(me + 1, owners - 1)))
         bounds.append((begin, end - begin))
+    copies = []
     for i in range(count):
         source, slot = i // capacity, i % capacity
         begin, length = bounds[source]
@@ -189,10 +192,16 @@
         ).astype(jnp.bfloat16)
         here = jnp.logical_and(lane == i % LANES, slot < length)
         local[i // LANES] = jnp.where(here, tail[:, 127:128], local[i // LANES])
+        if slot == capacity - 1:
+            part = pl.ds(source * capacity, capacity)
+            copies.append(pltpu.make_async_copy(rows_ref.at[part], rows_hbm.at[part], sems.at[source]))
+            copies[-1].start()
     local = jnp.concatenate(local, axis=1)[0:1, :count].astype(jnp.int32)
     group = lax.broadcasted_iota(jnp.int32, (1, count), 1) // capacity
     first = (group * lax.axis_size("row") + lax.axis_index("row")) * elements
     ids_ref[...] = jnp.where(local >= 0, first + local, -1)
+    for copy in copies:
+        copy.wait()
 
 
 def on_device(stiffness, lame, prolong, columns, ghost_count, ghost_offset, owner_map):
@@ -202,7 +211,7 @@
     owners = lax.axis_size("grp")
     capacity = 2 * ((elements + owners - 1) // owners)
     run = pltpu.VMEM((ghosts // 2, 3 * coarse, LANES), jnp.bfloat16)
-    by_odd, by_even, own, lame_slots, by_slot, owner, tables = pl.pallas_call(
+    by_odd, by_even, own, lame_slots, by_slot, owner = pl.pallas_call(
         pack_kernel,
         out_shape=(
             run, run,
@@ -210,21 +219,20 @@
             pltpu.SMEM((slots, 2, elements), jnp.float32),
             pltpu.SMEM((slots, elements), jnp.int32),
             pltpu.SMEM((1, elements), jnp.int32),
-            pltpu.VMEM(stiffness.shape, jnp.bfloat16),
         ),
-        in_specs=[HBM] * 7, out_specs=(VMEM, VMEM, VMEM, SMEM, SMEM, SMEM, VMEM),
+        in_specs=[HBM] * 6, out_specs=(VMEM,) * 3 + (SMEM,) * 3,
         scratch_shapes=[
             pltpu.SMEM(ghost_count.shape, jnp.int32),
             pltpu.SMEM(ghost_offset.shape, jnp.int32),
-            pltpu.SemaphoreType.DMA((7,)),
+            pltpu.SemaphoreType.DMA((6,)),
         ],
         compiler_params=params(), name="pack",
     )(
-        in_hbm(ghost_count), in_hbm(ghost_offset), in_hbm(prolong), in_hbm(lame.transpose(1, 2, 0)),
-        in_hbm(columns.T), in_hbm(owner_map.T), in_hbm(stiffness),
-    )
+        in_hbm(ghost_count), in_hbm(ghost_offset), in_hbm(prolong),
+        in_hbm(lame.transpose(1, 2, 0)), in_hbm(columns.T), in_hbm(owner_map.T),
+    )
+    from_even = swapped(by_even, "row", 0)
     from_odd = swapped(by_odd, "row", 1)
-    from_even = swapped(by_even, "row", 0)
     own = in_vmem(own.reshape(elements * coarse, fine))
     left, place, start = pl.pallas_call(
         left_kernel,
@@ -233,10 +241,14 @@
             pltpu.SMEM((elements,), jnp.int32),
             pltpu.SMEM((owners + 1,), jnp.int32),
         ),
-        in_specs=[SMEM, SMEM, VMEM, VMEM], out_specs=(VMEM, SMEM, SMEM),
-        scratch_shapes=[pltpu.SMEM((owners,), jnp.int32)],
+        in_specs=[SMEM, SMEM, HBM, VMEM], out_specs=(VMEM, SMEM, SMEM),
+        scratch_shapes=[
+            pltpu.VMEM(stiffness.shape, jnp.bfloat16),
+            pltpu.SMEM((owners,), jnp.int32),
+            pltpu.SemaphoreType.DMA((slots,)),
+        ],
         compiler_params=params(), name="left",
-    )(in_smem(lame_slots), in_smem(owner), in_vmem(tables), own)
+    )(in_smem(lame_slots), in_smem(owner), in_hbm(stiffness), own)
     packed = pl.pallas_call(
         rows_kernel,
         out_shape=pltpu.VMEM((elements, 32, LANES), jnp.bfloat16),
@@ -245,7 +257,7 @@
         compiler_params=params(), name="rows",
     )(
         in_smem(by_slot), in_smem(place), in_smem(start), own,
-        in_vmem(from_odd), in_vmem(from_even), in_vmem(left),
+        in_vmem(from_even), in_vmem(from_odd), in_vmem(left),
     )
     received = lax.all_gather(packed, "grp", axis=0, tiled=True)
     coarse_rows, ids = pl.pallas_call(
@@ -254,7 +266,11 @@
             jax.ShapeDtypeStruct((owners * capacity, coarse, slots * coarse), jnp.bfloat16),
             jax.ShapeDtypeStruct((1, owners * capacity), jnp.int32),
         ),
-        in_specs=[VMEM], out_specs=(VMEM, VMEM),
+        in_specs=[VMEM], out_specs=(HBM, VMEM),
+        scratch_shapes=[
+            pltpu.VMEM((owners * capacity, coarse, slots * coarse), jnp.bfloat16),
+            pltpu.SemaphoreType.DMA((owners,)),
+        ],
         compiler_params=params(), name="unpack",
     )(in_vmem(received))
     return (coarse_rows, ids.reshape(-1))

time: 24.1 us -> 23.3 us (0.967)
  waiting for transfers between devices: 4.44 us -> 1.26 us
  Pallas kernels: 5.4 us -> 7.46 us
  blocking collectives: 8.94 us -> 10.6 us
  starting transfers between devices: 4.45 us -> 3.18 us
    ppermute x2, waiting for transfers between devices: 4.44 us -> 1.26 us  [swapped(): return lax.ppermute(value, axis, pairs + [(j, i) for i, j in pairs])]
    pallas_call x1, Pallas kernels: 1.24 us -> 3.19 us  [on_device(): pl.pallas_call(left_kernel, out_shape=(pltpu.VMEM((elements, slots, 2 * c...]
    all_gather x1, blocking collectives: 8.94 us -> 10.6 us  [on_device(): received = lax.all_gather(packed, 'grp', axis=0, tiled=True)]
    ppermute x2, starting transfers between devices: 4.45 us -> 3.18 us  [swapped(): return lax.ppermute(value, axis, pairs + [(j, i) for i, j in pairs])]
    pallas_call x1, Pallas kernels: 1.17 us -> 1.62 us  [on_device(): pl.pallas_call(functools.partial(unpack_kernel, elements, capacity), out_...]
    pallas_call x1, Pallas kernels: 1.51 us -> 1.18 us  [on_device(): pl.pallas_call(pack_kernel, out_shape=(run, run, pltpu.VMEM(prolong.shape...]
  transfers between devices with their start and end apart: 2 -> 2, of which waited for: 2 -> 1; matrix products, arithmetic and copies ran while one was open for 0% -> 0% of each run, Pallas kernels for 5% -> 14%
where the time goes in v5:
time: 23.3 us; the launch traced here: 23.1 us
  blocking collectives  10.6 us (45%)
  Pallas kernels  7.46 us (32%)
  starting transfers between devices  3.18 us (14%)
  waiting for transfers between devices  1.26 us (5%)
  between operations  0.67 us (3%)
    all_gather x1, blocking collectives, on_device(): received = lax.all_gather(packed, 'grp', axis=0, tiled=True)  10.6 us
    pallas_call x1, Pallas kernels, on_device(): pl.pallas_call(left_kernel, out_shape=(pltpu.VMEM((elements, slots, 2 * c...  3.19 us
    ppermute x2, starting transfers between devices, swapped(): return lax.ppermute(value, axis, pairs + [(j, i) for i, j in pairs])  3.18 us
    pallas_call x1, Pallas kernels, on_device(): pl.pallas_call(functools.partial(unpack_kernel, elements, capacity), out_...  1.62 us
    pallas_call x1, Pallas kernels, on_device(): pl.pallas_call(rows_kernel, out_shape=pltpu.VMEM((elements, 32, LANES), j...  1.49 us
    ppermute x2, waiting for transfers between devices, swapped(): return lax.ppermute(value, axis, pairs + [(j, i) for i, j in pairs])  1.26 us
    pallas_call x1, Pallas kernels, on_device(): pl.pallas_call(pack_kernel, out_shape=(run, run, pltpu.VMEM(prolong.shape...  1.18 us
  transfers between devices with their start and end apart: 2, of which 1 were waited for; matrix products, arithmetic and copies ran while one was open for 0% of the time, Pallas kernels for 14%

profile of v5, /device:TPU:9, one launch (start us, length us, event | category | flops | bytes accessed | tf_op | source)
XLA Modules:
  0.0 23.1 jit_solution(6355023470938939961)
XLA Ops:
  0.6 1.2 %pack.1 = (bf16[6,72,128]{2,1,0:T(8,128)(2,1)S(1)}, bf16[6,72,128]{2,1,0:T(8,128)(2,1)S(1)}, bf16[24,24,192]{2,1,0:T(8,128)(2,1)S(1)}, f32[7,2,24]{2,1,0:T(2,128...) custom-call(s32[1,2]{1,0:T(1,128)} %count_hbm.1, s32[1,2]{1,0:T(1,128)} %offset_hbm.1, bf16[24,24,192]{2,1,0:T(8,128)(2,1)} %prolong_hbm.1, ...), custom_call_target="tpu_custom_call" | custom-call | tf_op jit(solution)/shard_map/pack/pallas_call | solution.py:214
  1.8 1.3 %collective-permute-start = (bf16[6,72,128]{2,1,0:T(8,128)(2,1)S(1)}, bf16[6,72,128]{2,1,0:T(8,128)(2,1)S(1)}, u32[]{:S(2)}, u32[]{:S(2)}) collective-permute-start(bf16[6,72,128]{2,1,0:T(8,128)(2,1)S(1)} %get-tuple-element.19), channel_id=1, source_target_pairs={{0,1},{2,3},{4,5},{6,7},{1,0},{3,2},{5,4},{7,6},{8,9},{10,11},{12,... | collective-permute-start | bytes 331784 | tf_op jit(solution)/shard_map/ppermute | solution.py:35
  3.1 1.9 %collective-permute-start.1 = (bf16[6,72,128]{2,1,0:T(8,128)(2,1)S(1)}, bf16[6,72,128]{2,1,0:T(8,128)(2,1)S(1)}, u32[]{:S(2)}, u32[]{:S(2)}) collective-permute-start(bf16[6,72,128]{2,1,0:T(8,128)(2,1)S(1)} %get-tuple-element.20), channel_id=1, source_target_pairs={{1,2},{3,4},{5,6},{2,1},{4,3},{6,5},{9,10},{11,12},{13,14},{10,9},... | collective-permute-start | bytes 331784 | tf_op jit(solution)/shard_map/ppermute | solution.py:35
  5.0 3.2 %left.1 = (bf16[24,7,48,192]{3,2,1,0:T(8,128)(2,1)S(1)}, s32[24]{0:T(128)S(4)}, s32[5]{0:T(128)S(4)}) custom-call(f32[7,2,24]{2,1,0:T(2,128)S(4)} %get-tuple-element.14.lame_ref, s32[1,24]{1,0:T(1,128)S(4)} %get-tuple-element.15.owner_ref, bf16[7,2,192,192]{3,2,1,0:T(8,128)(2,1)} %stiffness_hbm.1, bf16[576,192]{1,0:T(8,128)(2,1)S(1)} %bitcast.5), custom_call_target="tpu_custom_call" | custom-call | tf_op jit(solution)/shard_map/left/pallas_call | solution.py:237
  8.2 0.0 collective-permute-done.even_ref
  8.2 1.3 %collective-permute-done.1.odd_ref = bf16[6,72,128]{2,1,0:T(8,128)(2,1)S(1)} collective-permute-done((bf16[6,72,128]{2,1,0:T(8,128)(2,1)S(1)}, bf16[6,72,128]{2,1,0:T(8,128)(2,1)S(1)}, u32[]{:S(2)}, u32[]{:S(2)}) %collective-permute-start.1) | collective-permute-done | bytes 110624 | tf_op jit(solution)/shard_map/ppermute | solution.py:35
  9.5 1.5 %rows.1 = bf16[24,32,128]{2,1,0:T(8,128)(2,1)S(1)} custom-call(s32[7,24]{1,0:T(8,128)S(4)} %get-tuple-element.13.columns_ref, s32[24]{0:T(128)S(4)} %get-tuple-element.17.place_ref, s32[5]{0:T(128)S(4)} %get-tuple-element.18.start_ref, bf16[576,192]{1,0:T(8,128)(2,1)S(1)} %bitcast.6, bf16[6,72,128]{2,1,0:T(8,128)(2,1)S(1)} %collective-permute-done.even_ref, ...), custom_call_target="tpu_custom_call" | custom-call | tf_op jit(solution)/shard_map/rows/pallas_call | solution.py:252
  11.0 10.6 %all_gather.3.received_ref = bf16[96,32,128]{2,1,0:T(8,128)(2,1)S(1)} all-gather(bf16[24,32,128]{2,1,0:T(8,128)(2,1)S(1)} %rows.1), channel_id=1, replica_groups=mesh['grp'=4,'row'=8] {'grp'}, dimensions={0}, use_global_device_ids=true | all-gather | bytes 983040 | tf_op jit(solution)/shard_map/all_gather | solution.py:262
  21.5 1.6 %unpack.1 = (bf16[48,24,168]{2,1,0:T(8,128)(2,1)}, s32[1,48]{1,0:T(1,128)}) custom-call(bf16[96,32,128]{2,1,0:T(8,128)(2,1)S(1)} %all_gather.3.received_ref), custom_call_target="tpu_custom_call" | custom-call | tf_op jit(solution)/shard_map/unpack/pallas_call | solution.py:263
Async XLA Ops:
  1.8 6.4 %collective-permute-start = (bf16[6,72,128]{2,1,0:T(8,128)(2,1)S(1)}, bf16[6,72,128]{2,1,0:T(8,128)(2,1)S(1)}, u32[]{:S(2)}, u32[]{:S(2)}) collective-permute-start(bf16[6,72,128]{2,1,0:T(8,128)(2,1)S(1)} %get-tuple-element.19), channel_id=1, source_target_pairs={{0,1},{2,3},{4,5},{6,7},{1,0},{3,2},{5,4},{7,6},{8,9},{10,11},{12,... | collective-permute-start | bytes 331784 | tf_op jit(solution)/shard_map/ppermute | solution.py:35
  3.1 6.4 %collective-permute-start.1 = (bf16[6,72,128]{2,1,0:T(8,128)(2,1)S(1)}, bf16[6,72,128]{2,1,0:T(8,128)(2,1)S(1)}, u32[]{:S(2)}, u32[]{:S(2)}) collective-permute-start(bf16[6,72,128]{2,1,0:T(8,128)(2,1)S(1)} %get-tuple-element.20), channel_id=1, source_target_pairs={{1,2},{3,4},{5,6},{2,1},{4,3},{6,5},{9,10},{11,12},{13,14},{10,9},... | collective-permute-start | bytes 331784 | tf_op jit(solution)/shard_map/ppermute | solution.py:35

commit v6 on v5

--- a/solution.py
+++ b/solution.py
@@ -75,29 +75,25 @@
 
 
 def left_kernel(
-    lame_ref, owner_ref, stiffness_hbm, prolong_ref, left_ref, place_ref, start_ref, stiffness_ref, filled, sems,
+    capacity, lame_ref, owner_ref, stiffness_hbm, prolong_ref, left_ref, order_ref, stiffness_ref, filled, sems,
 ):
     elements, slots, rows, _ = left_ref.shape
     coarse = rows // 2
-    owners = filled.shape[0]
-    copies = fetch([(stiffness_hbm.at[s], stiffness_ref.at[s]) for s in range(slots)], sems)
-    for t in range(owners):
+    copies = fetch([(stiffness_hbm, stiffness_ref)], sems)
+    me = lax.axis_index("grp")
+    for t in range(filled.shape[0]):
         filled[t] = 0
+    for i in range(order_ref.shape[0]):
+        order_ref[i] = elements
     for e in range(elements):
-        filled[owner_ref[0, e]] = filled[owner_ref[0, e]] + 1
-    total = jnp.int32(0)
-    for t in range(owners):
-        start_ref[t] = total
-        total = total + filled[t]
-        filled[t] = start_ref[t]
-    start_ref[owners] = total
-    for e in range(elements):
-        place_ref[e] = filled[owner_ref[0, e]]
-        filled[owner_ref[0, e]] = place_ref[e] + 1
-
+        away = lax.bitwise_xor(owner_ref[0, e], me)
+        position = filled[away]
+        filled[away] = position + 1
+        order_ref[away * capacity + position] = e
+
+    copies[0].wait()
     own = prolong_ref[...]
     for s in range(slots):
-        copies[s].wait()
         first = jnp.dot(own, stiffness_ref[s, 0], preferred_element_type=jnp.float32)
         second = jnp.dot(own, stiffness_ref[s, 1], preferred_element_type=jnp.float32)
         for e in range(elements):
@@ -107,13 +103,14 @@
             left_ref[e, s] = jnp.concatenate([high, total - high], axis=0).astype(jnp.bfloat16)
 
 
-def rows_kernel(columns_ref, place_ref, start_ref, prolong_ref, even_ref, odd_ref, left_ref, out_ref, table):
+def rows_kernel(columns_ref, order_ref, prolong_ref, even_ref, odd_ref, left_ref, *refs):
+    sends, (table, packed) = refs[:-2], refs[-2:]
     elements, slots, rows, fine = left_ref.shape
     coarse = rows // 2
     ghosts = 2 * odd_ref.shape[0]
     odd_row = lax.rem(lax.axis_index("row"), 2)
     half = fine - LANES
-    owners = start_ref.shape[0] - 1
+    capacity = sends[0].shape[0]
     for e in range(elements):
         table[e] = prolong_ref[e * coarse : (e + 1) * coarse].astype(jnp.float32)
     for start, ref in ((elements + ghosts * (1 - odd_row), even_ref), (elements + ghosts * odd_row, odd_ref)):
@@ -126,12 +123,10 @@
                 )
     table[elements + 2 * ghosts] = jnp.zeros((coarse, fine), jnp.float32)
 
-    row8 = lax.broadcasted_iota(jnp.int32, (8, 8), 0)
-    lane8 = lax.broadcasted_iota(jnp.int32, (8, 8), 1)
-    starts = jnp.zeros((8, 8), jnp.float32)
-    for t in range(owners):
-        here = jnp.logical_and(row8 == t % 8, lane8 == t // 8)
-        starts = jnp.where(here, start_ref[t].astype(jnp.float32), starts)
+    lane8 = lax.broadcasted_iota(jnp.int32, (8, LANES), 1)
+    packed[elements] = jnp.concatenate(
+        [jnp.zeros((coarse, LANES), jnp.float32), jnp.where(lane8 >= 120, -1.0, 0.0)], axis=0
+    ).astype(jnp.bfloat16)
 
     width = slots * coarse
     lane = lax.broadcasted_iota(jnp.int32, (coarse, width), 1)
@@ -151,57 +146,40 @@
             part = product[at : at + coarse] + product[at + coarse : at + 2 * coarse]
             result = part if s == 0 else jnp.where(lane >= s * coarse, part, result)
         rest = result[:, LANES:]
-        spare = jnp.where(lane8 >= 2, jnp.float32(e), starts)
+        spare = jnp.full((8, 8), e, jnp.float32)
         tail = jnp.concatenate([rest[0:8], rest[8:16], rest[16:24], spare], axis=1)
-        out_ref[place_ref[e]] = jnp.concatenate([result[:, :LANES], tail], axis=0).astype(jnp.bfloat16)
-
-
-def unpack_kernel(elements, capacity, received_ref, rows_hbm, ids_ref, rows_ref, sems):
+        packed[e] = jnp.concatenate([result[:, :LANES], tail], axis=0).astype(jnp.bfloat16)
+    for k, send in enumerate(sends):
+        for p in range(capacity):
+            send[p] = packed[order_ref[k * capacity + p]]
+
+
+def unpack_kernel(elements, away, *refs):
+    received, (rows_ref, ids_ref) = refs[:-2], refs[-2:]
+    capacity = received[0].shape[0]
     rest = rows_ref.shape[2] - LANES
     count = rows_ref.shape[0]
-    owners = count // capacity
+    wide = pl.cdiv(count, LANES) * LANES
     me = lax.axis_index("grp")
-    row = lax.broadcasted_iota(jnp.int32, (8, LANES), 0)
-    lane = lax.broadcasted_iota(jnp.int32, (8, LANES), 1)
-    wide = pl.cdiv(count, LANES)
-    local = [jnp.full((8, LANES), -1.0, jnp.float32) for _ in range(wide)]
-
-    def start_of(tail, t):
-        here = jnp.logical_and(row == t % 8, lane == 120 + t // 8)
-        return jnp.sum(jnp.where(here, tail, 0.0)).astype(jnp.int32)
-
-    bounds = []
-    for source in range(owners):
-        tail = received_ref[source * elements].astype(jnp.float32)[24:32]
-        begin = start_of(tail, me)
-        end = jnp.where(me == owners - 1, elements, start_of(tail, jnp.minimum(me + 1, owners - 1)))
-        bounds.append((begin, end - begin))
-    copies = []
-    for i in range(count):
-        source, slot = i // capacity, i % capacity
-        begin, length = bounds[source]
-        block = received_ref[source * elements + jnp.minimum(begin + slot, elements - 1)].astype(jnp.float32)
-        block = jnp.where(slot < length, block, 0.0)
-        tail = block[24:32]
-        rows_ref[i] = jnp.concatenate(
-            [
-                block[0:24],
-                jnp.concatenate([tail[:, rest * q : rest * (q + 1)] for q in range(3)], axis=0),
-            ],
-            axis=1,
-        ).astype(jnp.bfloat16)
-        here = jnp.logical_and(lane == i % LANES, slot < length)
-        local[i // LANES] = jnp.where(here, tail[:, 127:128], local[i // LANES])
-        if slot == capacity - 1:
-            part = pl.ds(source * capacity, capacity)
-            copies.append(pltpu.make_async_copy(rows_ref.at[part], rows_hbm.at[part], sems.at[source]))
-            copies[-1].start()
-    local = jnp.concatenate(local, axis=1)[0:1, :count].astype(jnp.int32)
+    lane = lax.broadcasted_iota(jnp.int32, (8, wide), 1)
+    local = jnp.full((8, wide), -1.0, jnp.float32)
+    for k, ref in zip(away, received):
+        first = lax.bitwise_xor(me, k) * capacity
+        for p in range(capacity):
+            block = ref[p].astype(jnp.float32)
+            tail = block[24:32]
+            rows_ref[first + p] = jnp.concatenate(
+                [
+                    block[0:24],
+                    jnp.concatenate([tail[:, rest * q : rest * (q + 1)] for q in range(3)], axis=0),
+                ],
+                axis=1,
+            ).astype(jnp.bfloat16)
+            local = jnp.where(lane == first + p, tail[:, 127:128], local)
+    local = local[0:1, :count].astype(jnp.int32)
     group = lax.broadcasted_iota(jnp.int32, (1, count), 1) // capacity
     first = (group * lax.axis_size("row") + lax.axis_index("row")) * elements
     ids_ref[...] = jnp.where(local >= 0, first + local, -1)
-    for copy in copies:
-        copy.wait()
 
 
 def on_device(stiffness, lame, prolong, columns, ghost_count, ghost_offset, owner_map):
@@ -234,45 +212,46 @@
     from_even = swapped(by_even, "row", 0)
     from_odd = swapped(by_odd, "row", 1)
     own = in_vmem(own.reshape(elements * coarse, fine))
-    left, place, start = pl.pallas_call(
-        left_kernel,
+    left, order = pl.pallas_call(
+        functools.partial(left_kernel, capacity),
         out_shape=(
             pltpu.VMEM((elements, slots, 2 * coarse, fine), jnp.bfloat16),
-            pltpu.SMEM((elements,), jnp.int32),
-            pltpu.SMEM((owners + 1,), jnp.int32),
+            pltpu.SMEM((owners * capacity,), jnp.int32),
         ),
-        in_specs=[SMEM, SMEM, HBM, VMEM], out_specs=(VMEM, SMEM, SMEM),
+        in_specs=[SMEM, SMEM, HBM, VMEM], out_specs=(VMEM, SMEM),
         scratch_shapes=[
             pltpu.VMEM(stiffness.shape, jnp.bfloat16),
             pltpu.SMEM((owners,), jnp.int32),
-            pltpu.SemaphoreType.DMA((slots,)),
+            pltpu.SemaphoreType.DMA((1,)),
         ],
         compiler_params=params(), name="left",
     )(in_smem(lame_slots), in_smem(owner), in_hbm(stiffness), own)
-    packed = pl.pallas_call(
+    sends = pl.pallas_call(
         rows_kernel,
-        out_shape=pltpu.VMEM((elements, 32, LANES), jnp.bfloat16),
-        in_specs=[SMEM, SMEM, SMEM, VMEM, VMEM, VMEM, VMEM], out_specs=VMEM,
-        scratch_shapes=[pltpu.VMEM((elements + 2 * ghosts + 1, coarse, fine), jnp.float32)],
+        out_shape=[pltpu.VMEM((capacity, 32, LANES), jnp.bfloat16)] * owners,
+        in_specs=[SMEM, SMEM, VMEM, VMEM, VMEM, VMEM], out_specs=[VMEM] * owners,
+        scratch_shapes=[
+            pltpu.VMEM((elements + 2 * ghosts + 1, coarse, fine), jnp.float32),
+            pltpu.VMEM((elements + 1, 32, LANES), jnp.bfloat16),
+        ],
         compiler_params=params(), name="rows",
     )(
-        in_smem(by_slot), in_smem(place), in_smem(start), own,
+        in_smem(by_slot), in_smem(order), own,
         in_vmem(from_even), in_vmem(from_odd), in_vmem(left),
     )
-    received = lax.all_gather(packed, "grp", axis=0, tiled=True)
+    arrival = [*range(2, owners), 1]
+    received = {0: sends[0]}
+    for k in arrival:
+        received[k] = lax.ppermute(sends[k], "grp", [(i, i ^ k) for i in range(owners)])
     coarse_rows, ids = pl.pallas_call(
-        functools.partial(unpack_kernel, elements, capacity),
+        functools.partial(unpack_kernel, elements, (*arrival, 0)),
         out_shape=(
             jax.ShapeDtypeStruct((owners * capacity, coarse, slots * coarse), jnp.bfloat16),
             jax.ShapeDtypeStruct((1, owners * capacity), jnp.int32),
         ),
-        in_specs=[VMEM], out_specs=(HBM, VMEM),
-        scratch_shapes=[
-            pltpu.VMEM((owners * capacity, coarse, slots * coarse), jnp.bfloat16),
-            pltpu.SemaphoreType.DMA((owners,)),
-        ],
+        in_specs=[VMEM] * owners, out_specs=(VMEM, VMEM),
         compiler_params=params(), name="unpack",
-    )(in_vmem(received))
+    )(*[in_vmem(received[k]) for k in (*arrival, 0)])
     return (coarse_rows, ids.reshape(-1))
 
 

time: 23.3 us -> 20.5 us (0.88)
  blocking collectives: 10.6 us -> 0 us
  waiting for transfers between devices: 1.26 us -> 6.43 us
  starting transfers between devices: 3.18 us -> 7 us
  Pallas kernels: 7.46 us -> 6.26 us
    all_gather x1 -> x0, blocking collectives: 10.6 us -> none  [on_device(): received = lax.all_gather(packed, 'grp', axis=0, tiled=True)]
    ppermute x0 -> x3, waiting for transfers between devices: none -> 4.57 us  [on_device(): lax.ppermute(sends[k], 'grp', [(i, i ^ k) for i in range(owners)])]
    ppermute x0 -> x3, starting transfers between devices: none -> 3.81 us  [on_device(): lax.ppermute(sends[k], 'grp', [(i, i ^ k) for i in range(owners)])]
    pallas_call x3, Pallas kernels: 6.29 us -> 5.08 us  [the longest x1 2.6 us: on_device(): pl.pallas_call(functools.partial(left_kernel, capacity), out_shape=(pltpu...]
    ppermute x2, waiting for transfers between devices: 1.26 us -> 1.85 us  [swapped(): return lax.ppermute(value, axis, pairs + [(j, i) for i, j in pairs])]
  transfers between devices with their start and end apart: 2 -> 5, of which waited for: 1 -> 2; matrix products, arithmetic and copies ran while one was open for 0% -> 0% of each run, Pallas kernels for 14% -> 13%
where the time goes in v6:
time: 20.5 us; the launch traced here: 20.4 us
  starting transfers between devices  7 us (34%)
  waiting for transfers between devices  6.43 us (31%)
  Pallas kernels  6.26 us (31%)
  between operations  0.68 us (3%)
    ppermute x3, waiting for transfers between devices, on_device(): lax.ppermute(sends[k], 'grp', [(i, i ^ k) for i in range(owners)])  4.57 us
    ppermute x3, starting transfers between devices, on_device(): lax.ppermute(sends[k], 'grp', [(i, i ^ k) for i in range(owners)])  3.81 us
    ppermute x2, starting transfers between devices, swapped(): return lax.ppermute(value, axis, pairs + [(j, i) for i, j in pairs])  3.18 us
    pallas_call x1, Pallas kernels, on_device(): pl.pallas_call(functools.partial(left_kernel, capacity), out_shape=(pltpu...  2.6 us
    ppermute x2, waiting for transfers between devices, swapped(): return lax.ppermute(value, axis, pairs + [(j, i) for i, j in pairs])  1.85 us
    pallas_call x1, Pallas kernels, on_device(): pl.pallas_call(rows_kernel, out_shape=[pltpu.VMEM((capacity, 32, LANES),...  1.51 us
    pallas_call x1, Pallas kernels, on_device(): pl.pallas_call(pack_kernel, out_shape=(run, run, pltpu.VMEM(prolong.shape...  1.18 us
    pallas_call x1, Pallas kernels, on_device(): pl.pallas_call(functools.partial(unpack_kernel, elements, (*arrival, 0)),...  0.97 us
  transfers between devices with their start and end apart: 5, of which 2 were waited for; matrix products, arithmetic and copies ran while one was open for 0% of the time, Pallas kernels for 13%

profile of v6, /device:TPU:9, one launch (start us, length us, event | category | flops | bytes accessed | tf_op | source)
XLA Modules:
  0.0 20.4 jit_solution(3970666389294434338)
XLA Ops:
  0.6 1.2 %pack.1 = (bf16[6,72,128]{2,1,0:T(8,128)(2,1)S(1)}, bf16[6,72,128]{2,1,0:T(8,128)(2,1)S(1)}, bf16[24,24,192]{2,1,0:T(8,128)(2,1)S(1)}, f32[7,2,24]{2,1,0:T(2,128...) custom-call(s32[1,2]{1,0:T(1,128)} %count_hbm.1, s32[1,2]{1,0:T(1,128)} %offset_hbm.1, bf16[24,24,192]{2,1,0:T(8,128)(2,1)} %prolong_hbm.1, ...), custom_call_target="tpu_custom_call" | custom-call | tf_op jit(solution)/shard_map/pack/pallas_call | solution.py:192
  1.8 1.3 %collective-permute-start = (bf16[6,72,128]{2,1,0:T(8,128)(2,1)S(1)}, bf16[6,72,128]{2,1,0:T(8,128)(2,1)S(1)}, u32[]{:S(2)}, u32[]{:S(2)}) collective-permute-start(bf16[6,72,128]{2,1,0:T(8,128)(2,1)S(1)} %get-tuple-element.21), channel_id=1, source_target_pairs={{0,1},{2,3},{4,5},{6,7},{1,0},{3,2},{5,4},{7,6},{8,9},{10,11},{12,... | collective-permute-start | bytes 331784 | tf_op jit(solution)/shard_map/ppermute | solution.py:35
  3.1 1.9 %collective-permute-start.1 = (bf16[6,72,128]{2,1,0:T(8,128)(2,1)S(1)}, bf16[6,72,128]{2,1,0:T(8,128)(2,1)S(1)}, u32[]{:S(2)}, u32[]{:S(2)}) collective-permute-start(bf16[6,72,128]{2,1,0:T(8,128)(2,1)S(1)} %get-tuple-element.22), channel_id=1, source_target_pairs={{1,2},{3,4},{5,6},{2,1},{4,3},{6,5},{9,10},{11,12},{13,14},{10,9},... | collective-permute-start | bytes 331784 | tf_op jit(solution)/shard_map/ppermute | solution.py:35
  5.0 2.6 %left.1 = (bf16[24,7,48,192]{3,2,1,0:T(8,128)(2,1)S(1)}, s32[48]{0:T(128)S(4)}) custom-call(f32[7,2,24]{2,1,0:T(2,128)S(4)} %get-tuple-element.17.lame_ref, s32[1,24]{1,0:T(1,128)S(4)} %get-tuple-element.18.owner_ref, bf16[7,2,192,192]{3,2,1,0:T(8,128)(2,1)} %stiffness_hbm.1, bf16[576,192]{1,0:T(8,128)(2,1)S(1)} %bitcast.5), custom_call_target="tpu_custom_call" | custom-call | tf_op jit(solution)/shard_map/left/pallas_call | solution.py:215
  7.6 0.0 collective-permute-done.even_ref
  7.6 1.8 %collective-permute-done.1.odd_ref = bf16[6,72,128]{2,1,0:T(8,128)(2,1)S(1)} collective-permute-done((bf16[6,72,128]{2,1,0:T(8,128)(2,1)S(1)}, bf16[6,72,128]{2,1,0:T(8,128)(2,1)S(1)}, u32[]{:S(2)}, u32[]{:S(2)}) %collective-permute-start.1) | collective-permute-done | bytes 110624 | tf_op jit(solution)/shard_map/ppermute | solution.py:35
  9.5 1.5 %rows.1 = (bf16[12,32,128]{2,1,0:T(8,128)(2,1)S(1)}, bf16[12,32,128]{2,1,0:T(8,128)(2,1)S(1)}, bf16[12,32,128]{2,1,0:T(8,128)(2,1)S(1)}, bf16[12,32,128]{2,1,0:T(8,128)(2,1)S(1)}) custom-call(s32[7,24]{1,0:T(8,128)S(4)} %get-tuple-element.16.columns_ref, s32[48]{0:T(128)S(4)} %get-tuple-element.20.order_ref, bf16[576,192]{1,0:T(8,128)(2,1)S(1)} %bitcast.6, ...), custom_call_target="tpu_custom_call" | custom-call | tf_op jit(solution)/shard_map/rows/pallas_call | solution.py:229
  11.0 1.3 %collective-permute-start.2 = (bf16[12,32,128]{2,1,0:T(8,128)(2,1)S(1)}, bf16[12,32,128]{2,1,0:T(8,128)(2,1)S(1)}, u32[]{:S(2)}, u32[]{:S(2)}) collective-permute-start(bf16[12,32,128]{2,1,0:T(8,128)(2,1)S(1)} %get-tuple-element.24), channel_id=1, source_target_pairs={{0,16},{8,24},{16,0},{24,8},{1,17},{9,25},{17,1},{25,9},{2,18},{10... | collective-permute-start | bytes 294920 | tf_op jit(solution)/shard_map/ppermute | solution.py:245
  12.3 2.5 %collective-permute-start.3 = (bf16[12,32,128]{2,1,0:T(8,128)(2,1)S(1)}, bf16[12,32,128]{2,1,0:T(8,128)(2,1)S(1)}, u32[]{:S(2)}, u32[]{:S(2)}) collective-permute-start(bf16[12,32,128]{2,1,0:T(8,128)(2,1)S(1)} %get-tuple-element.25), channel_id=1, source_target_pairs={{0,24},{8,16},{16,8},{24,0},{1,25},{9,17},{17,9},{25,1},{2,26},{10... | collective-permute-start | bytes 294920 | tf_op jit(solution)/shard_map/ppermute | solution.py:245
  14.8 0.0 collective-permute-start.4
  14.8 0.0 collective-permute-done.2.refs_0_
  14.8 4.6 %collective-permute-done.3.refs_1_ = bf16[12,32,128]{2,1,0:T(8,128)(2,1)S(1)} collective-permute-done((bf16[12,32,128]{2,1,0:T(8,128)(2,1)S(1)}, bf16[12,32,128]{2,1,0:T(8,128)(2,1)S(1)}, u32[]{:S(2)}, u32[]{:S(2)}) %collective-permute-start.3) | collective-permute-done | bytes 98336 | tf_op jit(solution)/shard_map/ppermute | solution.py:245
  19.4 0.0 collective-permute-done.4.refs_2_
  19.4 1.0 %unpack.1 = (bf16[48,24,168]{2,1,0:T(8,128)(2,1)}, s32[1,48]{1,0:T(1,128)}) custom-call(bf16[12,32,128]{2,1,0:T(8,128)(2,1)S(1)} %collective-permute-done.2.refs_0_, bf16[12,32,128]{2,1,0:T(8,128)(2,1)S(1)} %collective-permute-done.3.refs_1_, bf16[12,32,128]{2,1,0:T(8,128)(2,1)S(1)} %collective-permute-done.4.refs_2_, ...), custom_call_target="tpu_custom_call" | custom-call | tf_op jit(solution)/shard_map/unpack/pallas_call | solution.py:246
Async XLA Ops:
  1.8 5.8 %collective-permute-start = (bf16[6,72,128]{2,1,0:T(8,128)(2,1)S(1)}, bf16[6,72,128]{2,1,0:T(8,128)(2,1)S(1)}, u32[]{:S(2)}, u32[]{:S(2)}) collective-permute-start(bf16[6,72,128]{2,1,0:T(8,128)(2,1)S(1)} %get-tuple-element.21), channel_id=1, source_target_pairs={{0,1},{2,3},{4,5},{6,7},{1,0},{3,2},{5,4},{7,6},{8,9},{10,11},{12,... | collective-permute-start | bytes 331784 | tf_op jit(solution)/shard_map/ppermute | solution.py:35
  3.1 6.4 %collective-permute-start.1 = (bf16[6,72,128]{2,1,0:T(8,128)(2,1)S(1)}, bf16[6,72,128]{2,1,0:T(8,128)(2,1)S(1)}, u32[]{:S(2)}, u32[]{:S(2)}) collective-permute-start(bf16[6,72,128]{2,1,0:T(8,128)(2,1)S(1)} %get-tuple-element.22), channel_id=1, source_target_pairs={{1,2},{3,4},{5,6},{2,1},{4,3},{6,5},{9,10},{11,12},{13,14},{10,9},... | collective-permute-start | bytes 331784 | tf_op jit(solution)/shard_map/ppermute | solution.py:35
  11.0 3.8 %collective-permute-start.2 = (bf16[12,32,128]{2,1,0:T(8,128)(2,1)S(1)}, bf16[12,32,128]{2,1,0:T(8,128)(2,1)S(1)}, u32[]{:S(2)}, u32[]{:S(2)}) collective-permute-start(bf16[12,32,128]{2,1,0:T(8,128)(2,1)S(1)} %get-tuple-element.24), channel_id=1, source_target_pairs={{0,16},{8,24},{16,0},{24,8},{1,17},{9,25},{17,1},{25,9},{2,18},{10... | collective-permute-start | bytes 294920 | tf_op jit(solution)/shard_map/ppermute | solution.py:245
  12.3 7.1 %collective-permute-start.3 = (bf16[12,32,128]{2,1,0:T(8,128)(2,1)S(1)}, bf16[12,32,128]{2,1,0:T(8,128)(2,1)S(1)}, u32[]{:S(2)}, u32[]{:S(2)}) collective-permute-start(bf16[12,32,128]{2,1,0:T(8,128)(2,1)S(1)} %get-tuple-element.25), channel_id=1, source_target_pairs={{0,24},{8,16},{16,8},{24,0},{1,25},{9,17},{17,9},{25,1},{2,26},{10... | collective-permute-start | bytes 294920 | tf_op jit(solution)/shard_map/ppermute | solution.py:245
  14.8 4.6 %collective-permute-start.4 = (bf16[12,32,128]{2,1,0:T(8,128)(2,1)S(1)}, bf16[12,32,128]{2,1,0:T(8,128)(2,1)S(1)}, u32[]{:S(2)}, u32[]{:S(2)}) collective-permute-start(bf16[12,32,128]{2,1,0:T(8,128)(2,1)S(1)} %get-tuple-element.26), channel_id=1, source_target_pairs={{0,8},{8,0},{16,24},{24,16},{1,9},{9,1},{17,25},{25,17},{2,10},{10... | collective-permute-start | bytes 294920 | tf_op jit(solution)/shard_map/ppermute | solution.py:245

commit v7 on v6

--- a/solution.py
+++ b/solution.py
@@ -239,7 +239,7 @@
         in_smem(by_slot), in_smem(order), own,
         in_vmem(from_even), in_vmem(from_odd), in_vmem(left),
     )
-    arrival = [*range(2, owners), 1]
+    arrival = range(owners - 1, 0, -1)
     received = {0: sends[0]}
     for k in arrival:
         received[k] = lax.ppermute(sends[k], "grp", [(i, i ^ k) for i in range(owners)])

time: 20.5 us -> 21.1 us (1.029)
  waiting for transfers between devices: 6.43 us -> 6.95 us
    ppermute x3, waiting for transfers between devices: 4.57 us -> 5.1 us  [on_device(): lax.ppermute(sends[k], 'grp', [(i, i ^ k) for i in range(owners)])]
  transfers between devices with their start and end apart: 5 -> 5, of which waited for: 2 -> 3; matrix products, arithmetic and copies ran while one was open for 0% -> 0% of each run, Pallas kernels for 13% -> 12%
where the time goes in v7:
time: 21.1 us; the launch traced here: 20.9 us
  starting transfers between devices  6.96 us (33%)
  waiting for transfers between devices  6.95 us (33%)
  Pallas kernels  6.27 us (30%)
  between operations  0.68 us (3%)
    ppermute x3, waiting for transfers between devices, on_device(): lax.ppermute(sends[k], 'grp', [(i, i ^ k) for i in range(owners)])  5.1 us
    ppermute x3, starting transfers between devices, on_device(): lax.ppermute(sends[k], 'grp', [(i, i ^ k) for i in range(owners)])  3.78 us
    ppermute x2, starting transfers between devices, swapped(): return lax.ppermute(value, axis, pairs + [(j, i) for i, j in pairs])  3.18 us
    pallas_call x1, Pallas kernels, on_device(): pl.pallas_call(functools.partial(left_kernel, capacity), out_shape=(pltpu...  2.6 us
    ppermute x2, waiting for transfers between devices, swapped(): return lax.ppermute(value, axis, pairs + [(j, i) for i, j in pairs])  1.85 us
    pallas_call x1, Pallas kernels, on_device(): pl.pallas_call(rows_kernel, out_shape=[pltpu.VMEM((capacity, 32, LANES),...  1.53 us
    pallas_call x1, Pallas kernels, on_device(): pl.pallas_call(pack_kernel, out_shape=(run, run, pltpu.VMEM(prolong.shape...  1.18 us
    pallas_call x1, Pallas kernels, on_device(): pl.pallas_call(functools.partial(unpack_kernel, elements, (*arrival, 0)),...  0.97 us
  transfers between devices with their start and end apart: 5, of which 3 were waited for; matrix products, arithmetic and copies ran while one was open for 0% of the time, Pallas kernels for 12%

profile of v7, /device:TPU:9, one launch (start us, length us, event | category | flops | bytes accessed | tf_op | source)
XLA Modules:
  0.0 20.9 jit_solution(15062874256265104886)
XLA Ops:
  0.6 1.2 %pack.1 = (bf16[6,72,128]{2,1,0:T(8,128)(2,1)S(1)}, bf16[6,72,128]{2,1,0:T(8,128)(2,1)S(1)}, bf16[24,24,192]{2,1,0:T(8,128)(2,1)S(1)}, f32[7,2,24]{2,1,0:T(2,128...) custom-call(s32[1,2]{1,0:T(1,128)} %count_hbm.1, s32[1,2]{1,0:T(1,128)} %offset_hbm.1, bf16[24,24,192]{2,1,0:T(8,128)(2,1)} %prolong_hbm.1, ...), custom_call_target="tpu_custom_call" | custom-call | tf_op jit(solution)/shard_map/pack/pallas_call | solution.py:192
  1.8 1.3 %collective-permute-start = (bf16[6,72,128]{2,1,0:T(8,128)(2,1)S(1)}, bf16[6,72,128]{2,1,0:T(8,128)(2,1)S(1)}, u32[]{:S(2)}, u32[]{:S(2)}) collective-permute-start(bf16[6,72,128]{2,1,0:T(8,128)(2,1)S(1)} %get-tuple-element.21), channel_id=1, source_target_pairs={{0,1},{2,3},{4,5},{6,7},{1,0},{3,2},{5,4},{7,6},{8,9},{10,11},{12,... | collective-permute-start | bytes 331784 | tf_op jit(solution)/shard_map/ppermute | solution.py:35
  3.1 1.9 %collective-permute-start.1 = (bf16[6,72,128]{2,1,0:T(8,128)(2,1)S(1)}, bf16[6,72,128]{2,1,0:T(8,128)(2,1)S(1)}, u32[]{:S(2)}, u32[]{:S(2)}) collective-permute-start(bf16[6,72,128]{2,1,0:T(8,128)(2,1)S(1)} %get-tuple-element.22), channel_id=1, source_target_pairs={{1,2},{3,4},{5,6},{2,1},{4,3},{6,5},{9,10},{11,12},{13,14},{10,9},... | collective-permute-start | bytes 331784 | tf_op jit(solution)/shard_map/ppermute | solution.py:35
  5.0 2.6 %left.1 = (bf16[24,7,48,192]{3,2,1,0:T(8,128)(2,1)S(1)}, s32[48]{0:T(128)S(4)}) custom-call(f32[7,2,24]{2,1,0:T(2,128)S(4)} %get-tuple-element.17.lame_ref, s32[1,24]{1,0:T(1,128)S(4)} %get-tuple-element.18.owner_ref, bf16[7,2,192,192]{3,2,1,0:T(8,128)(2,1)} %stiffness_hbm.1, bf16[576,192]{1,0:T(8,128)(2,1)S(1)} %bitcast.5), custom_call_target="tpu_custom_call" | custom-call | tf_op jit(solution)/shard_map/left/pallas_call | solution.py:215
  7.6 0.0 collective-permute-done.even_ref
  7.6 1.8 %collective-permute-done.1.odd_ref = bf16[6,72,128]{2,1,0:T(8,128)(2,1)S(1)} collective-permute-done((bf16[6,72,128]{2,1,0:T(8,128)(2,1)S(1)}, bf16[6,72,128]{2,1,0:T(8,128)(2,1)S(1)}, u32[]{:S(2)}, u32[]{:S(2)}) %collective-permute-start.1) | collective-permute-done | bytes 110624 | tf_op jit(solution)/shard_map/ppermute | solution.py:35
  9.5 1.5 %rows.1 = (bf16[12,32,128]{2,1,0:T(8,128)(2,1)S(1)}, bf16[12,32,128]{2,1,0:T(8,128)(2,1)S(1)}, bf16[12,32,128]{2,1,0:T(8,128)(2,1)S(1)}, bf16[12,32,128]{2,1,0:T(8,128)(2,1)S(1)}) custom-call(s32[7,24]{1,0:T(8,128)S(4)} %get-tuple-element.16.columns_ref, s32[48]{0:T(128)S(4)} %get-tuple-element.20.order_ref, bf16[576,192]{1,0:T(8,128)(2,1)S(1)} %bitcast.6, ...), custom_call_target="tpu_custom_call" | custom-call | tf_op jit(solution)/shard_map/rows/pallas_call | solution.py:229
  11.0 3.3 %collective-permute-start.2 = (bf16[12,32,128]{2,1,0:T(8,128)(2,1)S(1)}, bf16[12,32,128]{2,1,0:T(8,128)(2,1)S(1)}, u32[]{:S(2)}, u32[]{:S(2)}) collective-permute-start(bf16[12,32,128]{2,1,0:T(8,128)(2,1)S(1)} %get-tuple-element.24), channel_id=1, source_target_pairs={{0,24},{8,16},{16,8},{24,0},{1,25},{9,17},{17,9},{25,1},{2,26},{10... | collective-permute-start | bytes 294920 | tf_op jit(solution)/shard_map/ppermute | solution.py:245
  14.3 0.2 %collective-permute-start.3 = (bf16[12,32,128]{2,1,0:T(8,128)(2,1)S(1)}, bf16[12,32,128]{2,1,0:T(8,128)(2,1)S(1)}, u32[]{:S(2)}, u32[]{:S(2)}) collective-permute-start(bf16[12,32,128]{2,1,0:T(8,128)(2,1)S(1)} %get-tuple-element.25), channel_id=1, source_target_pairs={{0,16},{8,24},{16,0},{24,8},{1,17},{9,25},{17,1},{25,9},{2,18},{10... | collective-permute-start | bytes 294920 | tf_op jit(solution)/shard_map/ppermute | solution.py:245
  14.5 0.3 %collective-permute-start.4 = (bf16[12,32,128]{2,1,0:T(8,128)(2,1)S(1)}, bf16[12,32,128]{2,1,0:T(8,128)(2,1)S(1)}, u32[]{:S(2)}, u32[]{:S(2)}) collective-permute-start(bf16[12,32,128]{2,1,0:T(8,128)(2,1)S(1)} %get-tuple-element.26), channel_id=1, source_target_pairs={{0,8},{8,0},{16,24},{24,16},{1,9},{9,1},{17,25},{25,17},{2,10},{10... | collective-permute-start | bytes 294920 | tf_op jit(solution)/shard_map/ppermute | solution.py:245
  14.8 3.0 %collective-permute-done.2.refs_0_ = bf16[12,32,128]{2,1,0:T(8,128)(2,1)S(1)} collective-permute-done((bf16[12,32,128]{2,1,0:T(8,128)(2,1)S(1)}, bf16[12,32,128]{2,1,0:T(8,128)(2,1)S(1)}, u32[]{:S(2)}, u32[]{:S(2)}) %collective-permute-start.2) | collective-permute-done | bytes 98336 | tf_op jit(solution)/shard_map/ppermute | solution.py:245
  17.8 2.1 %collective-permute-done.3.refs_1_ = bf16[12,32,128]{2,1,0:T(8,128)(2,1)S(1)} collective-permute-done((bf16[12,32,128]{2,1,0:T(8,128)(2,1)S(1)}, bf16[12,32,128]{2,1,0:T(8,128)(2,1)S(1)}, u32[]{:S(2)}, u32[]{:S(2)}) %collective-permute-start.3) | collective-permute-done | bytes 98336 | tf_op jit(solution)/shard_map/ppermute | solution.py:245
  19.9 0.0 collective-permute-done.4.refs_2_
  19.9 1.0 %unpack.1 = (bf16[48,24,168]{2,1,0:T(8,128)(2,1)}, s32[1,48]{1,0:T(1,128)}) custom-call(bf16[12,32,128]{2,1,0:T(8,128)(2,1)S(1)} %collective-permute-done.2.refs_0_, bf16[12,32,128]{2,1,0:T(8,128)(2,1)S(1)} %collective-permute-done.3.refs_1_, bf16[12,32,128]{2,1,0:T(8,128)(2,1)S(1)} %collective-permute-done.4.refs_2_, ...), custom_call_target="tpu_custom_call" | custom-call | tf_op jit(solution)/shard_map/unpack/pallas_call | solution.py:246
Async XLA Ops:
  1.8 5.8 %collective-permute-start = (bf16[6,72,128]{2,1,0:T(8,128)(2,1)S(1)}, bf16[6,72,128]{2,1,0:T(8,128)(2,1)S(1)}, u32[]{:S(2)}, u32[]{:S(2)}) collective-permute-start(bf16[6,72,128]{2,1,0:T(8,128)(2,1)S(1)} %get-tuple-element.21), channel_id=1, source_target_pairs={{0,1},{2,3},{4,5},{6,7},{1,0},{3,2},{5,4},{7,6},{8,9},{10,11},{12,... | collective-permute-start | bytes 331784 | tf_op jit(solution)/shard_map/ppermute | solution.py:35
  3.1 6.4 %collective-permute-start.1 = (bf16[6,72,128]{2,1,0:T(8,128)(2,1)S(1)}, bf16[6,72,128]{2,1,0:T(8,128)(2,1)S(1)}, u32[]{:S(2)}, u32[]{:S(2)}) collective-permute-start(bf16[6,72,128]{2,1,0:T(8,128)(2,1)S(1)} %get-tuple-element.22), channel_id=1, source_target_pairs={{1,2},{3,4},{5,6},{2,1},{4,3},{6,5},{9,10},{11,12},{13,14},{10,9},... | collective-permute-start | bytes 331784 | tf_op jit(solution)/shard_map/ppermute | solution.py:35
  11.0 6.8 %collective-permute-start.2 = (bf16[12,32,128]{2,1,0:T(8,128)(2,1)S(1)}, bf16[12,32,128]{2,1,0:T(8,128)(2,1)S(1)}, u32[]{:S(2)}, u32[]{:S(2)}) collective-permute-start(bf16[12,32,128]{2,1,0:T(8,128)(2,1)S(1)} %get-tuple-element.24), channel_id=1, source_target_pairs={{0,24},{8,16},{16,8},{24,0},{1,25},{9,17},{17,9},{25,1},{2,26},{10... | collective-permute-start | bytes 294920 | tf_op jit(solution)/shard_map/ppermute | solution.py:245
  14.3 5.6 %collective-permute-start.3 = (bf16[12,32,128]{2,1,0:T(8,128)(2,1)S(1)}, bf16[12,32,128]{2,1,0:T(8,128)(2,1)S(1)}, u32[]{:S(2)}, u32[]{:S(2)}) collective-permute-start(bf16[12,32,128]{2,1,0:T(8,128)(2,1)S(1)} %get-tuple-element.25), channel_id=1, source_target_pairs={{0,16},{8,24},{16,0},{24,8},{1,17},{9,25},{17,1},{25,9},{2,18},{10... | collective-permute-start | bytes 294920 | tf_op jit(solution)/shard_map/ppermute | solution.py:245
  14.5 5.4 %collective-permute-start.4 = (bf16[12,32,128]{2,1,0:T(8,128)(2,1)S(1)}, bf16[12,32,128]{2,1,0:T(8,128)(2,1)S(1)}, u32[]{:S(2)}, u32[]{:S(2)}) collective-permute-start(bf16[12,32,128]{2,1,0:T(8,128)(2,1)S(1)} %get-tuple-element.26), channel_id=1, source_target_pairs={{0,8},{8,0},{16,24},{24,16},{1,9},{9,1},{17,25},{25,17},{2,10},{10... | collective-permute-start | bytes 294920 | tf_op jit(solution)/shard_map/ppermute | solution.py:245

commit v8 on v7

--- a/solution.py
+++ b/solution.py
@@ -33,6 +33,13 @@
     peers = lax.axis_size(axis)
     pairs = [(i, i + 1) for i in range(parity, peers - 1, 2)]
     return lax.ppermute(value, axis, pairs + [(j, i) for i, j in pairs])
+
+
+def exchanges(owners):
+    same, cross = range(2, owners, 2), range(3, owners, 2)
+    return (
+        [(k, (1,)) for k in same] + [(k, (0, 1)) for k in cross] + [(k, (0,)) for k in same] + [(1, (0, 1))]
+    )
 
 
 def fetch(pairs, sems):
@@ -75,7 +82,8 @@
 
 
 def left_kernel(
-    capacity, lame_ref, owner_ref, stiffness_hbm, prolong_ref, left_ref, order_ref, stiffness_ref, filled, sems,
+    capacity, lame_ref, owner_ref, stiffness_hbm, prolong_ref, left_ref, order_ref, table_ref,
+    stiffness_ref, filled, sems,
 ):
     elements, slots, rows, _ = left_ref.shape
     coarse = rows // 2
@@ -91,6 +99,9 @@
         filled[away] = position + 1
         order_ref[away * capacity + position] = e
 
+    for e in range(elements):
+        table_ref[e] = prolong_ref[e * coarse : (e + 1) * coarse].astype(jnp.float32)
+    table_ref[table_ref.shape[0] - 1] = jnp.zeros(table_ref.shape[1:], jnp.float32)
     copies[0].wait()
     own = prolong_ref[...]
     for s in range(slots):
@@ -103,7 +114,7 @@
             left_ref[e, s] = jnp.concatenate([high, total - high], axis=0).astype(jnp.bfloat16)
 
 
-def rows_kernel(columns_ref, order_ref, prolong_ref, even_ref, odd_ref, left_ref, *refs):
+def rows_kernel(away, columns_ref, order_ref, even_ref, odd_ref, left_ref, _, *refs):
     sends, (table, packed) = refs[:-2], refs[-2:]
     elements, slots, rows, fine = left_ref.shape
     coarse = rows // 2
@@ -111,8 +122,6 @@
     odd_row = lax.rem(lax.axis_index("row"), 2)
     half = fine - LANES
     capacity = sends[0].shape[0]
-    for e in range(elements):
-        table[e] = prolong_ref[e * coarse : (e + 1) * coarse].astype(jnp.float32)
     for start, ref in ((elements + ghosts * (1 - odd_row), even_ref), (elements + ghosts * odd_row, odd_ref)):
         for pair in range(ghosts // 2):
             block = ref[pair].astype(jnp.float32)
@@ -121,7 +130,6 @@
                 table[start + 2 * pair + odd] = jnp.concatenate(
                     [block[odd * coarse : (odd + 1) * coarse], tail[:, odd * half : (odd + 1) * half]], axis=1
                 )
-    table[elements + 2 * ghosts] = jnp.zeros((coarse, fine), jnp.float32)
 
     lane8 = lax.broadcasted_iota(jnp.int32, (8, LANES), 1)
     packed[elements] = jnp.concatenate(
@@ -149,7 +157,7 @@
         spare = jnp.full((8, 8), e, jnp.float32)
         tail = jnp.concatenate([rest[0:8], rest[8:16], rest[16:24], spare], axis=1)
         packed[e] = jnp.concatenate([result[:, :LANES], tail], axis=0).astype(jnp.bfloat16)
-    for k, send in enumerate(sends):
+    for k, send in zip(away, sends):
         for p in range(capacity):
             send[p] = packed[order_ref[k * capacity + p]]
 
@@ -163,10 +171,10 @@
     me = lax.axis_index("grp")
     lane = lax.broadcasted_iota(jnp.int32, (8, wide), 1)
     local = jnp.full((8, wide), -1.0, jnp.float32)
-    for k, ref in zip(away, received):
+    for k in sorted(set(away)):
         first = lax.bitwise_xor(me, k) * capacity
         for p in range(capacity):
-            block = ref[p].astype(jnp.float32)
+            block = sum(ref[p].astype(jnp.float32) for way, ref in zip(away, received) if way == k)
             tail = block[24:32]
             rows_ref[first + p] = jnp.concatenate(
                 [
@@ -212,13 +220,15 @@
     from_even = swapped(by_even, "row", 0)
     from_odd = swapped(by_odd, "row", 1)
     own = in_vmem(own.reshape(elements * coarse, fine))
-    left, order = pl.pallas_call(
+    table = pltpu.VMEM((elements + 2 * ghosts + 1, coarse, fine), jnp.float32)
+    left, order, local = pl.pallas_call(
         functools.partial(left_kernel, capacity),
         out_shape=(
             pltpu.VMEM((elements, slots, 2 * coarse, fine), jnp.bfloat16),
             pltpu.SMEM((owners * capacity,), jnp.int32),
+            table,
         ),
-        in_specs=[SMEM, SMEM, HBM, VMEM], out_specs=(VMEM, SMEM),
+        in_specs=[SMEM, SMEM, HBM, VMEM], out_specs=(VMEM, SMEM, VMEM),
         scratch_shapes=[
             pltpu.VMEM(stiffness.shape, jnp.bfloat16),
             pltpu.SMEM((owners,), jnp.int32),
@@ -226,32 +236,32 @@
         ],
         compiler_params=params(), name="left",
     )(in_smem(lame_slots), in_smem(owner), in_hbm(stiffness), own)
-    sends = pl.pallas_call(
-        rows_kernel,
-        out_shape=[pltpu.VMEM((capacity, 32, LANES), jnp.bfloat16)] * owners,
-        in_specs=[SMEM, SMEM, VMEM, VMEM, VMEM, VMEM], out_specs=[VMEM] * owners,
-        scratch_shapes=[
-            pltpu.VMEM((elements + 2 * ghosts + 1, coarse, fine), jnp.float32),
-            pltpu.VMEM((elements + 1, 32, LANES), jnp.bfloat16),
-        ],
+    steps = exchanges(owners)
+    away = [k for k, _ in steps] + [0]
+    *sends, own_rows, _ = pl.pallas_call(
+        functools.partial(rows_kernel, away),
+        out_shape=[pltpu.VMEM((capacity, 32, LANES), jnp.bfloat16)] * len(away) + [table],
+        in_specs=[SMEM, SMEM, VMEM, VMEM, VMEM, VMEM], out_specs=[VMEM] * (len(away) + 1),
+        scratch_shapes=[pltpu.VMEM((elements + 1, 32, LANES), jnp.bfloat16)],
+        input_output_aliases={5: len(away)},
         compiler_params=params(), name="rows",
     )(
-        in_smem(by_slot), in_smem(order), own,
-        in_vmem(from_even), in_vmem(from_odd), in_vmem(left),
-    )
-    arrival = range(owners - 1, 0, -1)
-    received = {0: sends[0]}
-    for k in arrival:
-        received[k] = lax.ppermute(sends[k], "grp", [(i, i ^ k) for i in range(owners)])
+        in_smem(by_slot), in_smem(order),
+        in_vmem(from_even), in_vmem(from_odd), in_vmem(left), in_vmem(local),
+    )
+    received = [
+        lax.ppermute(send, "grp", [(i, i ^ k) for i in range(owners) if i % 2 in parities])
+        for send, (k, parities) in zip(sends, steps)
+    ]
     coarse_rows, ids = pl.pallas_call(
-        functools.partial(unpack_kernel, elements, (*arrival, 0)),
+        functools.partial(unpack_kernel, elements, away),
         out_shape=(
             jax.ShapeDtypeStruct((owners * capacity, coarse, slots * coarse), jnp.bfloat16),
             jax.ShapeDtypeStruct((1, owners * capacity), jnp.int32),
         ),
-        in_specs=[VMEM] * owners, out_specs=(VMEM, VMEM),
+        in_specs=[VMEM] * len(away), out_specs=(VMEM, VMEM),
         compiler_params=params(), name="unpack",
-    )(*[in_vmem(received[k]) for k in (*arrival, 0)])
+    )(*[in_vmem(value) for value in received], in_vmem(own_rows))
     return (coarse_rows, ids.reshape(-1))
 
 

time: 21.1 us -> 21.9 us (1.038)
  the two profiles are of different devices: /device:TPU:9 before, /device:TPU:8 now
where the time goes in v8:
time: 21.9 us; the launch traced here: 21.7 us
  starting transfers between devices  8.68 us (40%)
  Pallas kernels  6.29 us (29%)
  waiting for transfers between devices  5.99 us (27%)
  between operations  0.71 us (3%)
    ppermute x4, starting transfers between devices, on_device(): lax.ppermute(send, 'grp', [(i, i ^ k) for i in range(owners) if i % 2 in...  5.22 us
    ppermute x2, starting transfers between devices, swapped(): return lax.ppermute(value, axis, pairs + [(j, i) for i, j in pairs])  3.46 us
    ppermute x2, waiting for transfers between devices, swapped(): return lax.ppermute(value, axis, pairs + [(j, i) for i, j in pairs])  3 us
    ppermute x4, waiting for transfers between devices, on_device(): lax.ppermute(send, 'grp', [(i, i ^ k) for i in range(owners) if i % 2 in...  2.99 us
    pallas_call x1, Pallas kernels, on_device(): pl.pallas_call(functools.partial(left_kernel, capacity), out_shape=(pltpu...  2.6 us
    pallas_call x1, Pallas kernels, on_device(): pl.pallas_call(functools.partial(rows_kernel, away), out_shape=[pltpu.VME...  1.54 us
    pallas_call x1, Pallas kernels, on_device(): pl.pallas_call(pack_kernel, out_shape=(run, run, pltpu.VMEM(prolong.shape...  1.18 us
    pallas_call x1, Pallas kernels, on_device(): pl.pallas_call(functools.partial(unpack_kernel, elements, away), out_shap...  0.98 us
  transfers between devices with their start and end apart: 6, of which 2 were waited for; matrix products, arithmetic and copies ran while one was open for 0% of the time, Pallas kernels for 12%

profile of v8, /device:TPU:8, one launch (start us, length us, event | category | flops | bytes accessed | tf_op | source)
XLA Modules:
  0.0 21.7 jit_solution(12200979300309171862)
XLA Ops:
  0.6 1.2 %pack.1 = (bf16[6,72,128]{2,1,0:T(8,128)(2,1)S(1)}, bf16[6,72,128]{2,1,0:T(8,128)(2,1)S(1)}, bf16[24,24,192]{2,1,0:T(8,128)(2,1)S(1)}, f32[7,2,24]{2,1,0:T(2,128...) custom-call(s32[1,2]{1,0:T(1,128)} %count_hbm.1, s32[1,2]{1,0:T(1,128)} %offset_hbm.1, bf16[24,24,192]{2,1,0:T(8,128)(2,1)} %prolong_hbm.1, ...), custom_call_target="tpu_custom_call" | custom-call | tf_op jit(solution)/shard_map/pack/pallas_call | solution.py:200
  1.8 1.6 %collective-permute-start = (bf16[6,72,128]{2,1,0:T(8,128)(2,1)S(1)}, bf16[6,72,128]{2,1,0:T(8,128)(2,1)S(1)}, u32[]{:S(2)}, u32[]{:S(2)}) collective-permute-start(bf16[6,72,128]{2,1,0:T(8,128)(2,1)S(1)} %get-tuple-element.23), channel_id=1, source_target_pairs={{0,1},{2,3},{4,5},{6,7},{1,0},{3,2},{5,4},{7,6},{8,9},{10,11},{12,... | collective-permute-start | bytes 331784 | tf_op jit(solution)/shard_map/ppermute | solution.py:35
  3.4 1.9 %collective-permute-start.1 = (bf16[6,72,128]{2,1,0:T(8,128)(2,1)S(1)}, bf16[6,72,128]{2,1,0:T(8,128)(2,1)S(1)}, u32[]{:S(2)}, u32[]{:S(2)}) collective-permute-start(bf16[6,72,128]{2,1,0:T(8,128)(2,1)S(1)} %get-tuple-element.24), channel_id=1, source_target_pairs={{1,2},{3,4},{5,6},{2,1},{4,3},{6,5},{9,10},{11,12},{13,14},{10,9},... | collective-permute-start | bytes 331784 | tf_op jit(solution)/shard_map/ppermute | solution.py:35
  5.3 2.6 %left.1 = (bf16[24,7,48,192]{3,2,1,0:T(8,128)(2,1)S(1)}, s32[48]{0:T(128)S(4)}, f32[49,24,192]{2,1,0:T(8,128)S(1)}) custom-call(f32[7,2,24]{2,1,0:T(2,128)S(4)} %get-tuple-element.19.lame_ref, s32[1,24]{1,0:T(1,128)S(4)} %get-tuple-element.20.owner_ref, bf16[7,2,192,192]{3,2,1,0:T(8,128)(2,1)} %stiffness_hbm.1, bf16[576,192]{1,0:T(8,128)(2,1)S(1)} %bitcast.5), custom_call_target="tpu_custom_call" | custom-call | tf_op jit(solution)/shard_map/left/pallas_call | solution.py:224
  7.9 0.0 collective-permute-done.even_ref
  7.9 3.0 %collective-permute-done.1.odd_ref = bf16[6,72,128]{2,1,0:T(8,128)(2,1)S(1)} collective-permute-done((bf16[6,72,128]{2,1,0:T(8,128)(2,1)S(1)}, bf16[6,72,128]{2,1,0:T(8,128)(2,1)S(1)}, u32[]{:S(2)}, u32[]{:S(2)}) %collective-permute-start.1) | collective-permute-done | bytes 110624 | tf_op jit(solution)/shard_map/ppermute | solution.py:35
  10.9 1.5 %rows.1 = (bf16[12,32,128]{2,1,0:T(8,128)(2,1)S(1)}, bf16[12,32,128]{2,1,0:T(8,128)(2,1)S(1)}, bf16[12,32,128]{2,1,0:T(8,128)(2,1)S(1)}, bf16[12,32,128]{2,1,0:T...) custom-call(s32[7,24]{1,0:T(8,128)S(4)} %get-tuple-element.18.column, ...), custom_call_target="tpu_custom_call", output_to_operand_aliasing={{5}: (5, {})} | custom-call | tf_op jit(solution)/shard_map/rows/pallas_call | solution.py:241
  12.5 0.7 %collective-permute-start.2 = (bf16[12,32,128]{2,1,0:T(8,128)(2,1)S(1)}, bf16[12,32,128]{2,1,0:T(8,128)(2,1)S(1)}, u32[]{:S(2)}, u32[]{:S(2)}) collective-permute-start(bf16[12,32,128]{2,1,0:T(8,128)(2,1)S(1)} %get-tuple-element.27), channel_id=1, source_target_pairs={{8,24},{24,8},{9,25},{25,9},{10,26},{26,10},{11,27},{27,11},{12,28... | collective-permute-start | bytes 294920 | tf_op jit(solution)/shard_map/ppermute | solution.py:253
  13.1 1.1 %collective-permute-start.3 = (bf16[12,32,128]{2,1,0:T(8,128)(2,1)S(1)}, bf16[12,32,128]{2,1,0:T(8,128)(2,1)S(1)}, u32[]{:S(2)}, u32[]{:S(2)}) collective-permute-start(bf16[12,32,128]{2,1,0:T(8,128)(2,1)S(1)} %get-tuple-element.28), channel_id=1, source_target_pairs={{0,24},{8,16},{16,8},{24,0},{1,25},{9,17},{17,9},{25,1},{2,26},{10... | collective-permute-start | bytes 294920 | tf_op jit(solution)/shard_map/ppermute | solution.py:253
  14.2 3.4 %collective-permute-start.4 = (bf16[12,32,128]{2,1,0:T(8,128)(2,1)S(1)}, bf16[12,32,128]{2,1,0:T(8,128)(2,1)S(1)}, u32[]{:S(2)}, u32[]{:S(2)}) collective-permute-start(bf16[12,32,128]{2,1,0:T(8,128)(2,1)S(1)} %get-tuple-element.29), channel_id=1, source_target_pairs={{0,16},{16,0},{1,17},{17,1},{2,18},{18,2},{3,19},{19,3},{4,20},{20... | collective-permute-start | bytes 294920 | tf_op jit(solution)/shard_map/ppermute | solution.py:253
  17.6 0.1 collective-permute-start.5
  17.7 0.0 collective-permute-done.2.refs_0_
  17.7 0.0 collective-permute-done.3.refs_1_
  17.7 3.0 %collective-permute-done.4.refs_2_ = bf16[12,32,128]{2,1,0:T(8,128)(2,1)S(1)} collective-permute-done((bf16[12,32,128]{2,1,0:T(8,128)(2,1)S(1)}, bf16[12,32,128]{2,1,0:T(8,128)(2,1)S(1)}, u32[]{:S(2)}, u32[]{:S(2)}) %collective-permute-start.4) | collective-permute-done | bytes 98336 | tf_op jit(solution)/shard_map/ppermute | solution.py:253
  20.7 0.0 collective-permute-done.5.refs_3_
  20.7 1.0 %unpack.1 = (bf16[48,24,168]{2,1,0:T(8,128)(2,1)}, s32[1,48]{1,0:T(1,128)}) custom-call(bf16[12,32,128]{2,1,0:T(8,128)(2,1)S(1)} %collective-permute-done.2.refs_0_, bf16[12,32,128]{2,1,0:T(8,128)(2,1)S(1)} %collective-permute-done.3.refs_1_, bf16[12,32,128]{2,1,0:T(8,128)(2,1)S(1)} %collective-permute-done.4.refs_2_, ...), custom_call_target="tpu_custom_call" | custom-call | tf_op jit(solution)/shard_map/unpack/pallas_call | solution.py:256
Async XLA Ops:
  1.8 6.1 %collective-permute-start = (bf16[6,72,128]{2,1,0:T(8,128)(2,1)S(1)}, bf16[6,72,128]{2,1,0:T(8,128)(2,1)S(1)}, u32[]{:S(2)}, u32[]{:S(2)}) collective-permute-start(bf16[6,72,128]{2,1,0:T(8,128)(2,1)S(1)} %get-tuple-element.23), channel_id=1, source_target_pairs={{0,1},{2,3},{4,5},{6,7},{1,0},{3,2},{5,4},{7,6},{8,9},{10,11},{12,... | collective-permute-start | bytes 331784 | tf_op jit(solution)/shard_map/ppermute | solution.py:35
  3.4 7.5 %collective-permute-start.1 = (bf16[6,72,128]{2,1,0:T(8,128)(2,1)S(1)}, bf16[6,72,128]{2,1,0:T(8,128)(2,1)S(1)}, u32[]{:S(2)}, u32[]{:S(2)}) collective-permute-start(bf16[6,72,128]{2,1,0:T(8,128)(2,1)S(1)} %get-tuple-element.24), channel_id=1, source_target_pairs={{1,2},{3,4},{5,6},{2,1},{4,3},{6,5},{9,10},{11,12},{13,14},{10,9},... | collective-permute-start | bytes 331784 | tf_op jit(solution)/shard_map/ppermute | solution.py:35
  12.5 5.2 %collective-permute-start.2 = (bf16[12,32,128]{2,1,0:T(8,128)(2,1)S(1)}, bf16[12,32,128]{2,1,0:T(8,128)(2,1)S(1)}, u32[]{:S(2)}, u32[]{:S(2)}) collective-permute-start(bf16[12,32,128]{2,1,0:T(8,128)(2,1)S(1)} %get-tuple-element.27), channel_id=1, source_target_pairs={{8,24},{24,8},{9,25},{25,9},{10,26},{26,10},{11,27},{27,11},{12,28... | collective-permute-start | bytes 294920 | tf_op jit(solution)/shard_map/ppermute | solution.py:253
  13.1 4.6 %collective-permute-start.3 = (bf16[12,32,128]{2,1,0:T(8,128)(2,1)S(1)}, bf16[12,32,128]{2,1,0:T(8,128)(2,1)S(1)}, u32[]{:S(2)}, u32[]{:S(2)}) collective-permute-start(bf16[12,32,128]{2,1,0:T(8,128)(2,1)S(1)} %get-tuple-element.28), channel_id=1, source_target_pairs={{0,24},{8,16},{16,8},{24,0},{1,25},{9,17},{17,9},{25,1},{2,26},{10... | collective-permute-start | bytes 294920 | tf_op jit(solution)/shard_map/ppermute | solution.py:253
  14.2 6.5 %collective-permute-start.4 = (bf16[12,32,128]{2,1,0:T(8,128)(2,1)S(1)}, bf16[12,32,128]{2,1,0:T(8,128)(2,1)S(1)}, u32[]{:S(2)}, u32[]{:S(2)}) collective-permute-start(bf16[12,32,128]{2,1,0:T(8,128)(2,1)S(1)} %get-tuple-element.29), channel_id=1, source_target_pairs={{0,16},{16,0},{1,17},{17,1},{2,18},{18,2},{3,19},{19,3},{4,20},{20... | collective-permute-start | bytes 294920 | tf_op jit(solution)/shard_map/ppermute | solution.py:253
  17.6 3.1 %collective-permute-start.5 = (bf16[12,32,128]{2,1,0:T(8,128)(2,1)S(1)}, bf16[12,32,128]{2,1,0:T(8,128)(2,1)S(1)}, u32[]{:S(2)}, u32[]{:S(2)}) collective-permute-start(bf16[12,32,128]{2,1,0:T(8,128)(2,1)S(1)} %get-tuple-element.30), channel_id=1, source_target_pairs={{0,8},{8,0},{16,24},{24,16},{1,9},{9,1},{17,25},{25,17},{2,10},{10... | collective-permute-start | bytes 294920 | tf_op jit(solution)/shard_map/ppermute | solution.py:253

commit v9 on v6

--- a/solution.py
+++ b/solution.py
@@ -32,7 +32,8 @@
 def swapped(value, axis, parity):
     peers = lax.axis_size(axis)
     pairs = [(i, i + 1) for i in range(parity, peers - 1, 2)]
-    return lax.ppermute(value, axis, pairs + [(j, i) for i, j in pairs])
+    alone = set(range(peers)) - {i for pair in pairs for i in pair}
+    return lax.ppermute(value, axis, pairs + [(j, i) for i, j in pairs] + [(i, i) for i in sorted(alone)])
 
 
 def fetch(pairs, sems):
@@ -108,14 +109,17 @@
     elements, slots, rows, fine = left_ref.shape
     coarse = rows // 2
     ghosts = 2 * odd_ref.shape[0]
-    odd_row = lax.rem(lax.axis_index("row"), 2)
+    row, last = lax.axis_index("row"), lax.axis_size("row") - 1
     half = fine - LANES
     capacity = sends[0].shape[0]
     for e in range(elements):
         table[e] = prolong_ref[e * coarse : (e + 1) * coarse].astype(jnp.float32)
-    for start, ref in ((elements + ghosts * (1 - odd_row), even_ref), (elements + ghosts * odd_row, odd_ref)):
+    for parity, ref in enumerate((even_ref, odd_ref)):
+        from_above = lax.rem(row, 2) == parity
+        start = jnp.where(from_above, elements + ghosts, elements)
+        has_partner = jnp.where(from_above, row < last, row > 0)
         for pair in range(ghosts // 2):
-            block = ref[pair].astype(jnp.float32)
+            block = jnp.where(has_partner, ref[pair].astype(jnp.float32), 0.0)
             tail = block[2 * coarse :]
             for odd in range(2):
                 table[start + 2 * pair + odd] = jnp.concatenate(

time: 20.5 us -> 20.5 us (level)
  no operation moved by 1% of the time
where the time goes in v9:
time: 20.5 us; the launch traced here: 20.4 us
  starting transfers between devices  6.97 us (34%)
  waiting for transfers between devices  6.43 us (31%)
  Pallas kernels  6.27 us (31%)
  between operations  0.68 us (3%)
    ppermute x3, waiting for transfers between devices, on_device(): lax.ppermute(sends[k], 'grp', [(i, i ^ k) for i in range(owners)])  4.58 us
    ppermute x3, starting transfers between devices, on_device(): lax.ppermute(sends[k], 'grp', [(i, i ^ k) for i in range(owners)])  3.79 us
    ppermute x2, starting transfers between devices, swapped(): lax.ppermute(value, axis, pairs + [(j, i) for i, j in pairs] + [(i, i) fo...  3.18 us
    pallas_call x1, Pallas kernels, on_device(): pl.pallas_call(functools.partial(left_kernel, capacity), out_shape=(pltpu...  2.6 us
    ppermute x2, waiting for transfers between devices, swapped(): lax.ppermute(value, axis, pairs + [(j, i) for i, j in pairs] + [(i, i) fo...  1.85 us
    pallas_call x1, Pallas kernels, on_device(): pl.pallas_call(rows_kernel, out_shape=[pltpu.VMEM((capacity, 32, LANES),...  1.53 us
    pallas_call x1, Pallas kernels, on_device(): pl.pallas_call(pack_kernel, out_shape=(run, run, pltpu.VMEM(prolong.shape...  1.18 us
    pallas_call x1, Pallas kernels, on_device(): pl.pallas_call(functools.partial(unpack_kernel, elements, (*arrival, 0)),...  0.97 us
  transfers between devices with their start and end apart: 5, of which 2 were waited for; matrix products, arithmetic and copies ran while one was open for 0% of the time, Pallas kernels for 13%

profile of v9, /device:TPU:9, one launch (start us, length us, event | category | flops | bytes accessed | tf_op | source)
XLA Modules:
  0.0 20.4 jit_solution(9081886115823980400)
XLA Ops:
  0.6 1.2 %pack.1 = (bf16[6,72,128]{2,1,0:T(8,128)(2,1)S(1)}, bf16[6,72,128]{2,1,0:T(8,128)(2,1)S(1)}, bf16[24,24,192]{2,1,0:T(8,128)(2,1)S(1)}, f32[7,2,24]{2,1,0:T(2,128...) custom-call(s32[1,2]{1,0:T(1,128)} %count_hbm.1, s32[1,2]{1,0:T(1,128)} %offset_hbm.1, bf16[24,24,192]{2,1,0:T(8,128)(2,1)} %prolong_hbm.1, ...), custom_call_target="tpu_custom_call" | custom-call | tf_op jit(solution)/shard_map/pack/pallas_call | solution.py:196
  1.8 1.3 %collective-permute-start = (bf16[6,72,128]{2,1,0:T(8,128)(2,1)S(1)}, bf16[6,72,128]{2,1,0:T(8,128)(2,1)S(1)}, u32[]{:S(2)}, u32[]{:S(2)}) collective-permute-start(bf16[6,72,128]{2,1,0:T(8,128)(2,1)S(1)} %get-tuple-element.21), channel_id=1, source_target_pairs={{0,1},{2,3},{4,5},{6,7},{1,0},{3,2},{5,4},{7,6},{8,9},{10,11},{12,... | collective-permute-start | bytes 331784 | tf_op jit(solution)/shard_map/ppermute | solution.py:36
  3.1 1.9 %collective-permute-start.1 = (bf16[6,72,128]{2,1,0:T(8,128)(2,1)S(1)}, bf16[6,72,128]{2,1,0:T(8,128)(2,1)S(1)}, u32[]{:S(2)}, u32[]{:S(2)}) collective-permute-start(bf16[6,72,128]{2,1,0:T(8,128)(2,1)S(1)} %get-tuple-element.22), channel_id=1, source_target_pairs={{1,2},{3,4},{5,6},{2,1},{4,3},{6,5},{0,0},{7,7},{9,10},{11,12},{13... | collective-permute-start | bytes 331784 | tf_op jit(solution)/shard_map/ppermute | solution.py:36
  5.0 2.6 %left.1 = (bf16[24,7,48,192]{3,2,1,0:T(8,128)(2,1)S(1)}, s32[48]{0:T(128)S(4)}) custom-call(f32[7,2,24]{2,1,0:T(2,128)S(4)} %get-tuple-element.17.lame_ref, s32[1,24]{1,0:T(1,128)S(4)} %get-tuple-element.18.owner_ref, bf16[7,2,192,192]{3,2,1,0:T(8,128)(2,1)} %stiffness_hbm.1, bf16[576,192]{1,0:T(8,128)(2,1)S(1)} %bitcast.5), custom_call_target="tpu_custom_call" | custom-call | tf_op jit(solution)/shard_map/left/pallas_call | solution.py:219
  7.6 0.0 collective-permute-done.even_ref
  7.6 1.8 %collective-permute-done.1.odd_ref = bf16[6,72,128]{2,1,0:T(8,128)(2,1)S(1)} collective-permute-done((bf16[6,72,128]{2,1,0:T(8,128)(2,1)S(1)}, bf16[6,72,128]{2,1,0:T(8,128)(2,1)S(1)}, u32[]{:S(2)}, u32[]{:S(2)}) %collective-permute-start.1) | collective-permute-done | bytes 110624 | tf_op jit(solution)/shard_map/ppermute | solution.py:36
  9.5 1.5 %rows.1 = (bf16[12,32,128]{2,1,0:T(8,128)(2,1)S(1)}, bf16[12,32,128]{2,1,0:T(8,128)(2,1)S(1)}, bf16[12,32,128]{2,1,0:T(8,128)(2,1)S(1)}, bf16[12,32,128]{2,1,0:T(8,128)(2,1)S(1)}) custom-call(s32[7,24]{1,0:T(8,128)S(4)} %get-tuple-element.16.columns_ref, s32[48]{0:T(128)S(4)} %get-tuple-element.20.order_ref, bf16[576,192]{1,0:T(8,128)(2,1)S(1)} %bitcast.6, ...), custom_call_target="tpu_custom_call" | custom-call | tf_op jit(solution)/shard_map/rows/pallas_call | solution.py:233
  11.0 1.3 %collective-permute-start.2 = (bf16[12,32,128]{2,1,0:T(8,128)(2,1)S(1)}, bf16[12,32,128]{2,1,0:T(8,128)(2,1)S(1)}, u32[]{:S(2)}, u32[]{:S(2)}) collective-permute-start(bf16[12,32,128]{2,1,0:T(8,128)(2,1)S(1)} %get-tuple-element.24), channel_id=1, source_target_pairs={{0,16},{8,24},{16,0},{24,8},{1,17},{9,25},{17,1},{25,9},{2,18},{10... | collective-permute-start | bytes 294920 | tf_op jit(solution)/shard_map/ppermute | solution.py:249
  12.3 2.5 %collective-permute-start.3 = (bf16[12,32,128]{2,1,0:T(8,128)(2,1)S(1)}, bf16[12,32,128]{2,1,0:T(8,128)(2,1)S(1)}, u32[]{:S(2)}, u32[]{:S(2)}) collective-permute-start(bf16[12,32,128]{2,1,0:T(8,128)(2,1)S(1)} %get-tuple-element.25), channel_id=1, source_target_pairs={{0,24},{8,16},{16,8},{24,0},{1,25},{9,17},{17,9},{25,1},{2,26},{10... | collective-permute-start | bytes 294920 | tf_op jit(solution)/shard_map/ppermute | solution.py:249
  14.8 0.0 collective-permute-start.4
  14.8 0.0 collective-permute-done.2.refs_0_
  14.8 4.6 %collective-permute-done.3.refs_1_ = bf16[12,32,128]{2,1,0:T(8,128)(2,1)S(1)} collective-permute-done((bf16[12,32,128]{2,1,0:T(8,128)(2,1)S(1)}, bf16[12,32,128]{2,1,0:T(8,128)(2,1)S(1)}, u32[]{:S(2)}, u32[]{:S(2)}) %collective-permute-start.3) | collective-permute-done | bytes 98336 | tf_op jit(solution)/shard_map/ppermute | solution.py:249
  19.4 0.0 collective-permute-done.4.refs_2_
  19.4 1.0 %unpack.1 = (bf16[48,24,168]{2,1,0:T(8,128)(2,1)}, s32[1,48]{1,0:T(1,128)}) custom-call(bf16[12,32,128]{2,1,0:T(8,128)(2,1)S(1)} %collective-permute-done.2.refs_0_, bf16[12,32,128]{2,1,0:T(8,128)(2,1)S(1)} %collective-permute-done.3.refs_1_, bf16[12,32,128]{2,1,0:T(8,128)(2,1)S(1)} %collective-permute-done.4.refs_2_, ...), custom_call_target="tpu_custom_call" | custom-call | tf_op jit(solution)/shard_map/unpack/pallas_call | solution.py:250
Async XLA Ops:
  1.8 5.8 %collective-permute-start = (bf16[6,72,128]{2,1,0:T(8,128)(2,1)S(1)}, bf16[6,72,128]{2,1,0:T(8,128)(2,1)S(1)}, u32[]{:S(2)}, u32[]{:S(2)}) collective-permute-start(bf16[6,72,128]{2,1,0:T(8,128)(2,1)S(1)} %get-tuple-element.21), channel_id=1, source_target_pairs={{0,1},{2,3},{4,5},{6,7},{1,0},{3,2},{5,4},{7,6},{8,9},{10,11},{12,... | collective-permute-start | bytes 331784 | tf_op jit(solution)/shard_map/ppermute | solution.py:36
  3.1 6.4 %collective-permute-start.1 = (bf16[6,72,128]{2,1,0:T(8,128)(2,1)S(1)}, bf16[6,72,128]{2,1,0:T(8,128)(2,1)S(1)}, u32[]{:S(2)}, u32[]{:S(2)}) collective-permute-start(bf16[6,72,128]{2,1,0:T(8,128)(2,1)S(1)} %get-tuple-element.22), channel_id=1, source_target_pairs={{1,2},{3,4},{5,6},{2,1},{4,3},{6,5},{0,0},{7,7},{9,10},{11,12},{13... | collective-permute-start | bytes 331784 | tf_op jit(solution)/shard_map/ppermute | solution.py:36
  11.0 3.8 %collective-permute-start.2 = (bf16[12,32,128]{2,1,0:T(8,128)(2,1)S(1)}, bf16[12,32,128]{2,1,0:T(8,128)(2,1)S(1)}, u32[]{:S(2)}, u32[]{:S(2)}) collective-permute-start(bf16[12,32,128]{2,1,0:T(8,128)(2,1)S(1)} %get-tuple-element.24), channel_id=1, source_target_pairs={{0,16},{8,24},{16,0},{24,8},{1,17},{9,25},{17,1},{25,9},{2,18},{10... | collective-permute-start | bytes 294920 | tf_op jit(solution)/shard_map/ppermute | solution.py:249
  12.3 7.1 %collective-permute-start.3 = (bf16[12,32,128]{2,1,0:T(8,128)(2,1)S(1)}, bf16[12,32,128]{2,1,0:T(8,128)(2,1)S(1)}, u32[]{:S(2)}, u32[]{:S(2)}) collective-permute-start(bf16[12,32,128]{2,1,0:T(8,128)(2,1)S(1)} %get-tuple-element.25), channel_id=1, source_target_pairs={{0,24},{8,16},{16,8},{24,0},{1,25},{9,17},{17,9},{25,1},{2,26},{10... | collective-permute-start | bytes 294920 | tf_op jit(solution)/shard_map/ppermute | solution.py:249
  14.8 4.6 %collective-permute-start.4 = (bf16[12,32,128]{2,1,0:T(8,128)(2,1)S(1)}, bf16[12,32,128]{2,1,0:T(8,128)(2,1)S(1)}, u32[]{:S(2)}, u32[]{:S(2)}) collective-permute-start(bf16[12,32,128]{2,1,0:T(8,128)(2,1)S(1)} %get-tuple-element.26), channel_id=1, source_target_pairs={{0,8},{8,0},{16,24},{24,16},{1,9},{9,1},{17,25},{25,17},{2,10},{10... | collective-permute-start | bytes 294920 | tf_op jit(solution)/shard_map/ppermute | solution.py:249

commit v10 on v9

--- a/solution.py
+++ b/solution.py
@@ -32,8 +32,9 @@
 def swapped(value, axis, parity):
     peers = lax.axis_size(axis)
     pairs = [(i, i + 1) for i in range(parity, peers - 1, 2)]
-    alone = set(range(peers)) - {i for pair in pairs for i in pair}
-    return lax.ppermute(value, axis, pairs + [(j, i) for i, j in pairs] + [(i, i) for i in sorted(alone)])
+    alone = sorted(set(range(peers)) - {i for pair in pairs for i in pair})
+    pairs += [(i, j) for i, j in zip(alone[::2], alone[1::2])]
+    return lax.ppermute(value, axis, pairs + [(j, i) for i, j in pairs])
 
 
 def fetch(pairs, sems):

time: 20.5 us -> 21.6 us (1.054)
  the two profiles are of different devices: /device:TPU:9 before, /device:TPU:0 now
where the time goes in v10:
time: 21.6 us; the launch traced here: 21.4 us
  starting transfers between devices  8.78 us (41%)
  Pallas kernels  6.27 us (29%)
  waiting for transfers between devices  5.73 us (27%)
  between operations  0.67 us (3%)
    ppermute x2, starting transfers between devices, swapped(): return lax.ppermute(value, axis, pairs + [(j, i) for i, j in pairs])  6.58 us
    ppermute x3, waiting for transfers between devices, on_device(): lax.ppermute(sends[k], 'grp', [(i, i ^ k) for i in range(owners)])  4.47 us
    pallas_call x1, Pallas kernels, on_device(): pl.pallas_call(functools.partial(left_kernel, capacity), out_shape=(pltpu...  2.59 us
    ppermute x3, starting transfers between devices, on_device(): lax.ppermute(sends[k], 'grp', [(i, i ^ k) for i in range(owners)])  2.21 us
    pallas_call x1, Pallas kernels, on_device(): pl.pallas_call(rows_kernel, out_shape=[pltpu.VMEM((capacity, 32, LANES),...  1.52 us
    ppermute x2, waiting for transfers between devices, swapped(): return lax.ppermute(value, axis, pairs + [(j, i) for i, j in pairs])  1.27 us
    pallas_call x1, Pallas kernels, on_device(): pl.pallas_call(pack_kernel, out_shape=(run, run, pltpu.VMEM(prolong.shape...  1.18 us
    pallas_call x1, Pallas kernels, on_device(): pl.pallas_call(functools.partial(unpack_kernel, elements, (*arrival, 0)),...  0.97 us
  transfers between devices with their start and end apart: 5, of which 3 were waited for; matrix products, arithmetic and copies ran while one was open for 0% of the time, Pallas kernels for 12%

profile of v10, /device:TPU:0, one launch (start us, length us, event | category | flops | bytes accessed | tf_op | source)
XLA Modules:
  0.0 21.4 jit_solution(9030410736225151378)
XLA Ops:
  0.6 1.2 %pack.1 = (bf16[6,72,128]{2,1,0:T(8,128)(2,1)S(1)}, bf16[6,72,128]{2,1,0:T(8,128)(2,1)S(1)}, bf16[24,24,192]{2,1,0:T(8,128)(2,1)S(1)}, f32[7,2,24]{2,1,0:T(2,128...) custom-call(s32[1,2]{1,0:T(1,128)} %count_hbm.1, s32[1,2]{1,0:T(1,128)} %offset_hbm.1, bf16[24,24,192]{2,1,0:T(8,128)(2,1)} %prolong_hbm.1, ...), custom_call_target="tpu_custom_call" | custom-call | tf_op jit(solution)/shard_map/pack/pallas_call | solution.py:197
  1.8 3.0 %collective-permute-start = (bf16[6,72,128]{2,1,0:T(8,128)(2,1)S(1)}, bf16[6,72,128]{2,1,0:T(8,128)(2,1)S(1)}, u32[]{:S(2)}, u32[]{:S(2)}) collective-permute-start(bf16[6,72,128]{2,1,0:T(8,128)(2,1)S(1)} %get-tuple-element.21), channel_id=1, source_target_pairs={{0,1},{2,3},{4,5},{6,7},{1,0},{3,2},{5,4},{7,6},{8,9},{10,11},{12,... | collective-permute-start | bytes 331784 | tf_op jit(solution)/shard_map/ppermute | solution.py:37
  4.8 3.6 %collective-permute-start.1 = (bf16[6,72,128]{2,1,0:T(8,128)(2,1)S(1)}, bf16[6,72,128]{2,1,0:T(8,128)(2,1)S(1)}, u32[]{:S(2)}, u32[]{:S(2)}) collective-permute-start(bf16[6,72,128]{2,1,0:T(8,128)(2,1)S(1)} %get-tuple-element.22), channel_id=1, source_target_pairs={{1,2},{3,4},{5,6},{0,7},{2,1},{4,3},{6,5},{7,0},{9,10},{11,12},{13... | collective-permute-start | bytes 331784 | tf_op jit(solution)/shard_map/ppermute | solution.py:37
  8.4 2.6 %left.1 = (bf16[24,7,48,192]{3,2,1,0:T(8,128)(2,1)S(1)}, s32[48]{0:T(128)S(4)}) custom-call(f32[7,2,24]{2,1,0:T(2,128)S(4)} %get-tuple-element.17.lame_ref, s32[1,24]{1,0:T(1,128)S(4)} %get-tuple-element.18.owner_ref, bf16[7,2,192,192]{3,2,1,0:T(8,128)(2,1)} %stiffness_hbm.1, bf16[576,192]{1,0:T(8,128)(2,1)S(1)} %bitcast.5), custom_call_target="tpu_custom_call" | custom-call | tf_op jit(solution)/shard_map/left/pallas_call | solution.py:220
  11.0 0.0 collective-permute-done.even_ref
  11.0 1.3 %collective-permute-done.1.odd_ref = bf16[6,72,128]{2,1,0:T(8,128)(2,1)S(1)} collective-permute-done((bf16[6,72,128]{2,1,0:T(8,128)(2,1)S(1)}, bf16[6,72,128]{2,1,0:T(8,128)(2,1)S(1)}, u32[]{:S(2)}, u32[]{:S(2)}) %collective-permute-start.1) | collective-permute-done | bytes 110624 | tf_op jit(solution)/shard_map/ppermute | solution.py:37
  12.3 1.5 %rows.1 = (bf16[12,32,128]{2,1,0:T(8,128)(2,1)S(1)}, bf16[12,32,128]{2,1,0:T(8,128)(2,1)S(1)}, bf16[12,32,128]{2,1,0:T(8,128)(2,1)S(1)}, bf16[12,32,128]{2,1,0:T(8,128)(2,1)S(1)}) custom-call(s32[7,24]{1,0:T(8,128)S(4)} %get-tuple-element.16.columns_ref, s32[48]{0:T(128)S(4)} %get-tuple-element.20.order_ref, bf16[576,192]{1,0:T(8,128)(2,1)S(1)} %bitcast.6, ...), custom_call_target="tpu_custom_call" | custom-call | tf_op jit(solution)/shard_map/rows/pallas_call | solution.py:234
  13.8 1.6 %collective-permute-start.2 = (bf16[12,32,128]{2,1,0:T(8,128)(2,1)S(1)}, bf16[12,32,128]{2,1,0:T(8,128)(2,1)S(1)}, u32[]{:S(2)}, u32[]{:S(2)}) collective-permute-start(bf16[12,32,128]{2,1,0:T(8,128)(2,1)S(1)} %get-tuple-element.24), channel_id=1, source_target_pairs={{0,16},{8,24},{16,0},{24,8},{1,17},{9,25},{17,1},{25,9},{2,18},{10... | collective-permute-start | bytes 294920 | tf_op jit(solution)/shard_map/ppermute | solution.py:250
  15.4 0.0 collective-permute-start.3
  15.4 0.6 %collective-permute-start.4 = (bf16[12,32,128]{2,1,0:T(8,128)(2,1)S(1)}, bf16[12,32,128]{2,1,0:T(8,128)(2,1)S(1)}, u32[]{:S(2)}, u32[]{:S(2)}) collective-permute-start(bf16[12,32,128]{2,1,0:T(8,128)(2,1)S(1)} %get-tuple-element.26), channel_id=1, source_target_pairs={{0,8},{8,0},{16,24},{24,16},{1,9},{9,1},{17,25},{25,17},{2,10},{10... | collective-permute-start | bytes 294920 | tf_op jit(solution)/shard_map/ppermute | solution.py:250
  16.0 2.6 %collective-permute-done.2.refs_0_ = bf16[12,32,128]{2,1,0:T(8,128)(2,1)S(1)} collective-permute-done((bf16[12,32,128]{2,1,0:T(8,128)(2,1)S(1)}, bf16[12,32,128]{2,1,0:T(8,128)(2,1)S(1)}, u32[]{:S(2)}, u32[]{:S(2)}) %collective-permute-start.2) | collective-permute-done | bytes 98336 | tf_op jit(solution)/shard_map/ppermute | solution.py:250
  18.6 1.9 %collective-permute-done.3.refs_1_ = bf16[12,32,128]{2,1,0:T(8,128)(2,1)S(1)} collective-permute-done((bf16[12,32,128]{2,1,0:T(8,128)(2,1)S(1)}, bf16[12,32,128]{2,1,0:T(8,128)(2,1)S(1)}, u32[]{:S(2)}, u32[]{:S(2)}) %collective-permute-start.3) | collective-permute-done | bytes 98336 | tf_op jit(solution)/shard_map/ppermute | solution.py:250
  20.5 0.0 collective-permute-done.4.refs_2_
  20.5 1.0 %unpack.1 = (bf16[48,24,168]{2,1,0:T(8,128)(2,1)}, s32[1,48]{1,0:T(1,128)}) custom-call(bf16[12,32,128]{2,1,0:T(8,128)(2,1)S(1)} %collective-permute-done.2.refs_0_, bf16[12,32,128]{2,1,0:T(8,128)(2,1)S(1)} %collective-permute-done.3.refs_1_, bf16[12,32,128]{2,1,0:T(8,128)(2,1)S(1)} %collective-permute-done.4.refs_2_, ...), custom_call_target="tpu_custom_call" | custom-call | tf_op jit(solution)/shard_map/unpack/pallas_call | solution.py:251
Async XLA Ops:
  1.8 9.2 %collective-permute-start = (bf16[6,72,128]{2,1,0:T(8,128)(2,1)S(1)}, bf16[6,72,128]{2,1,0:T(8,128)(2,1)S(1)}, u32[]{:S(2)}, u32[]{:S(2)}) collective-permute-start(bf16[6,72,128]{2,1,0:T(8,128)(2,1)S(1)} %get-tuple-element.21), channel_id=1, source_target_pairs={{0,1},{2,3},{4,5},{6,7},{1,0},{3,2},{5,4},{7,6},{8,9},{10,11},{12,... | collective-permute-start | bytes 331784 | tf_op jit(solution)/shard_map/ppermute | solution.py:37
  4.8 7.4 %collective-permute-start.1 = (bf16[6,72,128]{2,1,0:T(8,128)(2,1)S(1)}, bf16[6,72,128]{2,1,0:T(8,128)(2,1)S(1)}, u32[]{:S(2)}, u32[]{:S(2)}) collective-permute-start(bf16[6,72,128]{2,1,0:T(8,128)(2,1)S(1)} %get-tuple-element.22), channel_id=1, source_target_pairs={{1,2},{3,4},{5,6},{0,7},{2,1},{4,3},{6,5},{7,0},{9,10},{11,12},{13... | collective-permute-start | bytes 331784 | tf_op jit(solution)/shard_map/ppermute | solution.py:37
  13.8 4.8 %collective-permute-start.2 = (bf16[12,32,128]{2,1,0:T(8,128)(2,1)S(1)}, bf16[12,32,128]{2,1,0:T(8,128)(2,1)S(1)}, u32[]{:S(2)}, u32[]{:S(2)}) collective-permute-start(bf16[12,32,128]{2,1,0:T(8,128)(2,1)S(1)} %get-tuple-element.24), channel_id=1, source_target_pairs={{0,16},{8,24},{16,0},{24,8},{1,17},{9,25},{17,1},{25,9},{2,18},{10... | collective-permute-start | bytes 294920 | tf_op jit(solution)/shard_map/ppermute | solution.py:250
  15.4 5.1 %collective-permute-start.3 = (bf16[12,32,128]{2,1,0:T(8,128)(2,1)S(1)}, bf16[12,32,128]{2,1,0:T(8,128)(2,1)S(1)}, u32[]{:S(2)}, u32[]{:S(2)}) collective-permute-start(bf16[12,32,128]{2,1,0:T(8,128)(2,1)S(1)} %get-tuple-element.25), channel_id=1, source_target_pairs={{0,24},{8,16},{16,8},{24,0},{1,25},{9,17},{17,9},{25,1},{2,26},{10... | collective-permute-start | bytes 294920 | tf_op jit(solution)/shard_map/ppermute | solution.py:250
  15.4 5.1 %collective-permute-start.4 = (bf16[12,32,128]{2,1,0:T(8,128)(2,1)S(1)}, bf16[12,32,128]{2,1,0:T(8,128)(2,1)S(1)}, u32[]{:S(2)}, u32[]{:S(2)}) collective-permute-start(bf16[12,32,128]{2,1,0:T(8,128)(2,1)S(1)} %get-tuple-element.26), channel_id=1, source_target_pairs={{0,8},{8,0},{16,24},{24,16},{1,9},{9,1},{17,25},{25,17},{2,10},{10... | collective-permute-start | bytes 294920 | tf_op jit(solution)/shard_map/ppermute | solution.py:250

commit v11 on v9

--- a/solution.py
+++ b/solution.py
@@ -29,11 +29,15 @@
     return pltpu.CompilerParams(vmem_limit_bytes=24 * 1024 * 1024)
 
 
-def swapped(value, axis, parity):
-    peers = lax.axis_size(axis)
-    pairs = [(i, i + 1) for i in range(parity, peers - 1, 2)]
-    alone = set(range(peers)) - {i for pair in pairs for i in pair}
-    return lax.ppermute(value, axis, pairs + [(j, i) for i, j in pairs] + [(i, i) for i in sorted(alone)])
+def swapped(value, parity):
+    rows = lax.axis_size("row")
+    pairs = []
+    for group in range(lax.axis_size("grp")):
+        for row in range(rows):
+            other = row + 1 if row % 2 == parity else row - 1
+            there = (group, other) if 0 <= other < rows else (group ^ 1, row)
+            pairs.append((group * rows + row, there[0] * rows + there[1]))
+    return lax.ppermute(value, ("grp", "row"), pairs)
 
 
 def fetch(pairs, sems):
@@ -213,8 +217,8 @@
         in_hbm(ghost_count), in_hbm(ghost_offset), in_hbm(prolong),
         in_hbm(lame.transpose(1, 2, 0)), in_hbm(columns.T), in_hbm(owner_map.T),
     )
-    from_even = swapped(by_even, "row", 0)
-    from_odd = swapped(by_odd, "row", 1)
+    from_even = swapped(by_even, 0)
+    from_odd = swapped(by_odd, 1)
     own = in_vmem(own.reshape(elements * coarse, fine))
     left, order = pl.pallas_call(
         functools.partial(left_kernel, capacity),

time: 20.5 us -> 18.9 us (0.922); the launches traced: 20.4 us -> 18.5 us
  starting transfers between devices: 6.97 us -> 5.01 us
    ppermute x2, starting transfers between devices: 3.18 us -> 1.28 us  [swapped(): return lax.ppermute(value, ('grp', 'row'), pairs)]
  transfers between devices with their start and end apart: 5 -> 5, of which waited for: 2 -> 3; matrix products, arithmetic and copies ran while one was open for 0% -> 0% of each run, Pallas kernels for 13% -> 14%
where the time goes in v11:
time: 18.9 us; the launch traced here: 18.5 us
  waiting for transfers between devices  6.55 us (35%)
  Pallas kernels  6.27 us (33%)
  starting transfers between devices  5.01 us (27%)
  between operations  0.66 us (3%)
    ppermute x3, waiting for transfers between devices, on_device(): lax.ppermute(sends[k], 'grp', [(i, i ^ k) for i in range(owners)])  4.55 us
    ppermute x3, starting transfers between devices, on_device(): lax.ppermute(sends[k], 'grp', [(i, i ^ k) for i in range(owners)])  3.73 us
    pallas_call x1, Pallas kernels, on_device(): pl.pallas_call(functools.partial(left_kernel, capacity), out_shape=(pltpu...  2.59 us
    ppermute x2, waiting for transfers between devices, swapped(): return lax.ppermute(value, ('grp', 'row'), pairs)  2 us
    pallas_call x1, Pallas kernels, on_device(): pl.pallas_call(rows_kernel, out_shape=[pltpu.VMEM((capacity, 32, LANES),...  1.53 us
    ppermute x2, starting transfers between devices, swapped(): return lax.ppermute(value, ('grp', 'row'), pairs)  1.28 us
    pallas_call x1, Pallas kernels, on_device(): pl.pallas_call(pack_kernel, out_shape=(run, run, pltpu.VMEM(prolong.shape...  1.18 us
    pallas_call x1, Pallas kernels, on_device(): pl.pallas_call(functools.partial(unpack_kernel, elements, (*arrival, 0)),...  0.97 us
  transfers between devices with their start and end apart: 5, of which 3 were waited for; matrix products, arithmetic and copies ran while one was open for 0% of the time, Pallas kernels for 14%

profile of v11, /device:TPU:9, one launch (start us, length us, event | category | flops | bytes accessed | tf_op | source)
XLA Modules:
  0.0 18.5 jit_solution(14867455990992067806)
XLA Ops:
  0.6 1.2 %pack.1 = (bf16[6,72,128]{2,1,0:T(8,128)(2,1)S(1)}, bf16[6,72,128]{2,1,0:T(8,128)(2,1)S(1)}, bf16[24,24,192]{2,1,0:T(8,128)(2,1)S(1)}, f32[7,2,24]{2,1,0:T(2,128...) custom-call(s32[1,2]{1,0:T(1,128)} %count_hbm.1, s32[1,2]{1,0:T(1,128)} %offset_hbm.1, bf16[24,24,192]{2,1,0:T(8,128)(2,1)} %prolong_hbm.1, ...), custom_call_target="tpu_custom_call" | custom-call | tf_op jit(solution)/shard_map/pack/pallas_call | solution.py:200
  1.8 1.3 %collective-permute-start = (bf16[6,72,128]{2,1,0:T(8,128)(2,1)S(1)}, bf16[6,72,128]{2,1,0:T(8,128)(2,1)S(1)}, u32[]{:S(2)}, u32[]{:S(2)}) collective-permute-start(bf16[6,72,128]{2,1,0:T(8,128)(2,1)S(1)} %get-tuple-element.21), channel_id=1, source_target_pairs={{0,1},{1,0},{2,3},{3,2},{4,5},{5,4},{6,7},{7,6},{8,9},{9,8},{10,11... | collective-permute-start | bytes 331784 | tf_op jit(solution)/shard_map/ppermute | solution.py:40
  3.1 0.0 collective-permute-start.1
  3.1 2.6 %left.1 = (bf16[24,7,48,192]{3,2,1,0:T(8,128)(2,1)S(1)}, s32[48]{0:T(128)S(4)}) custom-call(f32[7,2,24]{2,1,0:T(2,128)S(4)} %get-tuple-element.17.lame_ref, s32[1,24]{1,0:T(1,128)S(4)} %get-tuple-element.18.owner_ref, bf16[7,2,192,192]{3,2,1,0:T(8,128)(2,1)} %stiffness_hbm.1, bf16[576,192]{1,0:T(8,128)(2,1)S(1)} %bitcast.5), custom_call_target="tpu_custom_call" | custom-call | tf_op jit(solution)/shard_map/left/pallas_call | solution.py:223
  5.7 0.1 collective-permute-done.even_ref
  5.8 1.9 %collective-permute-done.1.odd_ref = bf16[6,72,128]{2,1,0:T(8,128)(2,1)S(1)} collective-permute-done((bf16[6,72,128]{2,1,0:T(8,128)(2,1)S(1)}, bf16[6,72,128]{2,1,0:T(8,128)(2,1)S(1)}, u32[]{:S(2)}, u32[]{:S(2)}) %collective-permute-start.1) | collective-permute-done | bytes 110624 | tf_op jit(solution)/shard_map/ppermute | solution.py:40
  7.7 1.5 %rows.1 = (bf16[12,32,128]{2,1,0:T(8,128)(2,1)S(1)}, bf16[12,32,128]{2,1,0:T(8,128)(2,1)S(1)}, bf16[12,32,128]{2,1,0:T(8,128)(2,1)S(1)}, bf16[12,32,128]{2,1,0:T(8,128)(2,1)S(1)}) custom-call(s32[7,24]{1,0:T(8,128)S(4)} %get-tuple-element.16.columns_ref, s32[48]{0:T(128)S(4)} %get-tuple-element.20.order_ref, bf16[576,192]{1,0:T(8,128)(2,1)S(1)} %bitcast.6, ...), custom_call_target="tpu_custom_call" | custom-call | tf_op jit(solution)/shard_map/rows/pallas_call | solution.py:237
  9.2 1.3 %collective-permute-start.2 = (bf16[12,32,128]{2,1,0:T(8,128)(2,1)S(1)}, bf16[12,32,128]{2,1,0:T(8,128)(2,1)S(1)}, u32[]{:S(2)}, u32[]{:S(2)}) collective-permute-start(bf16[12,32,128]{2,1,0:T(8,128)(2,1)S(1)} %get-tuple-element.24), channel_id=1, source_target_pairs={{0,16},{8,24},{16,0},{24,8},{1,17},{9,25},{17,1},{25,9},{2,18},{10... | collective-permute-start | bytes 294920 | tf_op jit(solution)/shard_map/ppermute | solution.py:253
  10.5 2.4 %collective-permute-start.3 = (bf16[12,32,128]{2,1,0:T(8,128)(2,1)S(1)}, bf16[12,32,128]{2,1,0:T(8,128)(2,1)S(1)}, u32[]{:S(2)}, u32[]{:S(2)}) collective-permute-start(bf16[12,32,128]{2,1,0:T(8,128)(2,1)S(1)} %get-tuple-element.25), channel_id=1, source_target_pairs={{0,24},{8,16},{16,8},{24,0},{1,25},{9,17},{17,9},{25,1},{2,26},{10... | collective-permute-start | bytes 294920 | tf_op jit(solution)/shard_map/ppermute | solution.py:253
  13.0 0.0 collective-permute-start.4
  13.0 0.0 collective-permute-done.2.refs_0_
  13.0 4.5 %collective-permute-done.3.refs_1_ = bf16[12,32,128]{2,1,0:T(8,128)(2,1)S(1)} collective-permute-done((bf16[12,32,128]{2,1,0:T(8,128)(2,1)S(1)}, bf16[12,32,128]{2,1,0:T(8,128)(2,1)S(1)}, u32[]{:S(2)}, u32[]{:S(2)}) %collective-permute-start.3) | collective-permute-done | bytes 98336 | tf_op jit(solution)/shard_map/ppermute | solution.py:253
  17.5 0.0 collective-permute-done.4.refs_2_
  17.5 1.0 %unpack.1 = (bf16[48,24,168]{2,1,0:T(8,128)(2,1)}, s32[1,48]{1,0:T(1,128)}) custom-call(bf16[12,32,128]{2,1,0:T(8,128)(2,1)S(1)} %collective-permute-done.2.refs_0_, bf16[12,32,128]{2,1,0:T(8,128)(2,1)S(1)} %collective-permute-done.3.refs_1_, bf16[12,32,128]{2,1,0:T(8,128)(2,1)S(1)} %collective-permute-done.4.refs_2_, ...), custom_call_target="tpu_custom_call" | custom-call | tf_op jit(solution)/shard_map/unpack/pallas_call | solution.py:254
Async XLA Ops:
  1.8 4.0 %collective-permute-start = (bf16[6,72,128]{2,1,0:T(8,128)(2,1)S(1)}, bf16[6,72,128]{2,1,0:T(8,128)(2,1)S(1)}, u32[]{:S(2)}, u32[]{:S(2)}) collective-permute-start(bf16[6,72,128]{2,1,0:T(8,128)(2,1)S(1)} %get-tuple-element.21), channel_id=1, source_target_pairs={{0,1},{1,0},{2,3},{3,2},{4,5},{5,4},{6,7},{7,6},{8,9},{9,8},{10,11... | collective-permute-start | bytes 331784 | tf_op jit(solution)/shard_map/ppermute | solution.py:40
  3.1 4.6 %collective-permute-start.1 = (bf16[6,72,128]{2,1,0:T(8,128)(2,1)S(1)}, bf16[6,72,128]{2,1,0:T(8,128)(2,1)S(1)}, u32[]{:S(2)}, u32[]{:S(2)}) collective-permute-start(bf16[6,72,128]{2,1,0:T(8,128)(2,1)S(1)} %get-tuple-element.22), channel_id=1, source_target_pairs={{0,8},{1,2},{2,1},{3,4},{4,3},{5,6},{6,5},{7,15},{8,0},{9,10},{10,... | collective-permute-start | bytes 331784 | tf_op jit(solution)/shard_map/ppermute | solution.py:40
  9.2 3.7 %collective-permute-start.2 = (bf16[12,32,128]{2,1,0:T(8,128)(2,1)S(1)}, bf16[12,32,128]{2,1,0:T(8,128)(2,1)S(1)}, u32[]{:S(2)}, u32[]{:S(2)}) collective-permute-start(bf16[12,32,128]{2,1,0:T(8,128)(2,1)S(1)} %get-tuple-element.24), channel_id=1, source_target_pairs={{0,16},{8,24},{16,0},{24,8},{1,17},{9,25},{17,1},{25,9},{2,18},{10... | collective-permute-start | bytes 294920 | tf_op jit(solution)/shard_map/ppermute | solution.py:253
  10.5 7.0 %collective-permute-start.3 = (bf16[12,32,128]{2,1,0:T(8,128)(2,1)S(1)}, bf16[12,32,128]{2,1,0:T(8,128)(2,1)S(1)}, u32[]{:S(2)}, u32[]{:S(2)}) collective-permute-start(bf16[12,32,128]{2,1,0:T(8,128)(2,1)S(1)} %get-tuple-element.25), channel_id=1, source_target_pairs={{0,24},{8,16},{16,8},{24,0},{1,25},{9,17},{17,9},{25,1},{2,26},{10... | collective-permute-start | bytes 294920 | tf_op jit(solution)/shard_map/ppermute | solution.py:253
  13.0 4.6 %collective-permute-start.4 = (bf16[12,32,128]{2,1,0:T(8,128)(2,1)S(1)}, bf16[12,32,128]{2,1,0:T(8,128)(2,1)S(1)}, u32[]{:S(2)}, u32[]{:S(2)}) collective-permute-start(bf16[12,32,128]{2,1,0:T(8,128)(2,1)S(1)} %get-tuple-element.26), channel_id=1, source_target_pairs={{0,8},{8,0},{16,24},{24,16},{1,9},{9,1},{17,25},{25,17},{2,10},{10... | collective-permute-start | bytes 294920 | tf_op jit(solution)/shard_map/ppermute | solution.py:253

commit v12 on v11

--- a/solution.py
+++ b/solution.py
@@ -162,32 +162,53 @@
             send[p] = packed[order_ref[k * capacity + p]]
 
 
-def unpack_kernel(elements, away, *refs):
-    received, (rows_ref, ids_ref) = refs[:-2], refs[-2:]
+def unpack_kernel(elements, away, last, *refs):
+    received, refs = refs[: len(away)], refs[len(away) :]
+    if last:
+        _, before_ref, rows_hbm, ids_hbm, rows_ref, ids_ref, sems = refs
+        local = before_ref[...]
+    else:
+        rows_hbm, after_ref, rows_ref, sems = refs
+        local = jnp.full(after_ref.shape, -1.0, jnp.float32)
     capacity = received[0].shape[0]
     rest = rows_ref.shape[2] - LANES
-    count = rows_ref.shape[0]
-    wide = pl.cdiv(count, LANES) * LANES
     me = lax.axis_index("grp")
-    lane = lax.broadcasted_iota(jnp.int32, (8, wide), 1)
-    local = jnp.full((8, wide), -1.0, jnp.float32)
+    lane = lax.broadcasted_iota(jnp.int32, local.shape, 1)
     for k, ref in zip(away, received):
         first = lax.bitwise_xor(me, k) * capacity
         for p in range(capacity):
+            local = jnp.where(lane == first + p, ref[p].astype(jnp.float32)[24:32, 127:128], local)
+    copies = []
+    if last:
+        count = ids_ref.shape[1]
+        owned = local[0:1, :count].astype(jnp.int32)
+        group = lax.broadcasted_iota(jnp.int32, (1, count), 1) // capacity
+        start = (group * lax.axis_size("row") + lax.axis_index("row")) * elements
+        ids_ref[...] = jnp.where(owned >= 0, start + owned, -1)
+        copies.append(pltpu.make_async_copy(ids_ref, ids_hbm, sems.at[len(away)]))
+        copies[-1].start()
+    else:
+        after_ref[...] = local
+    for i, (k, ref) in enumerate(zip(away, received)):
+        for p in range(capacity):
             block = ref[p].astype(jnp.float32)
             tail = block[24:32]
-            rows_ref[first + p] = jnp.concatenate(
+            rows_ref[i * capacity + p] = jnp.concatenate(
                 [
                     block[0:24],
                     jnp.concatenate([tail[:, rest * q : rest * (q + 1)] for q in range(3)], axis=0),
                 ],
                 axis=1,
             ).astype(jnp.bfloat16)
-            local = jnp.where(lane == first + p, tail[:, 127:128], local)
-    local = local[0:1, :count].astype(jnp.int32)
-    group = lax.broadcasted_iota(jnp.int32, (1, count), 1) // capacity
-    first = (group * lax.axis_size("row") + lax.axis_index("row")) * elements
-    ids_ref[...] = jnp.where(local >= 0, first + local, -1)
+        first = lax.bitwise_xor(me, k) * capacity
+        copies.append(
+            pltpu.make_async_copy(
+                rows_ref.at[pl.ds(i * capacity, capacity)], rows_hbm.at[pl.ds(first, capacity)], sems.at[i]
+            )
+        )
+        copies[-1].start()
+    for copy in copies:
+        copy.wait()
 
 
 def on_device(stiffness, lame, prolong, columns, ghost_count, ghost_offset, owner_map):
@@ -247,19 +268,36 @@
         in_smem(by_slot), in_smem(order), own,
         in_vmem(from_even), in_vmem(from_odd), in_vmem(left),
     )
-    arrival = [*range(2, owners), 1]
     received = {0: sends[0]}
-    for k in arrival:
+    for k in [*range(2, owners), 1]:
         received[k] = lax.ppermute(sends[k], "grp", [(i, i ^ k) for i in range(owners)])
+    received = {k: in_vmem(value) for k, value in received.items()}
+    rows = jax.ShapeDtypeStruct((owners * capacity, coarse, slots * coarse), jnp.bfloat16)
+    wide = pl.cdiv(owners * capacity, LANES) * LANES
+
+    def scratch(blocks):
+        return pltpu.VMEM((blocks * capacity, coarse, slots * coarse), jnp.bfloat16)
+
+    early, late = [*range(2, owners - 1), 0], [owners - 1, 1]
+    partial, local = pl.pallas_call(
+        functools.partial(unpack_kernel, elements, early, False),
+        out_shape=(pltpu.HBM(rows.shape, rows.dtype), pltpu.VMEM((8, wide), jnp.float32)),
+        in_specs=[VMEM] * len(early), out_specs=(HBM, VMEM),
+        scratch_shapes=[scratch(len(early)), pltpu.SemaphoreType.DMA((len(early),))],
+        compiler_params=params(), name="unpack_early",
+    )(*[received[k] for k in early])
     coarse_rows, ids = pl.pallas_call(
-        functools.partial(unpack_kernel, elements, (*arrival, 0)),
-        out_shape=(
-            jax.ShapeDtypeStruct((owners * capacity, coarse, slots * coarse), jnp.bfloat16),
-            jax.ShapeDtypeStruct((1, owners * capacity), jnp.int32),
-        ),
-        in_specs=[VMEM] * owners, out_specs=(VMEM, VMEM),
-        compiler_params=params(), name="unpack",
-    )(*[in_vmem(received[k]) for k in (*arrival, 0)])
+        functools.partial(unpack_kernel, elements, late, True),
+        out_shape=(rows, jax.ShapeDtypeStruct((1, owners * capacity), jnp.int32)),
+        in_specs=[VMEM] * len(late) + [HBM, VMEM], out_specs=(HBM, HBM),
+        scratch_shapes=[
+            scratch(len(late)),
+            pltpu.VMEM((1, owners * capacity), jnp.int32),
+            pltpu.SemaphoreType.DMA((len(late) + 1,)),
+        ],
+        input_output_aliases={len(late): 0},
+        compiler_params=params(), name="unpack_late",
+    )(*[received[k] for k in late], in_hbm(partial), in_vmem(local))
     return (coarse_rows, ids.reshape(-1))
 
 

time: 18.9 us -> 18.7 us (0.989)
  waiting for transfers between devices: 6.55 us -> 5.74 us
  Pallas kernels: 6.27 us -> 6.95 us
    ppermute x3, waiting for transfers between devices: 4.55 us -> 3.74 us  [on_device(): lax.ppermute(sends[k], 'grp', [(i, i ^ k) for i in range(owners)])]
    pallas_call x1 -> x2, Pallas kernels: 0.97 us -> 1.66 us  [the longest x1 0.84 us: on_device(): pl.pallas_call(functools.partial(unpack_kernel, elements, late, True), ou...]
  transfers between devices with their start and end apart: 5 -> 5, of which waited for: 3 -> 3; matrix products, arithmetic and copies ran while one was open for 0% -> 0% of each run, Pallas kernels for 14% -> 19%
where the time goes in v12:
time: 18.7 us; the launch traced here: 18.4 us
  Pallas kernels  6.95 us (37%)
  waiting for transfers between devices  5.74 us (31%)
  starting transfers between devices  5.01 us (27%)
  between operations  0.67 us (4%)
    ppermute x3, waiting for transfers between devices, on_device(): lax.ppermute(sends[k], 'grp', [(i, i ^ k) for i in range(owners)])  3.74 us
    ppermute x3, starting transfers between devices, on_device(): lax.ppermute(sends[k], 'grp', [(i, i ^ k) for i in range(owners)])  3.73 us
    pallas_call x1, Pallas kernels, on_device(): pl.pallas_call(functools.partial(left_kernel, capacity), out_shape=(pltpu...  2.59 us
    ppermute x2, waiting for transfers between devices, swapped(): return lax.ppermute(value, ('grp', 'row'), pairs)  2 us
    pallas_call x1, Pallas kernels, on_device(): pl.pallas_call(rows_kernel, out_shape=[pltpu.VMEM((capacity, 32, LANES),...  1.52 us
    ppermute x2, starting transfers between devices, swapped(): return lax.ppermute(value, ('grp', 'row'), pairs)  1.28 us
    pallas_call x1, Pallas kernels, on_device(): pl.pallas_call(pack_kernel, out_shape=(run, run, pltpu.VMEM(prolong.shape...  1.18 us
    pallas_call x1, Pallas kernels, on_device(): pl.pallas_call(functools.partial(unpack_kernel, elements, late, True), ou...  0.84 us
  transfers between devices with their start and end apart: 5, of which 3 were waited for; matrix products, arithmetic and copies ran while one was open for 0% of the time, Pallas kernels for 19%

profile of v12, /device:TPU:9, one launch (start us, length us, event | category | flops | bytes accessed | tf_op | source)
XLA Modules:
  0.0 18.4 jit_solution(11211788663460086212)
XLA Ops:
  0.6 1.2 %pack.1 = (bf16[6,72,128]{2,1,0:T(8,128)(2,1)S(1)}, bf16[6,72,128]{2,1,0:T(8,128)(2,1)S(1)}, bf16[24,24,192]{2,1,0:T(8,128)(2,1)S(1)}, f32[7,2,24]{2,1,0:T(2,128...) custom-call(s32[1,2]{1,0:T(1,128)} %count_hbm.1, s32[1,2]{1,0:T(1,128)} %offset_hbm.1, bf16[24,24,192]{2,1,0:T(8,128)(2,1)} %prolong_hbm.1, ...), custom_call_target="tpu_custom_call" | custom-call | tf_op jit(solution)/shard_map/pack/pallas_call | solution.py:221
  1.8 1.3 %collective-permute-start = (bf16[6,72,128]{2,1,0:T(8,128)(2,1)S(1)}, bf16[6,72,128]{2,1,0:T(8,128)(2,1)S(1)}, u32[]{:S(2)}, u32[]{:S(2)}) collective-permute-start(bf16[6,72,128]{2,1,0:T(8,128)(2,1)S(1)} %get-tuple-element.23), channel_id=1, source_target_pairs={{0,1},{1,0},{2,3},{3,2},{4,5},{5,4},{6,7},{7,6},{8,9},{9,8},{10,11... | collective-permute-start | bytes 331784 | tf_op jit(solution)/shard_map/ppermute | solution.py:40
  3.1 0.0 collective-permute-start.1
  3.1 2.6 %left.1 = (bf16[24,7,48,192]{3,2,1,0:T(8,128)(2,1)S(1)}, s32[48]{0:T(128)S(4)}) custom-call(f32[7,2,24]{2,1,0:T(2,128)S(4)} %get-tuple-element.19.lame_ref, s32[1,24]{1,0:T(1,128)S(4)} %get-tuple-element.20.owner_ref, bf16[7,2,192,192]{3,2,1,0:T(8,128)(2,1)} %stiffness_hbm.1, bf16[576,192]{1,0:T(8,128)(2,1)S(1)} %bitcast.5), custom_call_target="tpu_custom_call" | custom-call | tf_op jit(solution)/shard_map/left/pallas_call | solution.py:244
  5.7 0.1 collective-permute-done.even_ref
  5.8 1.9 %collective-permute-done.1.odd_ref = bf16[6,72,128]{2,1,0:T(8,128)(2,1)S(1)} collective-permute-done((bf16[6,72,128]{2,1,0:T(8,128)(2,1)S(1)}, bf16[6,72,128]{2,1,0:T(8,128)(2,1)S(1)}, u32[]{:S(2)}, u32[]{:S(2)}) %collective-permute-start.1) | collective-permute-done | bytes 110624 | tf_op jit(solution)/shard_map/ppermute | solution.py:40
  7.7 1.5 %rows.1 = (bf16[12,32,128]{2,1,0:T(8,128)(2,1)S(1)}, bf16[12,32,128]{2,1,0:T(8,128)(2,1)S(1)}, bf16[12,32,128]{2,1,0:T(8,128)(2,1)S(1)}, bf16[12,32,128]{2,1,0:T(8,128)(2,1)S(1)}) custom-call(s32[7,24]{1,0:T(8,128)S(4)} %get-tuple-element.18.columns_ref, s32[48]{0:T(128)S(4)} %get-tuple-element.22.order_ref, bf16[576,192]{1,0:T(8,128)(2,1)S(1)} %bitcast.6, ...), custom_call_target="tpu_custom_call" | custom-call | tf_op jit(solution)/shard_map/rows/pallas_call | solution.py:258
  9.2 1.3 %collective-permute-start.4 = (bf16[12,32,128]{2,1,0:T(8,128)(2,1)S(1)}, bf16[12,32,128]{2,1,0:T(8,128)(2,1)S(1)}, u32[]{:S(2)}, u32[]{:S(2)}) collective-permute-start(bf16[12,32,128]{2,1,0:T(8,128)(2,1)S(1)} %get-tuple-element.28), channel_id=1, source_target_pairs={{0,16},{8,24},{16,0},{24,8},{1,17},{9,25},{17,1},{25,9},{2,18},{10... | collective-permute-start | bytes 294920 | tf_op jit(solution)/shard_map/ppermute | solution.py:273
  10.5 2.4 %collective-permute-start.2 = (bf16[12,32,128]{2,1,0:T(8,128)(2,1)S(1)}, bf16[12,32,128]{2,1,0:T(8,128)(2,1)S(1)}, u32[]{:S(2)}, u32[]{:S(2)}) collective-permute-start(bf16[12,32,128]{2,1,0:T(8,128)(2,1)S(1)} %get-tuple-element.26), channel_id=1, source_target_pairs={{0,24},{8,16},{16,8},{24,0},{1,25},{9,17},{17,9},{25,1},{2,26},{10... | collective-permute-start | bytes 294920 | tf_op jit(solution)/shard_map/ppermute | solution.py:273
  13.0 0.0 collective-permute-start.3
  13.0 0.0 collective-permute-done.4.refs_0_
  13.0 0.8 %unpack_early.1 = (bf16[48,24,168]{2,1,0:T(8,128)(2,1)}, f32[8,128]{1,0:T(8,128)S(1)}) custom-call(bf16[12,32,128]{2,1,0:T(8,128)(2,1)S(1)} %collective-permute-done.4.refs_0_, bf16[12,32,128]{2,1,0:T(8,128)(2,1)S(1)} %get-tuple-element.29.refs_1_), custom_call_target="tpu_custom_call" | custom-call | tf_op jit(solution)/shard_map/unpack_early/pallas_call | solution.py:282
  13.8 3.7 %collective-permute-done.2.refs_0_ = bf16[12,32,128]{2,1,0:T(8,128)(2,1)S(1)} collective-permute-done((bf16[12,32,128]{2,1,0:T(8,128)(2,1)S(1)}, bf16[12,32,128]{2,1,0:T(8,128)(2,1)S(1)}, u32[]{:S(2)}, u32[]{:S(2)}) %collective-permute-start.2) | collective-permute-done | bytes 98336 | tf_op jit(solution)/shard_map/ppermute | solution.py:273
  17.5 0.0 collective-permute-done.3.refs_1_
  17.5 0.8 %unpack_late.1 = (bf16[48,24,168]{2,1,0:T(8,128)(2,1)}, s32[1,48]{1,0:T(1,128)}) custom-call(bf16[12,32,128]{2,1,0:T(8,128)(2,1)S(1)} %collective-permute-done.2.refs_0_, bf16[12,32,128]{2,1,0:T(8,128)(2,1)S(1)} %collective-permute-done.3.refs_1_, bf16[48,24,168]{2,1,0:T(8,128)(2,1)} %get-tuple-element.30.refs_2_, ...), custom_call_target="tpu_custom_call", output_to_operand_aliasing={{0}: (2, {})} | custom-call | tf_op jit(solution)/shard_map/unpack_late/pallas_call | solution.py:289
Async XLA Ops:
  1.8 4.0 %collective-permute-start = (bf16[6,72,128]{2,1,0:T(8,128)(2,1)S(1)}, bf16[6,72,128]{2,1,0:T(8,128)(2,1)S(1)}, u32[]{:S(2)}, u32[]{:S(2)}) collective-permute-start(bf16[6,72,128]{2,1,0:T(8,128)(2,1)S(1)} %get-tuple-element.23), channel_id=1, source_target_pairs={{0,1},{1,0},{2,3},{3,2},{4,5},{5,4},{6,7},{7,6},{8,9},{9,8},{10,11... | collective-permute-start | bytes 331784 | tf_op jit(solution)/shard_map/ppermute | solution.py:40
  3.1 4.6 %collective-permute-start.1 = (bf16[6,72,128]{2,1,0:T(8,128)(2,1)S(1)}, bf16[6,72,128]{2,1,0:T(8,128)(2,1)S(1)}, u32[]{:S(2)}, u32[]{:S(2)}) collective-permute-start(bf16[6,72,128]{2,1,0:T(8,128)(2,1)S(1)} %get-tuple-element.24), channel_id=1, source_target_pairs={{0,8},{1,2},{2,1},{3,4},{4,3},{5,6},{6,5},{7,15},{8,0},{9,10},{10,... | collective-permute-start | bytes 331784 | tf_op jit(solution)/shard_map/ppermute | solution.py:40
  9.2 3.7 %collective-permute-start.4 = (bf16[12,32,128]{2,1,0:T(8,128)(2,1)S(1)}, bf16[12,32,128]{2,1,0:T(8,128)(2,1)S(1)}, u32[]{:S(2)}, u32[]{:S(2)}) collective-permute-start(bf16[12,32,128]{2,1,0:T(8,128)(2,1)S(1)} %get-tuple-element.28), channel_id=1, source_target_pairs={{0,16},{8,24},{16,0},{24,8},{1,17},{9,25},{17,1},{25,9},{2,18},{10... | collective-permute-start | bytes 294920 | tf_op jit(solution)/shard_map/ppermute | solution.py:273
  10.5 7.0 %collective-permute-start.2 = (bf16[12,32,128]{2,1,0:T(8,128)(2,1)S(1)}, bf16[12,32,128]{2,1,0:T(8,128)(2,1)S(1)}, u32[]{:S(2)}, u32[]{:S(2)}) collective-permute-start(bf16[12,32,128]{2,1,0:T(8,128)(2,1)S(1)} %get-tuple-element.26), channel_id=1, source_target_pairs={{0,24},{8,16},{16,8},{24,0},{1,25},{9,17},{17,9},{25,1},{2,26},{10... | collective-permute-start | bytes 294920 | tf_op jit(solution)/shard_map/ppermute | solution.py:273
  13.0 4.6 %collective-permute-start.3 = (bf16[12,32,128]{2,1,0:T(8,128)(2,1)S(1)}, bf16[12,32,128]{2,1,0:T(8,128)(2,1)S(1)}, u32[]{:S(2)}, u32[]{:S(2)}) collective-permute-start(bf16[12,32,128]{2,1,0:T(8,128)(2,1)S(1)} %get-tuple-element.27), channel_id=1, source_target_pairs={{0,8},{8,0},{16,24},{24,16},{1,9},{9,1},{17,25},{25,17},{2,10},{10... | collective-permute-start | bytes 294920 | tf_op jit(solution)/shard_map/ppermute | solution.py:273

commit v13 on v12

--- a/solution.py
+++ b/solution.py
@@ -48,18 +48,9 @@
 
 
 def pack_kernel(
-    count_hbm, offset_hbm, prolong_hbm, lame_hbm, columns_hbm, owner_hbm,
-    odd_ref, even_ref, prolong_ref, lame_ref, columns_ref, owner_ref,
-    count_ref, offset_ref, sems,
+    count_hbm, offset_hbm, prolong_hbm, odd_ref, even_ref, prolong_ref, count_ref, offset_ref, sems,
 ):
-    copies = fetch(
-        [
-            (prolong_hbm, prolong_ref), (count_hbm, count_ref), (offset_hbm, offset_ref),
-            (lame_hbm, lame_ref), (columns_hbm, columns_ref), (owner_hbm, owner_ref),
-        ],
-        sems,
-    )
-    for copy in copies:
+    for copy in fetch([(prolong_hbm, prolong_ref), (count_hbm, count_ref), (offset_hbm, offset_ref)], sems):
         copy.wait()
     elements = prolong_ref.shape[0]
     odd_row = lax.rem(lax.axis_index("row"), 2)
@@ -80,11 +71,16 @@
 
 
 def left_kernel(
-    capacity, lame_ref, owner_ref, stiffness_hbm, prolong_ref, left_ref, order_ref, stiffness_ref, filled, sems,
+    capacity, lame_hbm, owner_hbm, columns_hbm, stiffness_hbm, prolong_ref, left_ref, order_ref, columns_ref,
+    lame_ref, owner_ref, stiffness_ref, filled, sems,
 ):
     elements, slots, rows, _ = left_ref.shape
     coarse = rows // 2
-    copies = fetch([(stiffness_hbm, stiffness_ref)], sems)
+    copies = fetch(
+        [(owner_hbm, owner_ref), (lame_hbm, lame_ref), (columns_hbm, columns_ref), (stiffness_hbm, stiffness_ref)],
+        sems,
+    )
+    copies[0].wait()
     me = lax.axis_index("grp")
     for t in range(filled.shape[0]):
         filled[t] = 0
@@ -96,8 +92,10 @@
         filled[away] = position + 1
         order_ref[away * capacity + position] = e
 
-    copies[0].wait()
+    for copy in copies[1:]:
+        copy.wait()
     own = prolong_ref[...]
+    spare = jnp.zeros((rows, left_ref.shape[3] - own.shape[1]), jnp.float32)
     for s in range(slots):
         first = jnp.dot(own, stiffness_ref[s, 0], preferred_element_type=jnp.float32)
         second = jnp.dot(own, stiffness_ref[s, 1], preferred_element_type=jnp.float32)
@@ -105,19 +103,22 @@
             part = slice(e * coarse, (e + 1) * coarse)
             total = lame_ref[s, 0, e] * first[part] + lame_ref[s, 1, e] * second[part]
             high = total.astype(jnp.bfloat16).astype(jnp.float32)
-            left_ref[e, s] = jnp.concatenate([high, total - high], axis=0).astype(jnp.bfloat16)
+            both = jnp.concatenate([high, total - high], axis=0)
+            left_ref[e, s] = jnp.concatenate([both, spare], axis=1).astype(jnp.bfloat16)
 
 
 def rows_kernel(columns_ref, order_ref, prolong_ref, even_ref, odd_ref, left_ref, *refs):
     sends, (table, packed) = refs[:-2], refs[-2:]
-    elements, slots, rows, fine = left_ref.shape
-    coarse = rows // 2
+    elements, slots, rows, depth = left_ref.shape
+    coarse, fine = rows // 2, prolong_ref.shape[1]
+    spare = jnp.zeros((coarse, depth - fine), jnp.float32)
     ghosts = 2 * odd_ref.shape[0]
     row, last = lax.axis_index("row"), lax.axis_size("row") - 1
     half = fine - LANES
     capacity = sends[0].shape[0]
     for e in range(elements):
-        table[e] = prolong_ref[e * coarse : (e + 1) * coarse].astype(jnp.float32)
+        own = prolong_ref[e * coarse : (e + 1) * coarse].astype(jnp.float32)
+        table[e] = jnp.concatenate([own, spare], axis=1)
     for parity, ref in enumerate((even_ref, odd_ref)):
         from_above = lax.rem(row, 2) == parity
         start = jnp.where(from_above, elements + ghosts, elements)
@@ -127,9 +128,9 @@
             tail = block[2 * coarse :]
             for odd in range(2):
                 table[start + 2 * pair + odd] = jnp.concatenate(
-                    [block[odd * coarse : (odd + 1) * coarse], tail[:, odd * half : (odd + 1) * half]], axis=1
+                    [block[odd * coarse : (odd + 1) * coarse], tail[:, odd * half : (odd + 1) * half], spare], axis=1
                 )
-    table[elements + 2 * ghosts] = jnp.zeros((coarse, fine), jnp.float32)
+    table[elements + 2 * ghosts] = jnp.zeros((coarse, depth), jnp.float32)
 
     lane8 = lax.broadcasted_iota(jnp.int32, (8, LANES), 1)
     packed[elements] = jnp.concatenate(
@@ -144,7 +145,7 @@
             c = columns_ref[s, e]
             blocks.append(table[jnp.where(c < 0, elements + 2 * ghosts, c)])
         right = jnp.concatenate(blocks, axis=0).astype(jnp.bfloat16)
-        left = left_ref[e].reshape(slots * 2 * coarse, fine)
+        left = left_ref[e].reshape(slots * 2 * coarse, depth)
         product = lax.dot_general(
             left, right, (((1,), (1,)), ((), ())), preferred_element_type=jnp.float32
         )
@@ -218,49 +219,44 @@
     owners = lax.axis_size("grp")
     capacity = 2 * ((elements + owners - 1) // owners)
     run = pltpu.VMEM((ghosts // 2, 3 * coarse, LANES), jnp.bfloat16)
-    by_odd, by_even, own, lame_slots, by_slot, owner = pl.pallas_call(
+    depth = pl.cdiv(fine, 2 * LANES) * 2 * LANES
+    by_odd, by_even, own = pl.pallas_call(
         pack_kernel,
-        out_shape=(
-            run, run,
-            pltpu.VMEM(prolong.shape, jnp.bfloat16),
-            pltpu.SMEM((slots, 2, elements), jnp.float32),
-            pltpu.SMEM((slots, elements), jnp.int32),
-            pltpu.SMEM((1, elements), jnp.int32),
-        ),
-        in_specs=[HBM] * 6, out_specs=(VMEM,) * 3 + (SMEM,) * 3,
+        out_shape=(run, run, pltpu.VMEM(prolong.shape, jnp.bfloat16)),
+        in_specs=[HBM] * 3, out_specs=(VMEM,) * 3,
         scratch_shapes=[
             pltpu.SMEM(ghost_count.shape, jnp.int32),
             pltpu.SMEM(ghost_offset.shape, jnp.int32),
-            pltpu.SemaphoreType.DMA((6,)),
+            pltpu.SemaphoreType.DMA((3,)),
         ],
         compiler_params=params(), name="pack",
-    )(
-        in_hbm(ghost_count), in_hbm(ghost_offset), in_hbm(prolong),
-        in_hbm(lame.transpose(1, 2, 0)), in_hbm(columns.T), in_hbm(owner_map.T),
-    )
+    )(in_hbm(ghost_count), in_hbm(ghost_offset), in_hbm(prolong))
     from_even = swapped(by_even, 0)
     from_odd = swapped(by_odd, 1)
     own = in_vmem(own.reshape(elements * coarse, fine))
-    left, order = pl.pallas_call(
+    left, order, by_slot = pl.pallas_call(
         functools.partial(left_kernel, capacity),
         out_shape=(
-            pltpu.VMEM((elements, slots, 2 * coarse, fine), jnp.bfloat16),
+            pltpu.VMEM((elements, slots, 2 * coarse, depth), jnp.bfloat16),
             pltpu.SMEM((owners * capacity,), jnp.int32),
+            pltpu.SMEM((slots, elements), jnp.int32),
         ),
-        in_specs=[SMEM, SMEM, HBM, VMEM], out_specs=(VMEM, SMEM),
+        in_specs=[HBM] * 4 + [VMEM], out_specs=(VMEM, SMEM, SMEM),
         scratch_shapes=[
+            pltpu.SMEM((slots, 2, elements), jnp.float32),
+            pltpu.SMEM((1, elements), jnp.int32),
             pltpu.VMEM(stiffness.shape, jnp.bfloat16),
             pltpu.SMEM((owners,), jnp.int32),
-            pltpu.SemaphoreType.DMA((1,)),
+            pltpu.SemaphoreType.DMA((4,)),
         ],
         compiler_params=params(), name="left",
-    )(in_smem(lame_slots), in_smem(owner), in_hbm(stiffness), own)
+    )(in_hbm(lame.transpose(1, 2, 0)), in_hbm(owner_map.T), in_hbm(columns.T), in_hbm(stiffness), own)
     sends = pl.pallas_call(
         rows_kernel,
         out_shape=[pltpu.VMEM((capacity, 32, LANES), jnp.bfloat16)] * owners,
         in_specs=[SMEM, SMEM, VMEM, VMEM, VMEM, VMEM], out_specs=[VMEM] * owners,
         scratch_shapes=[
-            pltpu.VMEM((elements + 2 * ghosts + 1, coarse, fine), jnp.float32),
+            pltpu.VMEM((elements + 2 * ghosts + 1, coarse, depth), jnp.float32),
             pltpu.VMEM((elements + 1, 32, LANES), jnp.bfloat16),
         ],
         compiler_params=params(), name="rows",

time: 18.7 us -> 18.7 us (level)
  no operation moved by 1% of the time
where the time goes in v13:
time: 18.7 us; the launch traced here: 18.3 us
  Pallas kernels  6.94 us (37%)
  waiting for transfers between devices  5.71 us (31%)
  starting transfers between devices  5.01 us (27%)
  between operations  0.67 us (4%)
    ppermute x3, waiting for transfers between devices, on_device(): lax.ppermute(sends[k], 'grp', [(i, i ^ k) for i in range(owners)])  3.75 us
    ppermute x3, starting transfers between devices, on_device(): lax.ppermute(sends[k], 'grp', [(i, i ^ k) for i in range(owners)])  3.73 us
    pallas_call x1, Pallas kernels, on_device(): pl.pallas_call(functools.partial(left_kernel, capacity), out_shape=(pltpu...  2.63 us
    ppermute x2, waiting for transfers between devices, swapped(): return lax.ppermute(value, ('grp', 'row'), pairs)  1.96 us
    pallas_call x1, Pallas kernels, on_device(): pl.pallas_call(rows_kernel, out_shape=[pltpu.VMEM((capacity, 32, LANES),...  1.52 us
    ppermute x2, starting transfers between devices, swapped(): return lax.ppermute(value, ('grp', 'row'), pairs)  1.28 us
    pallas_call x1, Pallas kernels, on_device(): pl.pallas_call(pack_kernel, out_shape=(run, run, pltpu.VMEM(prolong.shape...  1.12 us
    pallas_call x1, Pallas kernels, on_device(): pl.pallas_call(functools.partial(unpack_kernel, elements, late, True), ou...  0.84 us
  transfers between devices with their start and end apart: 5, of which 3 were waited for; matrix products, arithmetic and copies ran while one was open for 0% of the time, Pallas kernels for 19%

profile of v13, /device:TPU:9, one launch (start us, length us, event | category | flops | bytes accessed | tf_op | source)
XLA Modules:
  0.0 18.3 jit_solution(5050807078606265748)
XLA Ops:
  0.6 1.1 %pack.1 = (bf16[6,72,128]{2,1,0:T(8,128)(2,1)S(1)}, bf16[6,72,128]{2,1,0:T(8,128)(2,1)S(1)}, bf16[24,24,192]{2,1,0:T(8,128)(2,1)S(1)}) custom-call(s32[1,2]{1,0:T(1,128)} %count_hbm.1, s32[1,2]{1,0:T(1,128)} %offset_hbm.1, bf16[24,24,192]{2,1,0:T(8,128)(2,1)} %prolong_hbm.1), custom_call_target="tpu_custom_call" | custom-call | tf_op jit(solution)/shard_map/pack/pallas_call | solution.py:223
  1.8 1.3 %collective-permute-start = (bf16[6,72,128]{2,1,0:T(8,128)(2,1)S(1)}, bf16[6,72,128]{2,1,0:T(8,128)(2,1)S(1)}, u32[]{:S(2)}, u32[]{:S(2)}) collective-permute-start(bf16[6,72,128]{2,1,0:T(8,128)(2,1)S(1)} %get-tuple-element.19), channel_id=1, source_target_pairs={{0,1},{1,0},{2,3},{3,2},{4,5},{5,4},{6,7},{7,6},{8,9},{9,8},{10,11... | collective-permute-start | bytes 331784 | tf_op jit(solution)/shard_map/ppermute | solution.py:40
  3.0 0.0 collective-permute-start.1
  3.0 2.6 %left.1 = (bf16[24,7,48,256]{3,2,1,0:T(8,128)(2,1)S(1)}, s32[48]{0:T(128)S(4)}, s32[7,24]{1,0:T(8,128)S(4)}) custom-call(f32[7,2,24]{2,1,0:T(2,128)} %bitcast.7, s32[1,24]{1,0:T(1,128)} %bitcast.9, s32[7,24]{1,0:T(8,128)} %bitcast.8, bf16[7,2,192,192]{3,2,1,0:T(8,128)(2,1)} %stiffness_hbm.1, bf16[576,192]{1,0:T(8,128)(2,1)S(1)} %bitcast.5), custom_call_target="tpu_custom_call" | custom-call | tf_op jit(solution)/shard_map/left/pallas_call | solution.py:237
  5.7 0.1 collective-permute-done.even_ref
  5.8 1.9 %collective-permute-done.1.odd_ref = bf16[6,72,128]{2,1,0:T(8,128)(2,1)S(1)} collective-permute-done((bf16[6,72,128]{2,1,0:T(8,128)(2,1)S(1)}, bf16[6,72,128]{2,1,0:T(8,128)(2,1)S(1)}, u32[]{:S(2)}, u32[]{:S(2)}) %collective-permute-start.1) | collective-permute-done | bytes 110624 | tf_op jit(solution)/shard_map/ppermute | solution.py:40
  7.6 1.5 %rows.1 = (bf16[12,32,128]{2,1,0:T(8,128)(2,1)S(1)}, bf16[12,32,128]{2,1,0:T(8,128)(2,1)S(1)}, bf16[12,32,128]{2,1,0:T(8,128)(2,1)S(1)}, bf16[12,32,128]{2,1,0:T(8,128)(2,1)S(1)}) custom-call(s32[7,24]{1,0:T(8,128)S(4)} %get-tuple-element.17.columns_ref, s32[48]{0:T(128)S(4)} %get-tuple-element.18.order_ref, bf16[576,192]{1,0:T(8,128)(2,1)S(1)} %bitcast.6, ...), custom_call_target="tpu_custom_call" | custom-call | tf_op jit(solution)/shard_map/rows/pallas_call | solution.py:254
  9.2 1.3 %collective-permute-start.4 = (bf16[12,32,128]{2,1,0:T(8,128)(2,1)S(1)}, bf16[12,32,128]{2,1,0:T(8,128)(2,1)S(1)}, u32[]{:S(2)}, u32[]{:S(2)}) collective-permute-start(bf16[12,32,128]{2,1,0:T(8,128)(2,1)S(1)} %get-tuple-element.24), channel_id=1, source_target_pairs={{0,16},{8,24},{16,0},{24,8},{1,17},{9,25},{17,1},{25,9},{2,18},{10... | collective-permute-start | bytes 294920 | tf_op jit(solution)/shard_map/ppermute | solution.py:269
  10.5 2.4 %collective-permute-start.2 = (bf16[12,32,128]{2,1,0:T(8,128)(2,1)S(1)}, bf16[12,32,128]{2,1,0:T(8,128)(2,1)S(1)}, u32[]{:S(2)}, u32[]{:S(2)}) collective-permute-start(bf16[12,32,128]{2,1,0:T(8,128)(2,1)S(1)} %get-tuple-element.22), channel_id=1, source_target_pairs={{0,24},{8,16},{16,8},{24,0},{1,25},{9,17},{17,9},{25,1},{2,26},{10... | collective-permute-start | bytes 294920 | tf_op jit(solution)/shard_map/ppermute | solution.py:269
  12.9 0.0 collective-permute-start.3
  12.9 0.0 collective-permute-done.4.refs_0_
  12.9 0.8 %unpack_early.1 = (bf16[48,24,168]{2,1,0:T(8,128)(2,1)}, f32[8,128]{1,0:T(8,128)S(1)}) custom-call(bf16[12,32,128]{2,1,0:T(8,128)(2,1)S(1)} %collective-permute-done.4.refs_0_, bf16[12,32,128]{2,1,0:T(8,128)(2,1)S(1)} %get-tuple-element.25.refs_1_), custom_call_target="tpu_custom_call" | custom-call | tf_op jit(solution)/shard_map/unpack_early/pallas_call | solution.py:278
  13.7 3.7 %collective-permute-done.2.refs_0_ = bf16[12,32,128]{2,1,0:T(8,128)(2,1)S(1)} collective-permute-done((bf16[12,32,128]{2,1,0:T(8,128)(2,1)S(1)}, bf16[12,32,128]{2,1,0:T(8,128)(2,1)S(1)}, u32[]{:S(2)}, u32[]{:S(2)}) %collective-permute-start.2) | collective-permute-done | bytes 98336 | tf_op jit(solution)/shard_map/ppermute | solution.py:269
  17.5 0.0 collective-permute-done.3.refs_1_
  17.5 0.8 %unpack_late.1 = (bf16[48,24,168]{2,1,0:T(8,128)(2,1)}, s32[1,48]{1,0:T(1,128)}) custom-call(bf16[12,32,128]{2,1,0:T(8,128)(2,1)S(1)} %collective-permute-done.2.refs_0_, bf16[12,32,128]{2,1,0:T(8,128)(2,1)S(1)} %collective-permute-done.3.refs_1_, bf16[48,24,168]{2,1,0:T(8,128)(2,1)} %get-tuple-element.26.refs_2_, ...), custom_call_target="tpu_custom_call", output_to_operand_aliasing={{0}: (2, {})} | custom-call | tf_op jit(solution)/shard_map/unpack_late/pallas_call | solution.py:285
Async XLA Ops:
  1.8 4.0 %collective-permute-start = (bf16[6,72,128]{2,1,0:T(8,128)(2,1)S(1)}, bf16[6,72,128]{2,1,0:T(8,128)(2,1)S(1)}, u32[]{:S(2)}, u32[]{:S(2)}) collective-permute-start(bf16[6,72,128]{2,1,0:T(8,128)(2,1)S(1)} %get-tuple-element.19), channel_id=1, source_target_pairs={{0,1},{1,0},{2,3},{3,2},{4,5},{5,4},{6,7},{7,6},{8,9},{9,8},{10,11... | collective-permute-start | bytes 331784 | tf_op jit(solution)/shard_map/ppermute | solution.py:40
  3.0 4.6 %collective-permute-start.1 = (bf16[6,72,128]{2,1,0:T(8,128)(2,1)S(1)}, bf16[6,72,128]{2,1,0:T(8,128)(2,1)S(1)}, u32[]{:S(2)}, u32[]{:S(2)}) collective-permute-start(bf16[6,72,128]{2,1,0:T(8,128)(2,1)S(1)} %get-tuple-element.20), channel_id=1, source_target_pairs={{0,8},{1,2},{2,1},{3,4},{4,3},{5,6},{6,5},{7,15},{8,0},{9,10},{10,... | collective-permute-start | bytes 331784 | tf_op jit(solution)/shard_map/ppermute | solution.py:40
  9.2 3.7 %collective-permute-start.4 = (bf16[12,32,128]{2,1,0:T(8,128)(2,1)S(1)}, bf16[12,32,128]{2,1,0:T(8,128)(2,1)S(1)}, u32[]{:S(2)}, u32[]{:S(2)}) collective-permute-start(bf16[12,32,128]{2,1,0:T(8,128)(2,1)S(1)} %get-tuple-element.24), channel_id=1, source_target_pairs={{0,16},{8,24},{16,0},{24,8},{1,17},{9,25},{17,1},{25,9},{2,18},{10... | collective-permute-start | bytes 294920 | tf_op jit(solution)/shard_map/ppermute | solution.py:269
  10.5 7.0 %collective-permute-start.2 = (bf16[12,32,128]{2,1,0:T(8,128)(2,1)S(1)}, bf16[12,32,128]{2,1,0:T(8,128)(2,1)S(1)}, u32[]{:S(2)}, u32[]{:S(2)}) collective-permute-start(bf16[12,32,128]{2,1,0:T(8,128)(2,1)S(1)} %get-tuple-element.22), channel_id=1, source_target_pairs={{0,24},{8,16},{16,8},{24,0},{1,25},{9,17},{17,9},{25,1},{2,26},{10... | collective-permute-start | bytes 294920 | tf_op jit(solution)/shard_map/ppermute | solution.py:269
  12.9 4.6 %collective-permute-start.3 = (bf16[12,32,128]{2,1,0:T(8,128)(2,1)S(1)}, bf16[12,32,128]{2,1,0:T(8,128)(2,1)S(1)}, u32[]{:S(2)}, u32[]{:S(2)}) collective-permute-start(bf16[12,32,128]{2,1,0:T(8,128)(2,1)S(1)} %get-tuple-element.23), channel_id=1, source_target_pairs={{0,8},{8,0},{16,24},{24,16},{1,9},{9,1},{17,25},{25,17},{2,10},{10... | collective-permute-start | bytes 294920 | tf_op jit(solution)/shard_map/ppermute | solution.py:269

commit v14 on v13

--- a/solution.py
+++ b/solution.py
@@ -71,7 +71,7 @@
 
 
 def left_kernel(
-    capacity, lame_hbm, owner_hbm, columns_hbm, stiffness_hbm, prolong_ref, left_ref, order_ref, columns_ref,
+    capacity, lame_hbm, owner_hbm, columns_hbm, stiffness_hbm, prolong_ref, left_ref, order_ref, columns_ref, table_ref,
     lame_ref, owner_ref, stiffness_ref, filled, sems,
 ):
     elements, slots, rows, _ = left_ref.shape
@@ -96,6 +96,10 @@
         copy.wait()
     own = prolong_ref[...]
     spare = jnp.zeros((rows, left_ref.shape[3] - own.shape[1]), jnp.float32)
+    for e in range(elements):
+        block = own[e * coarse : (e + 1) * coarse].astype(jnp.float32)
+        table_ref[e] = jnp.concatenate([block, spare[:coarse]], axis=1)
+    table_ref[table_ref.shape[0] - 1] = jnp.zeros(table_ref.shape[1:], jnp.float32)
     for s in range(slots):
         first = jnp.dot(own, stiffness_ref[s, 0], preferred_element_type=jnp.float32)
         second = jnp.dot(own, stiffness_ref[s, 1], preferred_element_type=jnp.float32)
@@ -107,18 +111,15 @@
             left_ref[e, s] = jnp.concatenate([both, spare], axis=1).astype(jnp.bfloat16)
 
 
-def rows_kernel(columns_ref, order_ref, prolong_ref, even_ref, odd_ref, left_ref, *refs):
+def rows_kernel(columns_ref, order_ref, even_ref, odd_ref, left_ref, _, *refs):
     sends, (table, packed) = refs[:-2], refs[-2:]
     elements, slots, rows, depth = left_ref.shape
-    coarse, fine = rows // 2, prolong_ref.shape[1]
-    spare = jnp.zeros((coarse, depth - fine), jnp.float32)
+    coarse = rows // 2
+    half = LANES // 2
+    spare = jnp.zeros((coarse, depth - LANES - half), jnp.float32)
     ghosts = 2 * odd_ref.shape[0]
     row, last = lax.axis_index("row"), lax.axis_size("row") - 1
-    half = fine - LANES
     capacity = sends[0].shape[0]
-    for e in range(elements):
-        own = prolong_ref[e * coarse : (e + 1) * coarse].astype(jnp.float32)
-        table[e] = jnp.concatenate([own, spare], axis=1)
     for parity, ref in enumerate((even_ref, odd_ref)):
         from_above = lax.rem(row, 2) == parity
         start = jnp.where(from_above, elements + ghosts, elements)
@@ -130,7 +131,6 @@
                 table[start + 2 * pair + odd] = jnp.concatenate(
                     [block[odd * coarse : (odd + 1) * coarse], tail[:, odd * half : (odd + 1) * half], spare], axis=1
                 )
-    table[elements + 2 * ghosts] = jnp.zeros((coarse, depth), jnp.float32)
 
     lane8 = lax.broadcasted_iota(jnp.int32, (8, LANES), 1)
     packed[elements] = jnp.concatenate(
@@ -234,14 +234,16 @@
     from_even = swapped(by_even, 0)
     from_odd = swapped(by_odd, 1)
     own = in_vmem(own.reshape(elements * coarse, fine))
-    left, order, by_slot = pl.pallas_call(
+    table = pltpu.VMEM((elements + 2 * ghosts + 1, coarse, depth), jnp.float32)
+    left, order, by_slot, local_table = pl.pallas_call(
         functools.partial(left_kernel, capacity),
         out_shape=(
             pltpu.VMEM((elements, slots, 2 * coarse, depth), jnp.bfloat16),
             pltpu.SMEM((owners * capacity,), jnp.int32),
             pltpu.SMEM((slots, elements), jnp.int32),
+            table,
         ),
-        in_specs=[HBM] * 4 + [VMEM], out_specs=(VMEM, SMEM, SMEM),
+        in_specs=[HBM] * 4 + [VMEM], out_specs=(VMEM, SMEM, SMEM, VMEM),
         scratch_shapes=[
             pltpu.SMEM((slots, 2, elements), jnp.float32),
             pltpu.SMEM((1, elements), jnp.int32),
@@ -251,18 +253,15 @@
         ],
         compiler_params=params(), name="left",
     )(in_hbm(lame.transpose(1, 2, 0)), in_hbm(owner_map.T), in_hbm(columns.T), in_hbm(stiffness), own)
-    sends = pl.pallas_call(
+    *sends, _ = pl.pallas_call(
         rows_kernel,
-        out_shape=[pltpu.VMEM((capacity, 32, LANES), jnp.bfloat16)] * owners,
-        in_specs=[SMEM, SMEM, VMEM, VMEM, VMEM, VMEM], out_specs=[VMEM] * owners,
-        scratch_shapes=[
-            pltpu.VMEM((elements + 2 * ghosts + 1, coarse, depth), jnp.float32),
-            pltpu.VMEM((elements + 1, 32, LANES), jnp.bfloat16),
-        ],
+        out_shape=[pltpu.VMEM((capacity, 32, LANES), jnp.bfloat16)] * owners + [table],
+        in_specs=[SMEM, SMEM, VMEM, VMEM, VMEM, VMEM], out_specs=[VMEM] * (owners + 1),
+        scratch_shapes=[pltpu.VMEM((elements + 1, 32, LANES), jnp.bfloat16)],
+        input_output_aliases={5: owners},
         compiler_params=params(), name="rows",
     )(
-        in_smem(by_slot), in_smem(order), own,
-        in_vmem(from_even), in_vmem(from_odd), in_vmem(left),
+        in_smem(by_slot), in_smem(order), in_vmem(from_even), in_vmem(from_odd), in_vmem(left), in_vmem(local_table),
     )
     received = {0: sends[0]}
     for k in [*range(2, owners), 1]:

time: 18.7 us -> 18.7 us (level)
  no operation moved by 1% of the time
where the time goes in v14:
time: 18.7 us; the launch traced here: 18.3 us
  Pallas kernels  6.96 us (37%)
  waiting for transfers between devices  5.69 us (30%)
  starting transfers between devices  5.01 us (27%)
  between operations  0.67 us (4%)
    ppermute x3, waiting for transfers between devices, on_device(): lax.ppermute(sends[k], 'grp', [(i, i ^ k) for i in range(owners)])  3.73 us
    ppermute x3, starting transfers between devices, on_device(): lax.ppermute(sends[k], 'grp', [(i, i ^ k) for i in range(owners)])  3.73 us
    pallas_call x1, Pallas kernels, on_device(): pl.pallas_call(functools.partial(left_kernel, capacity), out_shape=(pltpu...  2.64 us
    ppermute x2, waiting for transfers between devices, swapped(): return lax.ppermute(value, ('grp', 'row'), pairs)  1.95 us
    pallas_call x1, Pallas kernels, on_device(): pl.pallas_call(rows_kernel, out_shape=[pltpu.VMEM((capacity, 32, LANES),...  1.54 us
    ppermute x2, starting transfers between devices, swapped(): return lax.ppermute(value, ('grp', 'row'), pairs)  1.28 us
    pallas_call x1, Pallas kernels, on_device(): pl.pallas_call(pack_kernel, out_shape=(run, run, pltpu.VMEM(prolong.shape...  1.12 us
    pallas_call x1, Pallas kernels, on_device(): pl.pallas_call(functools.partial(unpack_kernel, elements, late, True), ou...  0.84 us
  transfers between devices with their start and end apart: 5, of which 3 were waited for; matrix products, arithmetic and copies ran while one was open for 0% of the time, Pallas kernels for 19%

profile of v14, /device:TPU:9, one launch (start us, length us, event | category | flops | bytes accessed | tf_op | source)
XLA Modules:
  0.0 18.3 jit_solution(2939323146415976996)
XLA Ops:
  0.6 1.1 %pack.1 = (bf16[6,72,128]{2,1,0:T(8,128)(2,1)S(1)}, bf16[6,72,128]{2,1,0:T(8,128)(2,1)S(1)}, bf16[24,24,192]{2,1,0:T(8,128)(2,1)S(1)}) custom-call(s32[1,2]{1,0:T(1,128)} %count_hbm.1, s32[1,2]{1,0:T(1,128)} %offset_hbm.1, bf16[24,24,192]{2,1,0:T(8,128)(2,1)} %prolong_hbm.1), custom_call_target="tpu_custom_call" | custom-call | tf_op jit(solution)/shard_map/pack/pallas_call | solution.py:223
  1.8 1.3 %collective-permute-start = (bf16[6,72,128]{2,1,0:T(8,128)(2,1)S(1)}, bf16[6,72,128]{2,1,0:T(8,128)(2,1)S(1)}, u32[]{:S(2)}, u32[]{:S(2)}) collective-permute-start(bf16[6,72,128]{2,1,0:T(8,128)(2,1)S(1)} %get-tuple-element.20), channel_id=1, source_target_pairs={{0,1},{1,0},{2,3},{3,2},{4,5},{5,4},{6,7},{7,6},{8,9},{9,8},{10,11... | collective-permute-start | bytes 331784 | tf_op jit(solution)/shard_map/ppermute | solution.py:40
  3.0 0.0 collective-permute-start.1
  3.0 2.6 %left.1 = (bf16[24,7,48,256]{3,2,1,0:T(8,128)(2,1)S(1)}, s32[48]{0:T(128)S(4)}, s32[7,24]{1,0:T(8,128)S(4)}, f32[49,24,256]{2,1,0:T(8,128)S(1)}) custom-call(f32[7,2,24]{2,1,0:T(2,128)} %bitcast.6, s32[1,24]{1,0:T(1,128)} %bitcast.8, s32[7,24]{1,0:T(8,128)} %bitcast.7, bf16[7,2,192,192]{3,2,1,0:T(8,128)(2,1)} %stiffness_hbm.1, bf16[576,192]{1,0:T(8,128)(2,1)S(1)} %bitcast.5), custom_call_target="tpu_custom_call" | custom-call | tf_op jit(solution)/shard_map/left/pallas_call | solution.py:238
  5.7 0.1 collective-permute-done.even_ref
  5.8 1.9 %collective-permute-done.1.odd_ref = bf16[6,72,128]{2,1,0:T(8,128)(2,1)S(1)} collective-permute-done((bf16[6,72,128]{2,1,0:T(8,128)(2,1)S(1)}, bf16[6,72,128]{2,1,0:T(8,128)(2,1)S(1)}, u32[]{:S(2)}, u32[]{:S(2)}) %collective-permute-start.1) | collective-permute-done | bytes 110624 | tf_op jit(solution)/shard_map/ppermute | solution.py:40
  7.6 1.5 %rows.1 = (bf16[12,32,128]{2,1,0:T(8,128)(2,1)S(1)}, bf16[12,32,128]{2,1,0:T(8,128)(2,1)S(1)}, bf16[12,32,128]{2,1,0:T(8,128)(2,1)S(1)}, bf16[12,32,128]{2,1,0:T(8,128)(2,1)S(1)}, f32[49,24,256]{2,1,0:T(8,128)S(1)}) custom-call(s32[7,24]{1,0:T(8,128)S(4)} %get-tuple-element.18.columns_ref, ...), custom_call_target="tpu_custom_call", output_to_operand_aliasing={{4}: (5, {})} | custom-call | tf_op jit(solution)/shard_map/rows/pallas_call | solution.py:256
  9.2 1.3 %collective-permute-start.4 = (bf16[12,32,128]{2,1,0:T(8,128)(2,1)S(1)}, bf16[12,32,128]{2,1,0:T(8,128)(2,1)S(1)}, u32[]{:S(2)}, u32[]{:S(2)}) collective-permute-start(bf16[12,32,128]{2,1,0:T(8,128)(2,1)S(1)} %get-tuple-element.26), channel_id=1, source_target_pairs={{0,16},{8,24},{16,0},{24,8},{1,17},{9,25},{17,1},{25,9},{2,18},{10... | collective-permute-start | bytes 294920 | tf_op jit(solution)/shard_map/ppermute | solution.py:268
  10.5 2.4 %collective-permute-start.2 = (bf16[12,32,128]{2,1,0:T(8,128)(2,1)S(1)}, bf16[12,32,128]{2,1,0:T(8,128)(2,1)S(1)}, u32[]{:S(2)}, u32[]{:S(2)}) collective-permute-start(bf16[12,32,128]{2,1,0:T(8,128)(2,1)S(1)} %get-tuple-element.24), channel_id=1, source_target_pairs={{0,24},{8,16},{16,8},{24,0},{1,25},{9,17},{17,9},{25,1},{2,26},{10... | collective-permute-start | bytes 294920 | tf_op jit(solution)/shard_map/ppermute | solution.py:268
  12.9 0.0 collective-permute-start.3
  12.9 0.0 collective-permute-done.4.refs_0_
  12.9 0.8 %unpack_early.1 = (bf16[48,24,168]{2,1,0:T(8,128)(2,1)}, f32[8,128]{1,0:T(8,128)S(1)}) custom-call(bf16[12,32,128]{2,1,0:T(8,128)(2,1)S(1)} %collective-permute-done.4.refs_0_, bf16[12,32,128]{2,1,0:T(8,128)(2,1)S(1)} %get-tuple-element.27.refs_1_), custom_call_target="tpu_custom_call" | custom-call | tf_op jit(solution)/shard_map/unpack_early/pallas_call | solution.py:277
  13.8 3.7 %collective-permute-done.2.refs_0_ = bf16[12,32,128]{2,1,0:T(8,128)(2,1)S(1)} collective-permute-done((bf16[12,32,128]{2,1,0:T(8,128)(2,1)S(1)}, bf16[12,32,128]{2,1,0:T(8,128)(2,1)S(1)}, u32[]{:S(2)}, u32[]{:S(2)}) %collective-permute-start.2) | collective-permute-done | bytes 98336 | tf_op jit(solution)/shard_map/ppermute | solution.py:268
  17.5 0.0 collective-permute-done.3.refs_1_
  17.5 0.8 %unpack_late.1 = (bf16[48,24,168]{2,1,0:T(8,128)(2,1)}, s32[1,48]{1,0:T(1,128)}) custom-call(bf16[12,32,128]{2,1,0:T(8,128)(2,1)S(1)} %collective-permute-done.2.refs_0_, bf16[12,32,128]{2,1,0:T(8,128)(2,1)S(1)} %collective-permute-done.3.refs_1_, bf16[48,24,168]{2,1,0:T(8,128)(2,1)} %get-tuple-element.28.refs_2_, ...), custom_call_target="tpu_custom_call", output_to_operand_aliasing={{0}: (2, {})} | custom-call | tf_op jit(solution)/shard_map/unpack_late/pallas_call | solution.py:284
Async XLA Ops:
  1.8 4.0 %collective-permute-start = (bf16[6,72,128]{2,1,0:T(8,128)(2,1)S(1)}, bf16[6,72,128]{2,1,0:T(8,128)(2,1)S(1)}, u32[]{:S(2)}, u32[]{:S(2)}) collective-permute-start(bf16[6,72,128]{2,1,0:T(8,128)(2,1)S(1)} %get-tuple-element.20), channel_id=1, source_target_pairs={{0,1},{1,0},{2,3},{3,2},{4,5},{5,4},{6,7},{7,6},{8,9},{9,8},{10,11... | collective-permute-start | bytes 331784 | tf_op jit(solution)/shard_map/ppermute | solution.py:40
  3.0 4.6 %collective-permute-start.1 = (bf16[6,72,128]{2,1,0:T(8,128)(2,1)S(1)}, bf16[6,72,128]{2,1,0:T(8,128)(2,1)S(1)}, u32[]{:S(2)}, u32[]{:S(2)}) collective-permute-start(bf16[6,72,128]{2,1,0:T(8,128)(2,1)S(1)} %get-tuple-element.21), channel_id=1, source_target_pairs={{0,8},{1,2},{2,1},{3,4},{4,3},{5,6},{6,5},{7,15},{8,0},{9,10},{10,... | collective-permute-start | bytes 331784 | tf_op jit(solution)/shard_map/ppermute | solution.py:40
  9.2 3.7 %collective-permute-start.4 = (bf16[12,32,128]{2,1,0:T(8,128)(2,1)S(1)}, bf16[12,32,128]{2,1,0:T(8,128)(2,1)S(1)}, u32[]{:S(2)}, u32[]{:S(2)}) collective-permute-start(bf16[12,32,128]{2,1,0:T(8,128)(2,1)S(1)} %get-tuple-element.26), channel_id=1, source_target_pairs={{0,16},{8,24},{16,0},{24,8},{1,17},{9,25},{17,1},{25,9},{2,18},{10... | collective-permute-start | bytes 294920 | tf_op jit(solution)/shard_map/ppermute | solution.py:268
  10.5 7.0 %collective-permute-start.2 = (bf16[12,32,128]{2,1,0:T(8,128)(2,1)S(1)}, bf16[12,32,128]{2,1,0:T(8,128)(2,1)S(1)}, u32[]{:S(2)}, u32[]{:S(2)}) collective-permute-start(bf16[12,32,128]{2,1,0:T(8,128)(2,1)S(1)} %get-tuple-element.24), channel_id=1, source_target_pairs={{0,24},{8,16},{16,8},{24,0},{1,25},{9,17},{17,9},{25,1},{2,26},{10... | collective-permute-start | bytes 294920 | tf_op jit(solution)/shard_map/ppermute | solution.py:268
  12.9 4.6 %collective-permute-start.3 = (bf16[12,32,128]{2,1,0:T(8,128)(2,1)S(1)}, bf16[12,32,128]{2,1,0:T(8,128)(2,1)S(1)}, u32[]{:S(2)}, u32[]{:S(2)}) collective-permute-start(bf16[12,32,128]{2,1,0:T(8,128)(2,1)S(1)} %get-tuple-element.25), channel_id=1, source_target_pairs={{0,8},{8,0},{16,24},{24,16},{1,9},{9,1},{17,25},{25,17},{2,10},{10... | collective-permute-start | bytes 294920 | tf_op jit(solution)/shard_map/ppermute | solution.py:268

commit v15 on v14

--- a/solution.py
+++ b/solution.py
@@ -149,15 +149,19 @@
         product = lax.dot_general(
             left, right, (((1,), (1,)), ((), ())), preferred_element_type=jnp.float32
         )
-        result = None
-        for s in range(slots):
-            at = 2 * coarse * s
-            part = product[at : at + coarse] + product[at + coarse : at + 2 * coarse]
-            result = part if s == 0 else jnp.where(lane >= s * coarse, part, result)
-        rest = result[:, LANES:]
+        sides = []
+        for side in (slice(0, LANES), slice(LANES, width)):
+            result = None
+            for s in range(slots):
+                if s * coarse < side.stop and (s + 1) * coarse > side.start:
+                    at = 2 * coarse * s
+                    part = product[at : at + coarse, side] + product[at + coarse : at + 2 * coarse, side]
+                    result = part if result is None else jnp.where(lane[:, side] >= s * coarse, part, result)
+            sides.append(result)
+        rest = sides[1]
         spare = jnp.full((8, 8), e, jnp.float32)
         tail = jnp.concatenate([rest[0:8], rest[8:16], rest[16:24], spare], axis=1)
-        packed[e] = jnp.concatenate([result[:, :LANES], tail], axis=0).astype(jnp.bfloat16)
+        packed[e] = jnp.concatenate([sides[0], tail], axis=0).astype(jnp.bfloat16)
     for k, send in enumerate(sends):
         for p in range(capacity):
             send[p] = packed[order_ref[k * capacity + p]]

time: 18.7 us -> 18.7 us (level)
  no operation moved by 1% of the time
where the time goes in v15:
time: 18.7 us; the launch traced here: 18.3 us
  Pallas kernels  6.95 us (37%)
  waiting for transfers between devices  5.7 us (30%)
  starting transfers between devices  5.01 us (27%)
  between operations  0.67 us (4%)
    ppermute x3, waiting for transfers between devices, on_device(): lax.ppermute(sends[k], 'grp', [(i, i ^ k) for i in range(owners)])  3.75 us
    ppermute x3, starting transfers between devices, on_device(): lax.ppermute(sends[k], 'grp', [(i, i ^ k) for i in range(owners)])  3.73 us
    pallas_call x1, Pallas kernels, on_device(): pl.pallas_call(functools.partial(left_kernel, capacity), out_shape=(pltpu...  2.64 us
    ppermute x2, waiting for transfers between devices, swapped(): return lax.ppermute(value, ('grp', 'row'), pairs)  1.95 us
    pallas_call x1, Pallas kernels, on_device(): pl.pallas_call(rows_kernel, out_shape=[pltpu.VMEM((capacity, 32, LANES),...  1.53 us
    ppermute x2, starting transfers between devices, swapped(): return lax.ppermute(value, ('grp', 'row'), pairs)  1.28 us
    pallas_call x1, Pallas kernels, on_device(): pl.pallas_call(pack_kernel, out_shape=(run, run, pltpu.VMEM(prolong.shape...  1.12 us
    pallas_call x1, Pallas kernels, on_device(): pl.pallas_call(functools.partial(unpack_kernel, elements, late, True), ou...  0.84 us
  transfers between devices with their start and end apart: 5, of which 3 were waited for; matrix products, arithmetic and copies ran while one was open for 0% of the time, Pallas kernels for 19%

profile of v15, /device:TPU:9, one launch (start us, length us, event | category | flops | bytes accessed | tf_op | source)
XLA Modules:
  0.0 18.3 jit_solution(2939323146415976996)
XLA Ops:
  0.6 1.1 %pack.1 = (bf16[6,72,128]{2,1,0:T(8,128)(2,1)S(1)}, bf16[6,72,128]{2,1,0:T(8,128)(2,1)S(1)}, bf16[24,24,192]{2,1,0:T(8,128)(2,1)S(1)}) custom-call(s32[1,2]{1,0:T(1,128)} %count_hbm.1, s32[1,2]{1,0:T(1,128)} %offset_hbm.1, bf16[24,24,192]{2,1,0:T(8,128)(2,1)} %prolong_hbm.1), custom_call_target="tpu_custom_call" | custom-call | tf_op jit(solution)/shard_map/pack/pallas_call | solution.py:227
  1.8 1.3 %collective-permute-start = (bf16[6,72,128]{2,1,0:T(8,128)(2,1)S(1)}, bf16[6,72,128]{2,1,0:T(8,128)(2,1)S(1)}, u32[]{:S(2)}, u32[]{:S(2)}) collective-permute-start(bf16[6,72,128]{2,1,0:T(8,128)(2,1)S(1)} %get-tuple-element.20), channel_id=1, source_target_pairs={{0,1},{1,0},{2,3},{3,2},{4,5},{5,4},{6,7},{7,6},{8,9},{9,8},{10,11... | collective-permute-start | bytes 331784 | tf_op jit(solution)/shard_map/ppermute | solution.py:40
  3.0 0.0 collective-permute-start.1
  3.0 2.6 %left.1 = (bf16[24,7,48,256]{3,2,1,0:T(8,128)(2,1)S(1)}, s32[48]{0:T(128)S(4)}, s32[7,24]{1,0:T(8,128)S(4)}, f32[49,24,256]{2,1,0:T(8,128)S(1)}) custom-call(f32[7,2,24]{2,1,0:T(2,128)} %bitcast.6, s32[1,24]{1,0:T(1,128)} %bitcast.8, s32[7,24]{1,0:T(8,128)} %bitcast.7, bf16[7,2,192,192]{3,2,1,0:T(8,128)(2,1)} %stiffness_hbm.1, bf16[576,192]{1,0:T(8,128)(2,1)S(1)} %bitcast.5), custom_call_target="tpu_custom_call" | custom-call | tf_op jit(solution)/shard_map/left/pallas_call | solution.py:242
  5.7 0.1 collective-permute-done.even_ref
  5.8 1.9 %collective-permute-done.1.odd_ref = bf16[6,72,128]{2,1,0:T(8,128)(2,1)S(1)} collective-permute-done((bf16[6,72,128]{2,1,0:T(8,128)(2,1)S(1)}, bf16[6,72,128]{2,1,0:T(8,128)(2,1)S(1)}, u32[]{:S(2)}, u32[]{:S(2)}) %collective-permute-start.1) | collective-permute-done | bytes 110624 | tf_op jit(solution)/shard_map/ppermute | solution.py:40
  7.6 1.5 %rows.1 = (bf16[12,32,128]{2,1,0:T(8,128)(2,1)S(1)}, bf16[12,32,128]{2,1,0:T(8,128)(2,1)S(1)}, bf16[12,32,128]{2,1,0:T(8,128)(2,1)S(1)}, bf16[12,32,128]{2,1,0:T(8,128)(2,1)S(1)}, f32[49,24,256]{2,1,0:T(8,128)S(1)}) custom-call(s32[7,24]{1,0:T(8,128)S(4)} %get-tuple-element.18.columns_ref, ...), custom_call_target="tpu_custom_call", output_to_operand_aliasing={{4}: (5, {})} | custom-call | tf_op jit(solution)/shard_map/rows/pallas_call | solution.py:260
  9.2 1.3 %collective-permute-start.4 = (bf16[12,32,128]{2,1,0:T(8,128)(2,1)S(1)}, bf16[12,32,128]{2,1,0:T(8,128)(2,1)S(1)}, u32[]{:S(2)}, u32[]{:S(2)}) collective-permute-start(bf16[12,32,128]{2,1,0:T(8,128)(2,1)S(1)} %get-tuple-element.26), channel_id=1, source_target_pairs={{0,16},{8,24},{16,0},{24,8},{1,17},{9,25},{17,1},{25,9},{2,18},{10... | collective-permute-start | bytes 294920 | tf_op jit(solution)/shard_map/ppermute | solution.py:272
  10.5 2.4 %collective-permute-start.2 = (bf16[12,32,128]{2,1,0:T(8,128)(2,1)S(1)}, bf16[12,32,128]{2,1,0:T(8,128)(2,1)S(1)}, u32[]{:S(2)}, u32[]{:S(2)}) collective-permute-start(bf16[12,32,128]{2,1,0:T(8,128)(2,1)S(1)} %get-tuple-element.24), channel_id=1, source_target_pairs={{0,24},{8,16},{16,8},{24,0},{1,25},{9,17},{17,9},{25,1},{2,26},{10... | collective-permute-start | bytes 294920 | tf_op jit(solution)/shard_map/ppermute | solution.py:272
  12.9 0.0 collective-permute-start.3
  12.9 0.0 collective-permute-done.4.refs_0_
  12.9 0.8 %unpack_early.1 = (bf16[48,24,168]{2,1,0:T(8,128)(2,1)}, f32[8,128]{1,0:T(8,128)S(1)}) custom-call(bf16[12,32,128]{2,1,0:T(8,128)(2,1)S(1)} %collective-permute-done.4.refs_0_, bf16[12,32,128]{2,1,0:T(8,128)(2,1)S(1)} %get-tuple-element.27.refs_1_), custom_call_target="tpu_custom_call" | custom-call | tf_op jit(solution)/shard_map/unpack_early/pallas_call | solution.py:281
  13.7 3.7 %collective-permute-done.2.refs_0_ = bf16[12,32,128]{2,1,0:T(8,128)(2,1)S(1)} collective-permute-done((bf16[12,32,128]{2,1,0:T(8,128)(2,1)S(1)}, bf16[12,32,128]{2,1,0:T(8,128)(2,1)S(1)}, u32[]{:S(2)}, u32[]{:S(2)}) %collective-permute-start.2) | collective-permute-done | bytes 98336 | tf_op jit(solution)/shard_map/ppermute | solution.py:272
  17.5 0.0 collective-permute-done.3.refs_1_
  17.5 0.8 %unpack_late.1 = (bf16[48,24,168]{2,1,0:T(8,128)(2,1)}, s32[1,48]{1,0:T(1,128)}) custom-call(bf16[12,32,128]{2,1,0:T(8,128)(2,1)S(1)} %collective-permute-done.2.refs_0_, bf16[12,32,128]{2,1,0:T(8,128)(2,1)S(1)} %collective-permute-done.3.refs_1_, bf16[48,24,168]{2,1,0:T(8,128)(2,1)} %get-tuple-element.28.refs_2_, ...), custom_call_target="tpu_custom_call", output_to_operand_aliasing={{0}: (2, {})} | custom-call | tf_op jit(solution)/shard_map/unpack_late/pallas_call | solution.py:288
Async XLA Ops:
  1.8 4.0 %collective-permute-start = (bf16[6,72,128]{2,1,0:T(8,128)(2,1)S(1)}, bf16[6,72,128]{2,1,0:T(8,128)(2,1)S(1)}, u32[]{:S(2)}, u32[]{:S(2)}) collective-permute-start(bf16[6,72,128]{2,1,0:T(8,128)(2,1)S(1)} %get-tuple-element.20), channel_id=1, source_target_pairs={{0,1},{1,0},{2,3},{3,2},{4,5},{5,4},{6,7},{7,6},{8,9},{9,8},{10,11... | collective-permute-start | bytes 331784 | tf_op jit(solution)/shard_map/ppermute | solution.py:40
  3.0 4.6 %collective-permute-start.1 = (bf16[6,72,128]{2,1,0:T(8,128)(2,1)S(1)}, bf16[6,72,128]{2,1,0:T(8,128)(2,1)S(1)}, u32[]{:S(2)}, u32[]{:S(2)}) collective-permute-start(bf16[6,72,128]{2,1,0:T(8,128)(2,1)S(1)} %get-tuple-element.21), channel_id=1, source_target_pairs={{0,8},{1,2},{2,1},{3,4},{4,3},{5,6},{6,5},{7,15},{8,0},{9,10},{10,... | collective-permute-start | bytes 331784 | tf_op jit(solution)/shard_map/ppermute | solution.py:40
  9.2 3.7 %collective-permute-start.4 = (bf16[12,32,128]{2,1,0:T(8,128)(2,1)S(1)}, bf16[12,32,128]{2,1,0:T(8,128)(2,1)S(1)}, u32[]{:S(2)}, u32[]{:S(2)}) collective-permute-start(bf16[12,32,128]{2,1,0:T(8,128)(2,1)S(1)} %get-tuple-element.26), channel_id=1, source_target_pairs={{0,16},{8,24},{16,0},{24,8},{1,17},{9,25},{17,1},{25,9},{2,18},{10... | collective-permute-start | bytes 294920 | tf_op jit(solution)/shard_map/ppermute | solution.py:272
  10.5 7.0 %collective-permute-start.2 = (bf16[12,32,128]{2,1,0:T(8,128)(2,1)S(1)}, bf16[12,32,128]{2,1,0:T(8,128)(2,1)S(1)}, u32[]{:S(2)}, u32[]{:S(2)}) collective-permute-start(bf16[12,32,128]{2,1,0:T(8,128)(2,1)S(1)} %get-tuple-element.24), channel_id=1, source_target_pairs={{0,24},{8,16},{16,8},{24,0},{1,25},{9,17},{17,9},{25,1},{2,26},{10... | collective-permute-start | bytes 294920 | tf_op jit(solution)/shard_map/ppermute | solution.py:272
  12.9 4.6 %collective-permute-start.3 = (bf16[12,32,128]{2,1,0:T(8,128)(2,1)S(1)}, bf16[12,32,128]{2,1,0:T(8,128)(2,1)S(1)}, u32[]{:S(2)}, u32[]{:S(2)}) collective-permute-start(bf16[12,32,128]{2,1,0:T(8,128)(2,1)S(1)} %get-tuple-element.25), channel_id=1, source_target_pairs={{0,8},{8,0},{16,24},{24,16},{1,9},{9,1},{17,25},{25,17},{2,10},{10... | collective-permute-start | bytes 294920 | tf_op jit(solution)/shard_map/ppermute | solution.py:272

commit v16 on v13

--- a/solution.py
+++ b/solution.py
@@ -175,21 +175,7 @@
     rest = rows_ref.shape[2] - LANES
     me = lax.axis_index("grp")
     lane = lax.broadcasted_iota(jnp.int32, local.shape, 1)
-    for k, ref in zip(away, received):
-        first = lax.bitwise_xor(me, k) * capacity
-        for p in range(capacity):
-            local = jnp.where(lane == first + p, ref[p].astype(jnp.float32)[24:32, 127:128], local)
     copies = []
-    if last:
-        count = ids_ref.shape[1]
-        owned = local[0:1, :count].astype(jnp.int32)
-        group = lax.broadcasted_iota(jnp.int32, (1, count), 1) // capacity
-        start = (group * lax.axis_size("row") + lax.axis_index("row")) * elements
-        ids_ref[...] = jnp.where(owned >= 0, start + owned, -1)
-        copies.append(pltpu.make_async_copy(ids_ref, ids_hbm, sems.at[len(away)]))
-        copies[-1].start()
-    else:
-        after_ref[...] = local
     for i, (k, ref) in enumerate(zip(away, received)):
         for p in range(capacity):
             block = ref[p].astype(jnp.float32)
@@ -208,6 +194,20 @@
             )
         )
         copies[-1].start()
+    for k, ref in zip(away, received):
+        first = lax.bitwise_xor(me, k) * capacity
+        for p in range(capacity):
+            local = jnp.where(lane == first + p, ref[p].astype(jnp.float32)[24:32, 127:128], local)
+    if last:
+        count = ids_ref.shape[1]
+        owned = local[0:1, :count].astype(jnp.int32)
+        group = lax.broadcasted_iota(jnp.int32, (1, count), 1) // capacity
+        start = (group * lax.axis_size("row") + lax.axis_index("row")) * elements
+        ids_ref[...] = jnp.where(owned >= 0, start + owned, -1)
+        copies.append(pltpu.make_async_copy(ids_ref, ids_hbm, sems.at[len(away)]))
+        copies[-1].start()
+    else:
+        after_ref[...] = local
     for copy in copies:
         copy.wait()
 

time: 18.7 us -> 18.7 us (level)
  no operation moved by 1% of the time
where the time goes in v16:
time: 18.7 us; the launch traced here: 18.3 us
  Pallas kernels  6.93 us (37%)
  waiting for transfers between devices  5.7 us (30%)
  starting transfers between devices  5.01 us (27%)
  between operations  0.67 us (4%)
    ppermute x3, waiting for transfers between devices, on_device(): lax.ppermute(sends[k], 'grp', [(i, i ^ k) for i in range(owners)])  3.74 us
    ppermute x3, starting transfers between devices, on_device(): lax.ppermute(sends[k], 'grp', [(i, i ^ k) for i in range(owners)])  3.73 us
    pallas_call x1, Pallas kernels, on_device(): pl.pallas_call(functools.partial(left_kernel, capacity), out_shape=(pltpu...  2.63 us
    ppermute x2, waiting for transfers between devices, swapped(): return lax.ppermute(value, ('grp', 'row'), pairs)  1.96 us
    pallas_call x1, Pallas kernels, on_device(): pl.pallas_call(rows_kernel, out_shape=[pltpu.VMEM((capacity, 32, LANES),...  1.53 us
    ppermute x2, starting transfers between devices, swapped(): return lax.ppermute(value, ('grp', 'row'), pairs)  1.28 us
    pallas_call x1, Pallas kernels, on_device(): pl.pallas_call(pack_kernel, out_shape=(run, run, pltpu.VMEM(prolong.shape...  1.12 us
    pallas_call x1, Pallas kernels, on_device(): pl.pallas_call(functools.partial(unpack_kernel, elements, late, True), ou...  0.83 us
  transfers between devices with their start and end apart: 5, of which 3 were waited for; matrix products, arithmetic and copies ran while one was open for 0% of the time, Pallas kernels for 19%

profile of v16, /device:TPU:9, one launch (start us, length us, event | category | flops | bytes accessed | tf_op | source)
XLA Modules:
  0.0 18.3 jit_solution(7845474901226681222)
XLA Ops:
  0.6 1.1 %pack.1 = (bf16[6,72,128]{2,1,0:T(8,128)(2,1)S(1)}, bf16[6,72,128]{2,1,0:T(8,128)(2,1)S(1)}, bf16[24,24,192]{2,1,0:T(8,128)(2,1)S(1)}) custom-call(s32[1,2]{1,0:T(1,128)} %count_hbm.1, s32[1,2]{1,0:T(1,128)} %offset_hbm.1, bf16[24,24,192]{2,1,0:T(8,128)(2,1)} %prolong_hbm.1), custom_call_target="tpu_custom_call" | custom-call | tf_op jit(solution)/shard_map/pack/pallas_call | solution.py:223
  1.8 1.3 %collective-permute-start = (bf16[6,72,128]{2,1,0:T(8,128)(2,1)S(1)}, bf16[6,72,128]{2,1,0:T(8,128)(2,1)S(1)}, u32[]{:S(2)}, u32[]{:S(2)}) collective-permute-start(bf16[6,72,128]{2,1,0:T(8,128)(2,1)S(1)} %get-tuple-element.19), channel_id=1, source_target_pairs={{0,1},{1,0},{2,3},{3,2},{4,5},{5,4},{6,7},{7,6},{8,9},{9,8},{10,11... | collective-permute-start | bytes 331784 | tf_op jit(solution)/shard_map/ppermute | solution.py:40
  3.0 0.0 collective-permute-start.1
  3.0 2.6 %left.1 = (bf16[24,7,48,256]{3,2,1,0:T(8,128)(2,1)S(1)}, s32[48]{0:T(128)S(4)}, s32[7,24]{1,0:T(8,128)S(4)}) custom-call(f32[7,2,24]{2,1,0:T(2,128)} %bitcast.7, s32[1,24]{1,0:T(1,128)} %bitcast.9, s32[7,24]{1,0:T(8,128)} %bitcast.8, bf16[7,2,192,192]{3,2,1,0:T(8,128)(2,1)} %stiffness_hbm.1, bf16[576,192]{1,0:T(8,128)(2,1)S(1)} %bitcast.5), custom_call_target="tpu_custom_call" | custom-call | tf_op jit(solution)/shard_map/left/pallas_call | solution.py:237
  5.7 0.1 collective-permute-done.even_ref
  5.8 1.9 %collective-permute-done.1.odd_ref = bf16[6,72,128]{2,1,0:T(8,128)(2,1)S(1)} collective-permute-done((bf16[6,72,128]{2,1,0:T(8,128)(2,1)S(1)}, bf16[6,72,128]{2,1,0:T(8,128)(2,1)S(1)}, u32[]{:S(2)}, u32[]{:S(2)}) %collective-permute-start.1) | collective-permute-done | bytes 110624 | tf_op jit(solution)/shard_map/ppermute | solution.py:40
  7.6 1.5 %rows.1 = (bf16[12,32,128]{2,1,0:T(8,128)(2,1)S(1)}, bf16[12,32,128]{2,1,0:T(8,128)(2,1)S(1)}, bf16[12,32,128]{2,1,0:T(8,128)(2,1)S(1)}, bf16[12,32,128]{2,1,0:T(8,128)(2,1)S(1)}) custom-call(s32[7,24]{1,0:T(8,128)S(4)} %get-tuple-element.17.columns_ref, s32[48]{0:T(128)S(4)} %get-tuple-element.18.order_ref, bf16[576,192]{1,0:T(8,128)(2,1)S(1)} %bitcast.6, ...), custom_call_target="tpu_custom_call" | custom-call | tf_op jit(solution)/shard_map/rows/pallas_call | solution.py:254
  9.2 1.3 %collective-permute-start.4 = (bf16[12,32,128]{2,1,0:T(8,128)(2,1)S(1)}, bf16[12,32,128]{2,1,0:T(8,128)(2,1)S(1)}, u32[]{:S(2)}, u32[]{:S(2)}) collective-permute-start(bf16[12,32,128]{2,1,0:T(8,128)(2,1)S(1)} %get-tuple-element.24), channel_id=1, source_target_pairs={{0,16},{8,24},{16,0},{24,8},{1,17},{9,25},{17,1},{25,9},{2,18},{10... | collective-permute-start | bytes 294920 | tf_op jit(solution)/shard_map/ppermute | solution.py:269
  10.5 2.4 %collective-permute-start.2 = (bf16[12,32,128]{2,1,0:T(8,128)(2,1)S(1)}, bf16[12,32,128]{2,1,0:T(8,128)(2,1)S(1)}, u32[]{:S(2)}, u32[]{:S(2)}) collective-permute-start(bf16[12,32,128]{2,1,0:T(8,128)(2,1)S(1)} %get-tuple-element.22), channel_id=1, source_target_pairs={{0,24},{8,16},{16,8},{24,0},{1,25},{9,17},{17,9},{25,1},{2,26},{10... | collective-permute-start | bytes 294920 | tf_op jit(solution)/shard_map/ppermute | solution.py:269
  12.9 0.0 collective-permute-start.3
  12.9 0.0 collective-permute-done.4.refs_0_
  12.9 0.8 %unpack_early.1 = (bf16[48,24,168]{2,1,0:T(8,128)(2,1)}, f32[8,128]{1,0:T(8,128)S(1)}) custom-call(bf16[12,32,128]{2,1,0:T(8,128)(2,1)S(1)} %collective-permute-done.4.refs_0_, bf16[12,32,128]{2,1,0:T(8,128)(2,1)S(1)} %get-tuple-element.25.refs_1_), custom_call_target="tpu_custom_call" | custom-call | tf_op jit(solution)/shard_map/unpack_early/pallas_call | solution.py:278
  13.7 3.7 %collective-permute-done.2.refs_0_ = bf16[12,32,128]{2,1,0:T(8,128)(2,1)S(1)} collective-permute-done((bf16[12,32,128]{2,1,0:T(8,128)(2,1)S(1)}, bf16[12,32,128]{2,1,0:T(8,128)(2,1)S(1)}, u32[]{:S(2)}, u32[]{:S(2)}) %collective-permute-start.2) | collective-permute-done | bytes 98336 | tf_op jit(solution)/shard_map/ppermute | solution.py:269
  17.5 0.0 collective-permute-done.3.refs_1_
  17.5 0.8 %unpack_late.1 = (bf16[48,24,168]{2,1,0:T(8,128)(2,1)}, s32[1,48]{1,0:T(1,128)}) custom-call(bf16[12,32,128]{2,1,0:T(8,128)(2,1)S(1)} %collective-permute-done.2.refs_0_, bf16[12,32,128]{2,1,0:T(8,128)(2,1)S(1)} %collective-permute-done.3.refs_1_, bf16[48,24,168]{2,1,0:T(8,128)(2,1)} %get-tuple-element.26.refs_2_, ...), custom_call_target="tpu_custom_call", output_to_operand_aliasing={{0}: (2, {})} | custom-call | tf_op jit(solution)/shard_map/unpack_late/pallas_call | solution.py:285
Async XLA Ops:
  1.8 4.0 %collective-permute-start = (bf16[6,72,128]{2,1,0:T(8,128)(2,1)S(1)}, bf16[6,72,128]{2,1,0:T(8,128)(2,1)S(1)}, u32[]{:S(2)}, u32[]{:S(2)}) collective-permute-start(bf16[6,72,128]{2,1,0:T(8,128)(2,1)S(1)} %get-tuple-element.19), channel_id=1, source_target_pairs={{0,1},{1,0},{2,3},{3,2},{4,5},{5,4},{6,7},{7,6},{8,9},{9,8},{10,11... | collective-permute-start | bytes 331784 | tf_op jit(solution)/shard_map/ppermute | solution.py:40
  3.0 4.6 %collective-permute-start.1 = (bf16[6,72,128]{2,1,0:T(8,128)(2,1)S(1)}, bf16[6,72,128]{2,1,0:T(8,128)(2,1)S(1)}, u32[]{:S(2)}, u32[]{:S(2)}) collective-permute-start(bf16[6,72,128]{2,1,0:T(8,128)(2,1)S(1)} %get-tuple-element.20), channel_id=1, source_target_pairs={{0,8},{1,2},{2,1},{3,4},{4,3},{5,6},{6,5},{7,15},{8,0},{9,10},{10,... | collective-permute-start | bytes 331784 | tf_op jit(solution)/shard_map/ppermute | solution.py:40
  9.2 3.7 %collective-permute-start.4 = (bf16[12,32,128]{2,1,0:T(8,128)(2,1)S(1)}, bf16[12,32,128]{2,1,0:T(8,128)(2,1)S(1)}, u32[]{:S(2)}, u32[]{:S(2)}) collective-permute-start(bf16[12,32,128]{2,1,0:T(8,128)(2,1)S(1)} %get-tuple-element.24), channel_id=1, source_target_pairs={{0,16},{8,24},{16,0},{24,8},{1,17},{9,25},{17,1},{25,9},{2,18},{10... | collective-permute-start | bytes 294920 | tf_op jit(solution)/shard_map/ppermute | solution.py:269
  10.5 7.0 %collective-permute-start.2 = (bf16[12,32,128]{2,1,0:T(8,128)(2,1)S(1)}, bf16[12,32,128]{2,1,0:T(8,128)(2,1)S(1)}, u32[]{:S(2)}, u32[]{:S(2)}) collective-permute-start(bf16[12,32,128]{2,1,0:T(8,128)(2,1)S(1)} %get-tuple-element.22), channel_id=1, source_target_pairs={{0,24},{8,16},{16,8},{24,0},{1,25},{9,17},{17,9},{25,1},{2,26},{10... | collective-permute-start | bytes 294920 | tf_op jit(solution)/shard_map/ppermute | solution.py:269
  12.9 4.6 %collective-permute-start.3 = (bf16[12,32,128]{2,1,0:T(8,128)(2,1)S(1)}, bf16[12,32,128]{2,1,0:T(8,128)(2,1)S(1)}, u32[]{:S(2)}, u32[]{:S(2)}) collective-permute-start(bf16[12,32,128]{2,1,0:T(8,128)(2,1)S(1)} %get-tuple-element.23), channel_id=1, source_target_pairs={{0,8},{8,0},{16,24},{24,16},{1,9},{9,1},{17,25},{25,17},{2,10},{10... | collective-permute-start | bytes 294920 | tf_op jit(solution)/shard_map/ppermute | solution.py:269
